TPU v7x, 32 devices: a whole 2x2x4 slice. The times are simulated.
32 devices in a mesh: win: 2 (over y), sta: 8 (over z, x), freq: 2 (over core).
Axes of the slice: x: 2, y: 2, z: 4, core: 2. Of those that a mesh axis runs over, the one named last changes fastest.
Arguments:
- traces: bfloat16 [256, 5120], P(('win', 'sta'), 'freq'), parts along dimension 0, may hold values from -6 to 6
- tables: float32 [16, 32768], replicated, may hold values from 0 to 20
- corrections: bfloat16 [128, 32768], P('sta'), may hold values from -1.5 to 1.5
- station_table: int32 [128], replicated, may hold values from 0 to 15
- node_ids: int32 [32768], replicated, may hold values from 0 to 32767, each once
- freq_bins: int32 [16], replicated, may hold values from 64 to 511
Outputs:
- spectrum: float32 [32, 32768], P('win', ('sta', 'freq')), parts along dimension 0
- beam_power: float32 [65536], P(('win', 'sta', 'freq')), parts along dimension 0
There are 2 independent parts, one for each index of `win`. A program takes and returns all parts, laid end to end along the dimension named above; an argument that names none is the same for every part. Nothing has to cross between parts.
Inputs may be any that keep to these rules, and one draw needn't show every extreme that they name: `node_ids`: a permutation of 0 to 32767.
All inputs are finite; a program needn't handle non-finite values.
Results may differ from a plain program's by a relative error of at most 0.0003.
Values may be sent and summed in bfloat16 or wider, within the bound.
No kernel may reach another device: no remote copies, remote signals or barrier semaphores. Data moves between devices by JAX's collectives and lax.ppermute only.
A program may use at most 320 MiB of HBM per device.

v0:
```python
import math

import jax
import jax.numpy as jnp
from jax import lax
from jax.sharding import PartitionSpec as P

NT = 5120
NF = 16


sample_rate = 20.0


def dft_table(sample_pos, freq_bins):
    turn_count = freq_bins[None, :] * sample_pos[:, None] % NT
    angles = 2.0 * math.pi / NT * turn_count.astype(jnp.float32)
    return jnp.concatenate([jnp.cos(angles), -jnp.sin(angles)], axis=1) / math.sqrt(NT)


def image_block(spec_real, spec_imag, travel_rows, omegas):
    planes = []
    for freq_pos in range(omegas.shape[0]):
        phases = omegas[freq_pos] * travel_rows
        cosine = jnp.cos(phases)
        sine_val = jnp.sin(phases)
        weight_real = spec_real[:, freq_pos : freq_pos + 1]
        weight_imag = spec_imag[:, freq_pos : freq_pos + 1]
        real_part = jnp.sum(weight_real * cosine - weight_imag * sine_val, axis=0)
        imag_part = jnp.sum(weight_real * sine_val + weight_imag * cosine, axis=0)
        planes.append(jnp.stack([real_part, imag_part]))
    return jnp.stack(planes)


def on_device(traces, tables, corrections, station_table, node_ids, freq_bins):
    stations_dev = corrections.shape[0]
    nf_dev = NF // lax.axis_size("freq")
    half_length = traces.shape[1]
    sample_pos = lax.axis_index("freq") * half_length + jnp.arange(half_length, dtype=jnp.int32)
    partial_value = jnp.dot(
        traces.astype(jnp.float32),
        dft_table(sample_pos, freq_bins),
        precision=lax.Precision.HIGHEST,
    )
    partial_value = partial_value.reshape(stations_dev, 2, NF)
    spectra = lax.psum_scatter(partial_value, "freq", scatter_dimension=2, tiled=True)
    freq_start = lax.axis_index("freq") * nf_dev
    my_bins = lax.dynamic_slice_in_dim(freq_bins, freq_start, nf_dev)
    omegas = 2.0 * math.pi * sample_rate / NT * my_bins.astype(jnp.float32)
    sta_start = lax.axis_index("sta") * stations_dev
    local_table = lax.dynamic_slice_in_dim(station_table, sta_start, stations_dev)
    node_cols = jnp.take(tables, node_ids, axis=1)
    travel_rows = jnp.take(node_cols, local_table, axis=0) + corrections.astype(jnp.float32)
    partial_images = image_block(spectra[:, 0, :], spectra[:, 1, :], travel_rows, omegas)
    images = lax.psum_scatter(partial_images, "sta", scatter_dimension=2, tiled=True)
    grid_major = lax.all_to_all(images, "freq", split_axis=2, concat_axis=0, tiled=True)
    power_grid = (
        grid_major[:, 0, :] * grid_major[:, 0, :] + grid_major[:, 1, :] * grid_major[:, 1, :]
    )
    power_total = jnp.sum(power_grid, axis=0)
    spectrum = NF * power_grid / power_total[None, :]
    beam_power = power_total / (NF * stations_dev * lax.axis_size("sta"))
    return (spectrum, beam_power)


def solution(mesh):
    return jax.shard_map(
        on_device,
        mesh=mesh,
        in_specs=(P(("win", "sta"), "freq"), P(), P("sta", None), P(), P(), P()),
        out_specs=(P("win", ("sta", "freq")), P(("win", "sta", "freq"))),
        check_vma=False,
    )
```

profile of v0, /device:TPU:0, one launch (start us, length us, event | category | flops | bytes accessed | tf_op | source)
XLA Modules:
  0.0 756.4 jit_solution(15730251764164370713)
XLA Ops:
  7.2 1.4 fusion.15
  8.9 0.7 copy.35
  9.7 0.9 fusion.18
  10.6 0.9 compare_and_fusion
  11.6 0.7 convert_multiply_fusion
  13.0 9.8 %copy.30 = f32[16,32768]{0,1:T(8,128)} copy(f32[16,32768]{1,0:T(8,128)} %param.7) | data formatting | bytes 4194304 | tf_op args[1]
  22.8 113.9 %gather_fusion = f32[32768,16]{1,0:T(8,128)} fusion(f32[16,32768]{0,1:T(8,128)} %copy.30, s32[32768]{0:T(1024)S(1)} %fusion.18), kind=kCustom, calls=%fused_computation | custom fusion | bytes 4325376 | tf_op jit(solution)/shard_map/jit(_take)/gather | solution.py:52
  136.8 19.1 %select_bitcast_fusion = f32[16,32768]{0,1:T(8,128)} fusion(f32[32768,16]{1,0:T(8,128)} %gather_fusion, pred[32768]{0:T(1024)(128)(4,1)S(1)} %compare_and_fusion), kind=kLoop, calls=%fused_computation.2 | loop fusion | flops 524288 | bytes 4227072 | tf_op jit(solution)/shard_map/jit(_take)/select_n | solution.py:52
  155.9 9.8 %copy.31 = f32[16,32768]{1,0:T(8,128)S(1)} copy(f32[16,32768]{0,1:T(8,128)} %select_bitcast_fusion) | data formatting | bytes 4194304 | tf_op jit(solution)/shard_map/jit(_take)/select_n | solution.py:52
  165.7 2.5 gather_fusion.1
  168.1 0.7 slice_bitcast_fusion.1
  168.8 62.0 %subtract_reduce_fusion = (f32[32768]{0:T(1024)S(1)}, f32[32768]{0:T(1024)S(1)}, f32[32768]{0:T(1024)S(1)}, f32[32768]{0:T(1024)S(1)}, f32[32768]{0:T(1024)S(1)}...) fusion(f32[16]{0:T(128)S(1)} %get-tuple-element.46, ...), kind=kLoop, calls=%fused_computation.4 | loop fusion | flops 29491200 | bytes 6816552 | tf_op jit(solution)/shard_map/reduce_sum | solution.py:29
  230.9 20.7 %subtract_reduce_fusion.6 = (f32[32768]{0:T(1024)S(1)}, f32[32768]{0:T(1024)S(1)}, f32[32768]{0:T(1024)S(1)}, f32[32768]{0:T(1024)S(1)}) fusion(f32[16,32768]{1,0:T(8,128)S(1)} %get-tuple-element.30, f32[16]{0:T(128)S(1)} %get-tuple-element.52, f32[]{:T(128)} %bitcast.12, f32[16]{0:T(128)S(1)} %get-tuple-element.61, f32[16]{0:T(128)S(1)} %get-tuple-element.45, ...), kind=kLoop, calls=%fused_computation.16 | loop fusion | flops 9306112 | bytes 2621704 | tf_op jit(solution)/shard_map/reduce_sum | solution.py:29
  253.7 60.6 %copy.38 = f32[8,2,32768]{1,0,2:T(8,128)} copy(f32[8,2,32768]{2,1,0:T(2,128)S(1)} %fusion.9) | data formatting | bytes 4194304
  314.3 82.3 %reshape.47 = f32[32768,16]{1,0:T(8,128)} reshape(f32[32768,8,2]{2,1,0:T(8,128)} %bitcast.59) | data formatting | bytes 4194304
  396.6 285.6 %reduce-scatter.7.cloned.1.call-done = f32[4096,16]{1,0:T(8,128)} async-done(((f32[32768,16]{1,0:T(8,128)}), f32[4096,16]{1,0:T(8,128)}) %reduce-scatter.7.cloned.1.call-update) | async-done | bytes 262160
  682.2 10.6 %reshape.48 = f32[4096,8,2]{2,1,0:T(8,128)} reshape(f32[4096,16]{1,0:T(8,128)} %reduce-scatter.7.cloned.1.call-done) | data formatting | bytes 524288
  692.8 26.8 %copy.32 = f32[8,2,4096]{0,1,2:T(2,128)} copy(f32[8,2,4096]{1,0,2:T(8,128)} %bitcast.109) | data formatting | bytes 524288 | tf_op jit(solution)/shard_map/reduce_scatter | solution.py:55
  719.6 8.5 %reshape.49 = f32[2,1,32768]{2,1,0:T(1,128)S(1)} reshape(f32[4096,2,8]{2,1,0:T(2,128)} %bitcast.110) | data formatting | bytes 524288
  728.2 3.9 all_to_all.18
  732.6 1.4 reduce.1
  734.1 8.5 %reshape.50 = f32[4096,2,8]{2,1,0:T(2,128)} reshape(f32[2,32768]{1,0:T(2,128)S(1)} %reduce.1) | data formatting | bytes 524288
  742.6 5.1 copy.34
  747.8 0.7 bitcast_divide_fusion
  (30 shorter events, 4.4 us)
Async XLA Ops:
  7.2 1.5 copy-start
  7.2 161.0 %reduce-scatter.5.cloned.1.call-start = ((), (), s32[]{:S(2)}) async-start(), calls=%async_computation.3 | async-start | bytes 24576 | tf_op jit(solution)/shard_map/reduce_scatter | solution.py:46
  9.6 672.6 %reduce-scatter.7.cloned.1.call-start = ((), (), s32[]{:S(2)}) async-start(), calls=%async_computation.4 | async-start | bytes 18874368
  13.0 9.8 %copy-start.2 = (s32[128]{0:T(128)S(1)}, s32[128]{0:T(128)}, u32[]{:S(2)}) copy-start(s32[128]{0:T(128)} %param.9) | copy-start | bytes 1540
  165.7 3.2 copy-start.3
  742.6 6.5 copy-start.1
Sparse Core Ops, SparseCore 0:
  10.8 10.0 reduce-scatter.4
  396.7 285.4 reduce-scatter.6
where the time goes:
time: 762 us; the launch traced here: 756 us
  local copies, waits for them, and re-layouts  341 us (45%)
  waiting for transfers between devices  286 us (38%)
  other arithmetic  111 us (15%)
  between operations  14.6 us (2%)
    unnamed x3, waiting for transfers between devices  286 us
    unnamed x14, local copies, waits for them, and re-layouts  180 us
    gather x1, local copies, waits for them, and re-layouts, on_device(): node_cols = jnp.take(tables, node_ids, axis=1)  114 us
    reduce_sum x2, other arithmetic, image_block(): real_part = jnp.sum(weight_real * cosine - weight_imag * sine_val, axis=0)  82.8 us
    reduce_scatter x1, local copies, waits for them, and re-layouts, on_device(): lax.psum_scatter(partial_images, 'sta', scatter_dimension=2, tiled=True)  26.8 us
    select_n x1, other arithmetic, on_device(): node_cols = jnp.take(tables, node_ids, axis=1)  19.1 us
  transfers between devices with their start and end apart: 2, of which 1 were waited for; matrix products, arithmetic and copies ran while one was open for 21% of the time, Pallas kernels for 0%

commit v1 on v0

v1 whole, which is shorter than its diff:
```python
import functools
import math

import jax
import jax.numpy as jnp
import numpy as np
from jax import lax
from jax.experimental import pallas as pl
from jax.experimental.pallas import tpu as pltpu
from jax.sharding import PartitionSpec as P

NT = 5120
NF = 16
LANES = 128
VMEM_LIMIT = 48 * 1024 * 1024


def chebyshev_fit(func, degree, low, high):
    fit = np.polynomial.chebyshev.Chebyshev.interpolate(func, degree, domain=[low, high])
    return [float(v) for v in fit.convert(kind=np.polynomial.Polynomial).coef]


SIN_HALF = chebyshev_fit(lambda z: np.pi * np.sinc(np.sqrt(z)), 4, 0.0, 0.25)
COS_HALF = chebyshev_fit(lambda z: np.cos(np.pi * np.sqrt(z)), 4, 0.0, 0.25)


def horner(coefs, arg):
    total = coefs[-1]
    for coef in coefs[-2::-1]:
        total = total * arg + coef
    return total


def turn_parts(rest):
    square = rest * rest
    root = math.sqrt(2.0)
    sine_half = rest * horner([root * c for c in SIN_HALF], square)
    cos_half = horner([root * c for c in COS_HALF], square)
    return sine_half * sine_half, sine_half * cos_half


def dft_kernel(half_length, bins_ref, traces_ref, out_ref):
    start = lax.axis_index("freq") * half_length
    bins = bins_ref[...].astype(jnp.float32)
    pos = (start + lax.broadcasted_iota(jnp.int32, (NF, half_length), 1)).astype(jnp.float32)
    product = bins * pos
    turns = jnp.round(product * (1.0 / NT))
    rest = (product - turns * NT) * (1.0 / NT)
    versine, sine = turn_parts(rest)
    scale = 1.0 / math.sqrt(NT)
    table = jnp.concatenate([(1.0 - versine) * scale, sine * -scale], axis=0)
    high = table.astype(jnp.bfloat16)
    low = (table - high.astype(jnp.float32)).astype(jnp.bfloat16)
    both = jnp.concatenate([high, low], axis=0)
    sums = lax.dot_general(
        traces_ref[...], both, (((1,), (1,)), ((), ())), preferred_element_type=jnp.float32
    )
    out_ref[...] = sums[:, : 2 * NF] + sums[:, 2 * NF :]


def gather_kernel(ids_ref, tables_ref, out_ref):
    count = ids_ref.shape[1] // LANES
    rows = tables_ref.shape[0]
    blocks = tables_ref.shape[1] // LANES
    low = []
    high = []
    for tile in range(count):
        ids = jnp.broadcast_to(ids_ref[:, tile * LANES : (tile + 1) * LANES], (rows, LANES))
        low.append(ids & (LANES - 1))
        high.append(ids >> 7)

    def body(block, found):
        piece = tables_ref[:, pl.ds(pl.multiple_of(block * LANES, LANES), LANES)]
        result = []
        for tile in range(count):
            picked = jnp.take_along_axis(piece, low[tile], axis=1, mode="promise_in_bounds")
            result.append(jnp.where(high[tile] == block, picked, found[tile]))
        return tuple(result)

    zero = jnp.zeros((rows, LANES), jnp.float32)
    found = lax.fori_loop(0, blocks, body, (zero,) * count)
    for tile in range(count):
        out_ref[:, tile * LANES : (tile + 1) * LANES] = found[tile]


def image_kernel(table_of, bins_ref, spectra_ref, corr_ref, times_ref, out_ref, turns_ref, weight_ref):
    stations, nodes = corr_ref.shape
    windows = spectra_ref.shape[0]
    for win in range(windows):
        weight_ref[win] = spectra_ref[win, 0] + spectra_ref[win, 1]
    turns_ref[...] = corr_ref[...].astype(jnp.float32)

    def add_times(station, carry):
        row = pl.ds(station, 1)
        travel = turns_ref[row, :] + times_ref[pl.ds(table_of[station], 1), :]
        turns_ref[row, :] = travel * (1.0 / 256.0)
        return carry

    lax.fori_loop(0, stations, add_times, 0)

    powers = [[] for _ in range(windows)]
    for freq in range(NF):
        bin_at = bins_ref[freq].astype(jnp.float32)

        def body(group, sums):
            rows = pl.ds(pl.multiple_of(group * 8, 8), 8)
            turns = turns_ref[rows, :] * bin_at
            rest = turns - jnp.round(turns)
            versine, sine = turn_parts(rest)
            result = []
            for win in range(windows):
                real = weight_ref[win, rows, freq : freq + 1]
                imag = weight_ref[win, rows, NF + freq : NF + freq + 1]
                result.append(sums[2 * win] + (real - real * versine - imag * sine))
                result.append(sums[2 * win + 1] + (real * sine + imag - imag * versine))
            return tuple(result)

        zero = jnp.zeros((8, nodes), jnp.float32)
        sums = lax.fori_loop(0, stations // 8, body, (zero,) * (2 * windows))
        for win in range(windows):
            real = jnp.sum(sums[2 * win], axis=0, keepdims=True)
            imag = jnp.sum(sums[2 * win + 1], axis=0, keepdims=True)
            powers[win].append(real * real + imag * imag)
    for win in range(windows):
        power = jnp.concatenate(powers[win], axis=0)
        total = jnp.sum(power, axis=0, keepdims=True)
        out_ref[win, :NF, :] = power * (NF / total)
        out_ref[win, NF :, :] = jnp.broadcast_to(total * (1.0 / (NF * stations)), (8, nodes))


def on_device(traces, tables, corrections, station_table, node_ids, freq_bins):
    windows, groups, cores = (lax.axis_size(a) for a in ("win", "sta", "freq"))
    win, sta, core = (lax.axis_index(a) for a in ("win", "sta", "freq"))
    stations_dev, grid = corrections.shape
    stations = stations_dev * groups
    nodes = grid // (windows * groups * cores)
    params = pltpu.CompilerParams(vmem_limit_bytes=VMEM_LIMIT)
    vmem = pl.BlockSpec(memory_space=pltpu.VMEM)
    smem = pl.BlockSpec(memory_space=pltpu.SMEM)

    blocks = corrections.reshape(stations_dev, groups, cores * windows, nodes)
    mine = lax.dynamic_index_in_dim(blocks, core * windows + win, axis=2, keepdims=False)
    corr = lax.all_to_all(mine.transpose(1, 0, 2), "sta", split_axis=0, concat_axis=0, tiled=True)
    corr = corr.reshape(stations, nodes)

    partial = pl.pallas_call(
        functools.partial(dft_kernel, traces.shape[1]),
        out_shape=jax.ShapeDtypeStruct((stations_dev, 2 * NF), jnp.float32),
        in_specs=[vmem, vmem],
        out_specs=vmem,
        compiler_params=params,
        name="dft",
    )(freq_bins.reshape(NF, 1), traces)
    copies = jnp.broadcast_to(partial[None], (windows * groups * cores, stations_dev, 2 * NF))
    spectra = lax.all_to_all(copies, ("win", "sta", "freq"), split_axis=0, concat_axis=0, tiled=True)
    spectra = spectra.reshape(windows, groups, cores, stations_dev, 2 * NF)
    spectra = spectra.transpose(0, 2, 1, 3, 4).reshape(windows, cores, stations, 2 * NF)

    first = ((sta * cores + core) * windows + win) * nodes
    my_ids = lax.dynamic_slice_in_dim(node_ids, first, nodes).reshape(1, nodes)
    times = pl.pallas_call(
        gather_kernel,
        out_shape=jax.ShapeDtypeStruct((tables.shape[0], nodes), jnp.float32),
        in_specs=[vmem, vmem],
        out_specs=vmem,
        compiler_params=params,
        name="gather",
    )(my_ids, tables)

    result = pl.pallas_call(
        image_kernel,
        out_shape=jax.ShapeDtypeStruct((windows, NF + 8, nodes), jnp.float32),
        in_specs=[smem, smem, vmem, vmem, vmem],
        out_specs=vmem,
        scratch_shapes=[
            pltpu.VMEM((stations, nodes), jnp.float32),
            pltpu.VMEM((windows, stations, 2 * NF), jnp.float32),
        ],
        compiler_params=params,
        name="image",
    )(station_table, freq_bins, spectra, corr, times)
    halves = lax.all_to_all(result, "win", split_axis=0, concat_axis=0, tiled=True)
    spectrum = halves[:, :NF, :].transpose(1, 0, 2).reshape(NF, windows * nodes)
    beam_power = halves[:, NF, :].reshape(windows * nodes)
    return spectrum, beam_power


def solution(mesh):
    return jax.shard_map(
        on_device,
        mesh=mesh,
        in_specs=(P(("win", "sta"), "freq"), P(), P("sta", None), P(), P(), P()),
        out_specs=(P("win", ("sta", "freq")), P(("win", "sta", "freq"))),
        check_vma=False,
    )
```

time: 762 us -> 87.1 us (0.11)
  local copies, waits for them, and re-layouts: 341 us -> 8.67 us
  waiting for transfers between devices: 286 us -> 3.76 us
  other arithmetic: 111 us -> 0.81 us
  Pallas kernels: 0 us -> 54.6 us
  between operations: 14.6 us -> 0.77 us
  starting transfers between devices: 0.08 us -> 10.7 us
    unnamed x3 -> x0, waiting for transfers between devices: 286 us -> none
    unnamed x14 -> x11, local copies, waits for them, and re-layouts: 180 us -> 1.82 us
    gather x2 -> x0, local copies, waits for them, and re-layouts: 116 us -> none  [the longest x1 114 us: on_device(): node_cols = jnp.take(tables, node_ids, axis=1)]
    reduce_sum x3 -> x0, other arithmetic: 82.8 us -> none  [the longest x2 82.8 us: image_block(): real_part = jnp.sum(weight_real * cosine - weight_imag * sine_val, axis=0)]
    pallas_call x0 -> x3, Pallas kernels: none -> 54.6 us  [the longest x1 27.6 us: on_device(): pl.pallas_call(image_kernel, out_shape=jax.ShapeDtypeStruct((windows, NF...]
    reduce_scatter x1 -> x0, local copies, waits for them, and re-layouts: 26.8 us -> none  [on_device(): lax.psum_scatter(partial_images, 'sta', scatter_dimension=2, tiled=True)]
    select_n x1 -> x0, other arithmetic: 19.1 us -> none  [on_device(): node_cols = jnp.take(tables, node_ids, axis=1)]
    all_to_all x0 -> x2, starting transfers between devices: none -> 10.7 us  [the longest x1 7.3 us: on_device(): lax.all_to_all(copies, ('win', 'sta', 'freq'), split_axis=0, concat_axis=...]
  transfers between devices with their start and end apart: 2 -> 2, of which waited for: 1 -> 1; matrix products, arithmetic and copies ran while one was open for 21% -> 7% of each run, Pallas kernels for 0% -> 31%
where the time goes in v1:
time: 87.1 us; the launch traced here: 86.7 us
  Pallas kernels  54.6 us (63%)
  starting transfers between devices  10.7 us (12%)
  local copies, waits for them, and re-layouts  8.67 us (10%)
  blocking collectives  7.4 us (8%)
  waiting for transfers between devices  3.76 us (4%)
    pallas_call x1, Pallas kernels, on_device(): pl.pallas_call(image_kernel, out_shape=jax.ShapeDtypeStruct((windows, NF...  27.6 us
    pallas_call x1, Pallas kernels, on_device(): pl.pallas_call(gather_kernel, out_shape=jax.ShapeDtypeStruct((tables.shap...  26.5 us
    all_to_all x1, blocking collectives, on_device(): lax.all_to_all(result, 'win', split_axis=0, concat_axis=0, tiled=True)  7.4 us
    all_to_all x1, starting transfers between devices, on_device(): lax.all_to_all(copies, ('win', 'sta', 'freq'), split_axis=0, concat_axis=...  7.3 us
    all_to_all x1, waiting for transfers between devices, on_device(): lax.all_to_all(copies, ('win', 'sta', 'freq'), split_axis=0, concat_axis=...  3.75 us
    all_to_all x1, starting transfers between devices, on_device(): lax.all_to_all(mine.transpose(1, 0, 2), 'sta', split_axis=0, concat_axis=...  3.41 us
    reshape x1, local copies, waits for them, and re-layouts, on_device(): blocks = corrections.reshape(stations_dev, groups, cores * windows, nodes)  2 us
    unnamed x11, local copies, waits for them, and re-layouts  1.82 us
  transfers between devices with their start and end apart: 2, of which 1 were waited for; matrix products, arithmetic and copies ran while one was open for 7% of the time, Pallas kernels for 31%

profile of v1, /device:TPU:0, one launch (start us, length us, event | category | flops | bytes accessed | tf_op | source)
XLA Modules:
  0.0 86.7 jit_solution(14709485698038077432)
XLA Ops:
  0.6 0.7 copy.10.bins_ref
  1.4 0.9 %copy-done.1 = bf16[16,2560]{1,0:T(8,128)(2,1)S(1)} copy-done((bf16[16,2560]{1,0:T(8,128)(2,1)S(1)}, bf16[16,2560]{1,0:T(8,128)(2,1)}, u32[]{:S(2)}) %copy-start.1) | copy-done | bytes 81944
  2.3 0.4 dft.1
  2.7 0.8 reshape.33
  3.5 7.3 %all-to-all-start = ((f32[32,1,512]{2,1,0:T(1,128)}), f32[32,1,512]{2,1,0:T(1,128)S(1)}, u32[]{:S(2)}, u32[]{:S(2)}) async-start(f32[32,1,512]{2,1,0:T(1,128)} %reshape.33), calls=%async_computation | async-start | bytes 131072 | tf_op jit(solution)/shard_map/all_to_all | solution.py:155
  10.8 0.0 copy-start
  10.8 2.0 %reshape.29 = bf16[16,8,4,1024]{3,2,1,0:T(4,128)(2,1)S(1)} reshape(bf16[16,32768]{1,0:T(8,128)(2,1)} %param.8) | data formatting | bytes 2097152 | tf_op jit(solution)/shard_map/reshape | solution.py:141
  12.9 0.6 constant_dynamic-slice_fusion
  13.5 0.0 copy-start.2
  13.5 0.0 copy-start.3
  13.5 1.0 %copy.16 = bf16[16,8,1,1024]{3,0,1,2:T(8,128)(2,1)} copy(bf16[16,8,1,1024]{3,2,1,0:T(2,128)(2,1)S(1)} %constant_dynamic-slice_fusion) | data formatting | bytes 524288 | tf_op jit(solution)/shard_map/jit(dynamic_index_in_dim)/dynamic_slice | solution.py:142
  14.5 3.8 %all-to-all-done = f32[32,1,512]{2,1,0:T(1,128)S(1)} async-done(((f32[32,1,512]{2,1,0:T(1,128)}), f32[32,1,512]{2,1,0:T(1,128)S(1)}, u32[]{:S(2)}, u32[]{:S(2)}) %all-to-all-start) | async-done | bytes 65568 | tf_op jit(solution)/shard_map/all_to_all | solution.py:155
  18.2 3.4 %all-to-all-start.1 = ((bf16[8,16,1024]{2,1,0:T(8,128)(2,1)}), bf16[8,16,1024]{2,1,0:T(8,128)(2,1)S(1)}, u32[]{:S(2)}, u32[]{:S(2)}) async-start(bf16[8,16,1024]{2,1,0:T(8,128)(2,1)} %bitcast.16), calls=%async_computation.1 | async-start | bytes 524288 | tf_op jit(solution)/shard_map/all_to_all | solution.py:143
  21.7 0.7 dynamic_slice.8
  22.4 0.0 copy-done
  22.4 26.5 %gather.1.times_ref = f32[16,1024]{1,0:T(8,128)S(1)} custom-call(s32[1,1024]{1,0:T(1,128)S(1)} %bitcast.19, f32[16,32768]{1,0:T(8,128)S(1)} %copy-done), custom_call_target="tpu_custom_call" | custom-call | tf_op jit(solution)/shard_map/gather/pallas_call | solution.py:161
  48.9 0.5 broadcast.1
  49.4 0.8 reduce
  50.2 0.1 reshape.34
  50.4 0.0 all-to-all-done.1
  50.4 27.6 %image.1 = f32[2,24,1024]{2,1,0:T(8,128)S(1)} custom-call(s32[128]{0:T(128)S(1)} %copy-done.3, s32[16]{0:T(128)S(1)} %copy-done.2, f32[2,2,128,32]{3,2,1,0:T(8,128)S(1)} %bitcast.18, bf16[128,1024]{1,0:T(8,128)(2,1)S(1)} %bitcast.17, f32[16,1024]{1,0:T(8,128)S(1)} %gather.1.times_ref), custom_call_target="tpu_custom_call" | custom-call | tf_op jit(solution)/shard_map/image/pallas_call | solution.py:170
  78.0 7.4 %all_to_all.15 = f32[2,24,1024]{2,1,0:T(8,128)S(1)} all-to-all(f32[2,24,1024]{2,1,0:T(8,128)S(1)} %image.1), channel_id=1, replica_groups=mesh['win'=2,'sta'=8,'freq'=2] {'win'}, dimensions={0} | all-to-all | bytes 393216 | tf_op jit(solution)/shard_map/all_to_all | solution.py:182
  85.4 0.7 copy.14
  86.1 0.6 slice.9
  (6 shorter events, 0.1 us)
Async XLA Ops:
  1.4 0.9 %copy-start.1 = (bf16[16,2560]{1,0:T(8,128)(2,1)S(1)}, bf16[16,2560]{1,0:T(8,128)(2,1)}, u32[]{:S(2)}) copy-start(bf16[16,2560]{1,0:T(8,128)(2,1)} %traces_ref.1) | copy-start | bytes 245764
  3.5 14.7 %all-to-all-start = ((f32[32,1,512]{2,1,0:T(1,128)}), f32[32,1,512]{2,1,0:T(1,128)S(1)}, u32[]{:S(2)}, u32[]{:S(2)}) async-start(f32[32,1,512]{2,1,0:T(1,128)} %reshape.33), calls=%async_computation | async-start | bytes 131072 | tf_op jit(solution)/shard_map/all_to_all | solution.py:155
  10.8 11.5 %copy-start = (f32[16,32768]{1,0:T(8,128)S(1)}, f32[16,32768]{1,0:T(8,128)}, u32[]{:S(2)}) copy-start(f32[16,32768]{1,0:T(8,128)} %tables_ref.1) | copy-start | bytes 6291460
  13.5 36.9 %copy-start.2 = (s32[16]{0:T(128)S(1)}, s32[16]{0:T(128)}, u32[]{:S(2)}) copy-start(s32[16]{0:T(128)} %bins_ref.1) | copy-start | bytes 196
  13.5 36.9 %copy-start.3 = (s32[128]{0:T(128)S(1)}, s32[128]{0:T(128)}, u32[]{:S(2)}) copy-start(s32[128]{0:T(128)} %table_of.1) | copy-start | bytes 1540
  18.2 32.1 %all-to-all-start.1 = ((bf16[8,16,1024]{2,1,0:T(8,128)(2,1)}), bf16[8,16,1024]{2,1,0:T(8,128)(2,1)S(1)}, u32[]{:S(2)}, u32[]{:S(2)}) async-start(bf16[8,16,1024]{2,1,0:T(8,128)(2,1)} %bitcast.16), calls=%async_computation.1 | async-start | bytes 524288 | tf_op jit(solution)/shard_map/all_to_all | solution.py:143

commit v2 on v1

v2 whole, which is shorter than its diff:
```python
import functools
import math

import jax
import jax.numpy as jnp
import numpy as np
from jax import lax
from jax.experimental import pallas as pl
from jax.experimental.pallas import tpu as pltpu
from jax.sharding import PartitionSpec as P

NT = 5120
NF = 16
LANES = 128
VMEM_LIMIT = 48 * 1024 * 1024


def chebyshev_fit(func, degree, low, high):
    fit = np.polynomial.chebyshev.Chebyshev.interpolate(func, degree, domain=[low, high])
    return [float(v) for v in fit.convert(kind=np.polynomial.Polynomial).coef]


SIN_HALF = chebyshev_fit(lambda z: np.pi * np.sinc(np.sqrt(z)), 4, 0.0, 0.25)
COS_HALF = chebyshev_fit(lambda z: np.cos(np.pi * np.sqrt(z)), 4, 0.0, 0.25)


def horner(coefs, arg):
    total = coefs[-1]
    for coef in coefs[-2::-1]:
        total = total * arg + coef
    return total


def turn_parts(rest):
    square = rest * rest
    root = math.sqrt(2.0)
    sine_half = rest * horner([root * c for c in SIN_HALF], square)
    cos_half = horner([root * c for c in COS_HALF], square)
    return sine_half * sine_half, sine_half * cos_half


def bins_column(bins_ref):
    rows = lax.broadcasted_iota(jnp.int32, (NF, NF), 0)
    lanes = lax.broadcasted_iota(jnp.int32, (NF, NF), 1)
    square = jnp.broadcast_to(bins_ref[...].astype(jnp.float32), (NF, NF))
    return jnp.sum(jnp.where(rows == lanes, square, 0.0), axis=1, keepdims=True)


def split_bf16(value, terms):
    pieces = []
    for term in range(terms):
        piece = value.astype(jnp.bfloat16)
        pieces.append(piece)
        if term < terms - 1:
            value = value - piece.astype(jnp.float32)
    return pieces


def dft_kernel(half_length, bins_ref, traces_ref, out_ref):
    start = lax.axis_index("freq") * half_length
    bins = bins_column(bins_ref)
    pos = (start + lax.broadcasted_iota(jnp.int32, (NF, half_length), 1)).astype(jnp.float32)
    product = bins * pos
    turns = jnp.round(product * (1.0 / NT))
    rest = (product - turns * NT) * (1.0 / NT)
    versine, sine = turn_parts(rest)
    scale = 1.0 / math.sqrt(NT)
    table = jnp.concatenate([(1.0 - versine) * scale, sine * -scale], axis=0)
    both = jnp.concatenate(split_bf16(table, 2), axis=0)
    sums = lax.dot_general(
        traces_ref[...], both, (((1,), (1,)), ((), ())), preferred_element_type=jnp.float32
    )
    sums = sums[:, : 2 * NF] + sums[:, 2 * NF :]
    pieces = [sums[at : at + 8] for at in range(0, sums.shape[0], 8)]
    pieces.append(jnp.zeros((8, LANES - 2 * NF * len(pieces)), jnp.float32))
    tile = jnp.concatenate(pieces, axis=1)
    for copy in range(out_ref.shape[0]):
        out_ref[copy] = tile


def pick_kernel(nodes, corr_ref, *rest):
    outs, sem = rest[:-1], rest[-1]
    cores, windows = lax.axis_size("freq"), lax.axis_size("win")
    place = lax.axis_index("freq") * windows + lax.axis_index("win")
    groups = lax.axis_size("sta")
    copies = []
    for step, out in enumerate(outs):
        owner = lax.rem(lax.axis_index("sta") + step, groups)
        first = pl.multiple_of((owner * (cores * windows) + place) * nodes, LANES)
        copies.append(pltpu.make_async_copy(corr_ref.at[:, pl.ds(first, nodes)], out, sem.at[step]))
    for copy in copies:
        copy.start()
    for copy in copies:
        copy.wait()


def gather_kernel(ids_ref, tables_ref, out_ref, left_ref, right_ref):
    ntab, grid = tables_ref.shape
    nodes = out_ref.shape[1]
    count = nodes // LANES
    wide = right_ref.shape[0] // 3
    blocks = grid // wide
    windows, cores = lax.axis_size("win"), lax.axis_size("freq")
    place = (lax.axis_index("sta") * cores + lax.axis_index("freq")) * windows + lax.axis_index("win")
    ids = ids_ref[pl.ds(place * count, count), :]
    ids = jnp.concatenate([ids[at : at + 1] for at in range(count)], axis=1)
    low, high = ids & (wide - 1), ids >> (wide.bit_length() - 1)
    spots = lax.broadcasted_iota(jnp.int32, (wide, nodes), 0)
    ones = jnp.where(spots == low, 1.0, 0.0).astype(jnp.bfloat16)
    for term in range(3):
        right_ref[term * wide : (term + 1) * wide, :] = ones
    for block in range(blocks):
        pieces = split_bf16(tables_ref[:, block * wide : (block + 1) * wide], 3)
        left_ref[block * ntab : (block + 1) * ntab, :] = jnp.concatenate(pieces, axis=1)
    found = jnp.zeros((ntab, nodes), jnp.float32)
    step = 16
    for first in range(0, blocks, step):
        rows = left_ref[first * ntab : (first + step) * ntab, :]
        picked = jnp.dot(rows, right_ref[...], preferred_element_type=jnp.float32)
        for block in range(step):
            part = picked[block * ntab : (block + 1) * ntab]
            found = jnp.where(high == first + block, part, found)
    out_ref[...] = found


def image_kernel(stations_dev, table_of, bins_ref, spectra_ref, times_ref, *rest):
    keep_ref, send_ref, turns_ref, weight_ref = rest[-4:]
    corr_refs = rest[:-4]
    stations, nodes = turns_ref.shape
    windows, groups, cores = (lax.axis_size(a) for a in ("win", "sta", "freq"))
    for win in range(windows):
        for group in range(groups):
            at = (win * groups + group) * cores
            tile = spectra_ref[at]
            for core in range(1, cores):
                tile = tile + spectra_ref[at + core]
            for piece in range(stations_dev // 8):
                first = group * stations_dev + piece * 8
                weight_ref[win, first : first + 8, :] = tile[:, piece * 2 * NF : (piece + 1) * 2 * NF]
    for step, corr_ref in enumerate(corr_refs):
        owner = lax.rem(lax.axis_index("sta") + (groups - step), groups)
        rows = corr_ref.shape[0]
        first = pl.multiple_of(owner * stations_dev, 16) if len(corr_refs) > 1 else 0
        turns_ref[pl.ds(first, rows), :] = corr_ref[...].astype(jnp.float32)

    def add_times(station, carry):
        row = pl.ds(station, 1)
        travel = turns_ref[row, :] + times_ref[pl.ds(table_of[station], 1), :]
        turns_ref[row, :] = travel * (1.0 / 256.0)
        return carry

    lax.fori_loop(0, stations, add_times, 0)

    powers = [[] for _ in range(windows)]
    for freq in range(NF):
        bin_at = bins_ref[freq].astype(jnp.float32)

        def body(group, sums):
            rows = pl.ds(pl.multiple_of(group * 8, 8), 8)
            turns = turns_ref[rows, :] * bin_at
            rest = turns - jnp.round(turns)
            versine, sine = turn_parts(rest)
            result = []
            for win in range(windows):
                real = weight_ref[win, rows, freq : freq + 1]
                imag = weight_ref[win, rows, NF + freq : NF + freq + 1]
                result.append(sums[2 * win] + (real * versine + imag * sine))
                result.append(sums[2 * win + 1] + (real * sine - imag * versine))
            return tuple(result)

        zero = jnp.zeros((8, nodes), jnp.float32)
        sums = lax.fori_loop(0, stations // 8, body, (zero,) * (2 * windows))
        for win in range(windows):
            constant = jnp.sum(weight_ref[win, :, freq : freq + 1], axis=0, keepdims=True)
            constant_imag = jnp.sum(weight_ref[win, :, NF + freq : NF + freq + 1], axis=0, keepdims=True)
            real = constant - jnp.sum(sums[2 * win], axis=0, keepdims=True)
            imag = constant_imag + jnp.sum(sums[2 * win + 1], axis=0, keepdims=True)
            powers[win].append(real * real + imag * imag)
    powers = [jnp.concatenate(rows, axis=0) for rows in powers]
    mine = lax.axis_index("win") == 0
    keep_ref[...] = jnp.where(mine, powers[0], powers[1])
    send_ref[...] = jnp.where(mine, powers[1], powers[0])


def finish_kernel(stations, keep_ref, got_ref, spectrum_ref, beam_ref):
    nodes = keep_ref.shape[1]
    win = lax.axis_index("win")
    for place, ref in ((win, keep_ref), (1 - win, got_ref)):
        power = ref[...]
        total = jnp.sum(power, axis=0, keepdims=True)
        at = pl.ds(pl.multiple_of(place * nodes, LANES), nodes)
        spectrum_ref[:, at] = power * (NF / total)
        beam_ref[:, at] = total * (1.0 / (NF * stations))


def on_device(traces, tables, corrections, station_table, node_ids, freq_bins):
    windows, groups, cores = (lax.axis_size(a) for a in ("win", "sta", "freq"))
    stations_dev, grid = corrections.shape
    stations = stations_dev * groups
    devices = windows * groups * cores
    nodes = grid // devices
    ntab = tables.shape[0]
    params = pltpu.CompilerParams(vmem_limit_bytes=VMEM_LIMIT)
    vmem = pl.BlockSpec(memory_space=pltpu.VMEM)
    smem = pl.BlockSpec(memory_space=pltpu.SMEM)
    anywhere = pl.BlockSpec(memory_space=pl.ANY)

    block = jax.ShapeDtypeStruct((stations_dev, nodes), jnp.bfloat16)
    blocks = pl.pallas_call(
        functools.partial(pick_kernel, nodes),
        out_shape=[block] * groups,
        in_specs=[anywhere],
        out_specs=[anywhere] * groups,
        scratch_shapes=[pltpu.SemaphoreType.DMA((groups,))],
        compiler_params=params,
        name="pick",
    )(corrections)
    if groups <= 8:
        corr = [blocks[0]]
        for step in range(1, groups):
            pairs = [(at, (at + step) % groups) for at in range(groups)]
            corr.append(lax.ppermute(blocks[step], "sta", pairs))
    else:
        ordered = jnp.roll(jnp.stack(blocks), lax.axis_index("sta"), axis=0)
        corr = lax.all_to_all(ordered, "sta", split_axis=0, concat_axis=0, tiled=True)
        corr = [corr.reshape(stations, nodes)]

    copies = pl.pallas_call(
        functools.partial(dft_kernel, traces.shape[1]),
        out_shape=jax.ShapeDtypeStruct((devices, 8, LANES), jnp.float32),
        in_specs=[vmem, vmem],
        out_specs=vmem,
        compiler_params=params,
        name="dft",
    )(freq_bins.reshape(1, NF), traces)
    spectra = lax.all_to_all(copies, ("win", "sta", "freq"), split_axis=0, concat_axis=0, tiled=True)

    wide = 512
    times = pl.pallas_call(
        gather_kernel,
        out_shape=jax.ShapeDtypeStruct((ntab, nodes), jnp.float32),
        in_specs=[vmem, vmem],
        out_specs=vmem,
        scratch_shapes=[
            pltpu.VMEM((grid // wide * ntab, 3 * wide), jnp.bfloat16),
            pltpu.VMEM((3 * wide, nodes), jnp.bfloat16),
        ],
        compiler_params=params,
        name="gather",
    )(node_ids.reshape(grid // LANES, LANES), tables)

    half = jax.ShapeDtypeStruct((NF, nodes), jnp.float32)
    keep, send = pl.pallas_call(
        functools.partial(image_kernel, stations_dev),
        out_shape=[half, half],
        in_specs=[smem, smem, vmem, vmem] + [vmem] * len(corr),
        out_specs=[vmem, vmem],
        scratch_shapes=[
            pltpu.VMEM((stations, nodes), jnp.float32),
            pltpu.VMEM((windows, stations, 2 * NF), jnp.float32),
        ],
        compiler_params=params,
        name="image",
    )(station_table, freq_bins, spectra, times, *corr)
    got = lax.ppermute(send, "win", [(0, 1), (1, 0)])
    spectrum, beam_power = pl.pallas_call(
        functools.partial(finish_kernel, stations),
        out_shape=[
            jax.ShapeDtypeStruct((NF, windows * nodes), jnp.float32),
            jax.ShapeDtypeStruct((1, windows * nodes), jnp.float32),
        ],
        in_specs=[vmem, vmem],
        out_specs=[vmem, vmem],
        compiler_params=params,
        name="finish",
    )(keep, got)
    return spectrum, beam_power.reshape(windows * nodes)


def solution(mesh):
    return jax.shard_map(
        on_device,
        mesh=mesh,
        in_specs=(P(("win", "sta"), "freq"), P(), P("sta", None), P(), P(), P()),
        out_specs=(P("win", ("sta", "freq")), P(("win", "sta", "freq"))),
        check_vma=False,
    )
```

time: 87.1 us -> 64.5 us (0.74)
  Pallas kernels: 54.6 us -> 34.1 us
  starting transfers between devices: 10.7 us -> 21.2 us
  blocking collectives: 7.4 us -> 0 us
  local copies, waits for them, and re-layouts: 8.67 us -> 5.27 us
  waiting for transfers between devices: 3.76 us -> 2.81 us
    pallas_call x2 -> x4, Pallas kernels: 54.1 us -> 32.9 us  [the longest x1 28.5 us: on_device(): pl.pallas_call(functools.partial(image_kernel, stations_dev), out_shape=[...]
    ppermute x0 -> x8, starting transfers between devices: none -> 13.9 us  [the longest x7 12.4 us: on_device(): corr.append(lax.ppermute(blocks[step], 'sta', pairs))]
    all_to_all x1 -> x0, blocking collectives: 7.4 us -> none  [on_device(): lax.all_to_all(result, 'win', split_axis=0, concat_axis=0, tiled=True)]
    all_to_all x1, waiting for transfers between devices: 3.75 us -> 0.01 us  [on_device(): lax.all_to_all(copies, ('win', 'sta', 'freq'), split_axis=0, concat_axis=...]
    unnamed x11 -> x14, local copies, waits for them, and re-layouts: 1.82 us -> 5.27 us
    all_to_all x1 -> x0, starting transfers between devices: 3.41 us -> none  [on_device(): lax.all_to_all(mine.transpose(1, 0, 2), 'sta', split_axis=0, concat_axis=...]
    reshape x3 -> x0, local copies, waits for them, and re-layouts: 3.4 us -> none  [the longest x1 2 us: on_device(): blocks = corrections.reshape(stations_dev, groups, cores * windows, nodes)]
    ppermute x0 -> x8, waiting for transfers between devices: none -> 2.81 us  [the longest x1 2.79 us: on_device(): got = lax.ppermute(send, 'win', [(0, 1), (1, 0)])]
  transfers between devices with their start and end apart: 2 -> 9, of which waited for: 1 -> 1; matrix products, arithmetic and copies ran while one was open for 7% -> 0% of each run, Pallas kernels for 31% -> 6%
where the time goes in v2:
time: 64.5 us; the launch traced here: 64.2 us
  Pallas kernels  34.1 us (53%)
  starting transfers between devices  21.2 us (33%)
  local copies, waits for them, and re-layouts  5.27 us (8%)
  waiting for transfers between devices  2.81 us (4%)
  between operations  0.76 us (1%)
    pallas_call x1, Pallas kernels, on_device(): pl.pallas_call(functools.partial(image_kernel, stations_dev), out_shape=[...  28.5 us
    ppermute x7, starting transfers between devices, on_device(): corr.append(lax.ppermute(blocks[step], 'sta', pairs))  12.4 us
    all_to_all x1, starting transfers between devices, on_device(): lax.all_to_all(copies, ('win', 'sta', 'freq'), split_axis=0, concat_axis=...  7.3 us
    unnamed x14, local copies, waits for them, and re-layouts  5.27 us
    pallas_call x1, Pallas kernels, on_device(): pl.pallas_call(gather_kernel, out_shape=jax.ShapeDtypeStruct((ntab, nodes...  3.49 us
    ppermute x1, waiting for transfers between devices, on_device(): got = lax.ppermute(send, 'win', [(0, 1), (1, 0)])  2.79 us
    ppermute x1, starting transfers between devices, on_device(): got = lax.ppermute(send, 'win', [(0, 1), (1, 0)])  1.54 us
  transfers between devices with their start and end apart: 9, of which 1 were waited for; matrix products, arithmetic and copies ran while one was open for 0% of the time, Pallas kernels for 6%

profile of v2, /device:TPU:0, one launch (start us, length us, event | category | flops | bytes accessed | tf_op | source)
XLA Modules:
  0.0 64.2 jit_solution(448318541359512032)
XLA Ops:
  0.7 0.9 %copy-done.3 = bf16[16,2560]{1,0:T(8,128)(2,1)S(1)} copy-done((bf16[16,2560]{1,0:T(8,128)(2,1)S(1)}, bf16[16,2560]{1,0:T(8,128)(2,1)}, u32[]{:S(2)}) %copy-start.3) | copy-done | bytes 81944
  1.6 0.7 %copy-done.4 = s32[16]{0:T(128)S(1)} copy-done((s32[16]{0:T(128)S(1)}, s32[16]{0:T(128)}, u32[]{:S(2)}) %copy-start.4) | copy-done | bytes 88
  2.2 1.2 %dft.1 = f32[32,8,128]{2,1,0:T(8,128)} custom-call(s32[1,16]{1,0:T(1,128)S(1)} %bitcast.4, bf16[16,2560]{1,0:T(8,128)(2,1)S(1)} %copy-done.3), custom_call_target="tpu_custom_call" | custom-call | tf_op jit(solution)/shard_map/dft/pallas_call | solution.py:228
  3.4 7.3 %all-to-all-start = ((f32[32,8,128]{2,1,0:T(8,128)}), f32[32,8,128]{2,1,0:T(8,128)S(1)}, u32[]{:S(2)}, u32[]{:S(2)}) async-start(f32[32,8,128]{2,1,0:T(8,128)} %dft.1), calls=%async_computation | async-start | bytes 262144 | tf_op jit(solution)/shard_map/all_to_all | solution.py:236
  10.7 0.0 copy-start.1
  10.7 1.2 %copy-done.1 = bf16[16,32768]{1,0:T(8,128)(2,1)S(1)} copy-done((bf16[16,32768]{1,0:T(8,128)(2,1)S(1)}, bf16[16,32768]{1,0:T(8,128)(2,1)}, u32[]{:S(2)}) %copy-start.1) | copy-done | bytes 1048600
  11.9 0.3 pick.1
  12.2 1.8 %collective-permute-start = (bf16[16,1024]{1,0:T(8,128)(2,1)S(1)}, bf16[16,1024]{1,0:T(8,128)(2,1)S(1)}, u32[]{:S(2)}, u32[]{:S(2)}) collective-permute-start(bf16[16,1024]{1,0:T(8,128)(2,1)S(1)} %get-tuple-element.15), channel_id=1, source_target_pairs={{0,2},{2,4},{4,6},{6,8},{8,10},{10,12},{12,14},{14,0},{1,3},{3,5},... | collective-permute-start | bytes 98312 | tf_op jit(solution)/shard_map/ppermute | solution.py:222
  14.0 1.5 %collective-permute-start.1 = (bf16[16,1024]{1,0:T(8,128)(2,1)S(1)}, bf16[16,1024]{1,0:T(8,128)(2,1)S(1)}, u32[]{:S(2)}, u32[]{:S(2)}) collective-permute-start(bf16[16,1024]{1,0:T(8,128)(2,1)S(1)} %get-tuple-element.16), channel_id=1, source_target_pairs={{0,4},{2,6},{4,8},{6,10},{8,12},{10,14},{12,0},{14,2},{1,5},{3,7},... | collective-permute-start | bytes 98312 | tf_op jit(solution)/shard_map/ppermute | solution.py:222
  15.5 2.4 %collective-permute-start.2 = (bf16[16,1024]{1,0:T(8,128)(2,1)S(1)}, bf16[16,1024]{1,0:T(8,128)(2,1)S(1)}, u32[]{:S(2)}, u32[]{:S(2)}) collective-permute-start(bf16[16,1024]{1,0:T(8,128)(2,1)S(1)} %get-tuple-element.17), channel_id=1, source_target_pairs={{0,6},{2,8},{4,10},{6,12},{8,14},{10,0},{12,2},{14,4},{1,7},{3,9},... | collective-permute-start | bytes 98312 | tf_op jit(solution)/shard_map/ppermute | solution.py:222
  17.9 1.4 %collective-permute-start.3 = (bf16[16,1024]{1,0:T(8,128)(2,1)S(1)}, bf16[16,1024]{1,0:T(8,128)(2,1)S(1)}, u32[]{:S(2)}, u32[]{:S(2)}) collective-permute-start(bf16[16,1024]{1,0:T(8,128)(2,1)S(1)} %get-tuple-element.18), channel_id=1, source_target_pairs={{0,8},{2,10},{4,12},{6,14},{8,0},{10,2},{12,4},{14,6},{1,9},{3,11}... | collective-permute-start | bytes 98312 | tf_op jit(solution)/shard_map/ppermute | solution.py:222
  19.3 2.4 %collective-permute-start.4 = (bf16[16,1024]{1,0:T(8,128)(2,1)S(1)}, bf16[16,1024]{1,0:T(8,128)(2,1)S(1)}, u32[]{:S(2)}, u32[]{:S(2)}) collective-permute-start(bf16[16,1024]{1,0:T(8,128)(2,1)S(1)} %get-tuple-element.19), channel_id=1, source_target_pairs={{0,10},{2,12},{4,14},{6,0},{8,2},{10,4},{12,6},{14,8},{1,11},{3,13... | collective-permute-start | bytes 98312 | tf_op jit(solution)/shard_map/ppermute | solution.py:222
  21.7 1.4 %collective-permute-start.5 = (bf16[16,1024]{1,0:T(8,128)(2,1)S(1)}, bf16[16,1024]{1,0:T(8,128)(2,1)S(1)}, u32[]{:S(2)}, u32[]{:S(2)}) collective-permute-start(bf16[16,1024]{1,0:T(8,128)(2,1)S(1)} %get-tuple-element.20), channel_id=1, source_target_pairs={{0,12},{2,14},{4,0},{6,2},{8,4},{10,6},{12,8},{14,10},{1,13},{3,15... | collective-permute-start | bytes 98312 | tf_op jit(solution)/shard_map/ppermute | solution.py:222
  23.1 0.0 collective-permute-done.1.rest_2_
  23.1 1.5 %collective-permute-start.6 = (bf16[16,1024]{1,0:T(8,128)(2,1)S(1)}, bf16[16,1024]{1,0:T(8,128)(2,1)S(1)}, u32[]{:S(2)}, u32[]{:S(2)}) collective-permute-start(bf16[16,1024]{1,0:T(8,128)(2,1)S(1)} %get-tuple-element.21), channel_id=1, source_target_pairs={{0,14},{2,0},{4,2},{6,4},{8,6},{10,8},{12,10},{14,12},{1,15},{3,1}... | collective-permute-start | bytes 98312 | tf_op jit(solution)/shard_map/ppermute | solution.py:222
  24.6 1.6 %copy-done = f32[16,32768]{1,0:T(8,128)S(1)} copy-done((f32[16,32768]{1,0:T(8,128)S(1)}, f32[16,32768]{1,0:T(8,128)}, u32[]{:S(2)}) %copy-start) | copy-done | bytes 2097176
  26.2 0.9 %copy-done.2 = s32[32768]{0:T(1024)S(1)} copy-done((s32[32768]{0:T(1024)S(1)}, s32[32768]{0:T(1024)}, u32[]{:S(2)}) %copy-start.2) | copy-done | bytes 131096
  27.1 3.5 %gather.1.times_ref = f32[16,1024]{1,0:T(8,128)S(1)} custom-call(s32[256,128]{1,0:T(8,128)S(1)} %bitcast.3, f32[16,32768]{1,0:T(8,128)S(1)} %copy-done), custom_call_target="tpu_custom_call" | custom-call | tf_op jit(solution)/shard_map/gather/pallas_call | solution.py:239
  30.6 0.0 collective-permute-done.3.rest_4_
  30.6 0.0 collective-permute-done.6.rest_7_
  30.7 28.5 %image.1 = (f32[16,1024]{1,0:T(8,128)S(1)}, f32[16,1024]{1,0:T(8,128)S(1)}) custom-call(s32[128]{0:T(128)S(1)} %copy-done.6, s32[16]{0:T(128)S(1)} %copy-done.5, f32[32,8,128]{2,1,0:T(8,128)S(1)} %all-to-all-done.spectra_ref, f32[16,1024]{1,0:T(8,128)S(1)} %gather.1.times_ref, bf16[16,1024]{1,0:T(8,128)(2,1)S(1)} %get-tuple-element.14.rest_0_, ...), custom_call_target="tpu_custom_call" | custom-call | tf_op jit(solution)/shard_map/image/pallas_call | solution.py:253
  59.2 1.5 %collective-permute-start.7 = (f32[16,1024]{1,0:T(8,128)S(1)}, f32[16,1024]{1,0:T(8,128)S(1)}, u32[]{:S(2)}, u32[]{:S(2)}) collective-permute-start(f32[16,1024]{1,0:T(8,128)S(1)} %get-tuple-element.23), channel_id=1, source_target_pairs={{0,16},{16,0},{1,17},{17,1},{2,18},{18,2},{3,19},{19,3},{4,20},{20... | collective-permute-start | bytes 196616 | tf_op jit(solution)/shard_map/ppermute | solution.py:265
  60.7 2.8 %collective-permute-done.7.got_ref = f32[16,1024]{1,0:T(8,128)S(1)} collective-permute-done((f32[16,1024]{1,0:T(8,128)S(1)}, f32[16,1024]{1,0:T(8,128)S(1)}, u32[]{:S(2)}, u32[]{:S(2)}) %collective-permute-start.7) | collective-permute-done | bytes 65568 | tf_op jit(solution)/shard_map/ppermute | solution.py:265
  63.5 0.7 %finish.1 = (f32[16,2048]{1,0:T(8,128)}, f32[1,2048]{1,0:T(1,128)}) custom-call(f32[16,1024]{1,0:T(8,128)S(1)} %get-tuple-element.22.keep_ref, f32[16,1024]{1,0:T(8,128)S(1)} %collective-permute-done.7.got_ref), custom_call_target="tpu_custom_call" | custom-call | tf_op jit(solution)/shard_map/finish/pallas_call | solution.py:266
  (13 shorter events, 0.0 us)
Async XLA Ops:
  0.6 30.0 %copy-start.5 = (s32[16]{0:T(128)S(1)}, s32[16]{0:T(128)}, u32[]{:S(2)}) copy-start(s32[16]{0:T(128)} %bins_ref.1) | copy-start | bytes 196
  0.6 30.0 %copy-start.6 = (s32[128]{0:T(128)S(1)}, s32[128]{0:T(128)}, u32[]{:S(2)}) copy-start(s32[128]{0:T(128)} %table_of.1) | copy-start | bytes 1540
  0.6 0.9 %copy-start.3 = (bf16[16,2560]{1,0:T(8,128)(2,1)S(1)}, bf16[16,2560]{1,0:T(8,128)(2,1)}, u32[]{:S(2)}) copy-start(bf16[16,2560]{1,0:T(8,128)(2,1)} %traces_ref.1) | copy-start | bytes 245764
  1.5 0.7 %copy-start.4 = (s32[16]{0:T(128)S(1)}, s32[16]{0:T(128)}, u32[]{:S(2)}) copy-start(s32[16]{0:T(128)} %bins_ref.1) | copy-start | bytes 196
  3.4 27.3 %all-to-all-start = ((f32[32,8,128]{2,1,0:T(8,128)}), f32[32,8,128]{2,1,0:T(8,128)S(1)}, u32[]{:S(2)}, u32[]{:S(2)}) async-start(f32[32,8,128]{2,1,0:T(8,128)} %dft.1), calls=%async_computation | async-start | bytes 262144 | tf_op jit(solution)/shard_map/all_to_all | solution.py:236
  10.7 1.2 %copy-start.1 = (bf16[16,32768]{1,0:T(8,128)(2,1)S(1)}, bf16[16,32768]{1,0:T(8,128)(2,1)}, u32[]{:S(2)}) copy-start(bf16[16,32768]{1,0:T(8,128)(2,1)} %corr_ref.1) | copy-start | bytes 3145732
  12.2 9.5 %collective-permute-start = (bf16[16,1024]{1,0:T(8,128)(2,1)S(1)}, bf16[16,1024]{1,0:T(8,128)(2,1)S(1)}, u32[]{:S(2)}, u32[]{:S(2)}) collective-permute-start(bf16[16,1024]{1,0:T(8,128)(2,1)S(1)} %get-tuple-element.15), channel_id=1, source_target_pairs={{0,2},{2,4},{4,6},{6,8},{8,10},{10,12},{12,14},{14,0},{1,3},{3,5},... | collective-permute-start | bytes 98312 | tf_op jit(solution)/shard_map/ppermute | solution.py:222
  14.0 9.1 %collective-permute-start.1 = (bf16[16,1024]{1,0:T(8,128)(2,1)S(1)}, bf16[16,1024]{1,0:T(8,128)(2,1)S(1)}, u32[]{:S(2)}, u32[]{:S(2)}) collective-permute-start(bf16[16,1024]{1,0:T(8,128)(2,1)S(1)} %get-tuple-element.16), channel_id=1, source_target_pairs={{0,4},{2,6},{4,8},{6,10},{8,12},{10,14},{12,0},{14,2},{1,5},{3,7},... | collective-permute-start | bytes 98312 | tf_op jit(solution)/shard_map/ppermute | solution.py:222
  15.5 15.1 %collective-permute-start.2 = (bf16[16,1024]{1,0:T(8,128)(2,1)S(1)}, bf16[16,1024]{1,0:T(8,128)(2,1)S(1)}, u32[]{:S(2)}, u32[]{:S(2)}) collective-permute-start(bf16[16,1024]{1,0:T(8,128)(2,1)S(1)} %get-tuple-element.17), channel_id=1, source_target_pairs={{0,6},{2,8},{4,10},{6,12},{8,14},{10,0},{12,2},{14,4},{1,7},{3,9},... | collective-permute-start | bytes 98312 | tf_op jit(solution)/shard_map/ppermute | solution.py:222
  17.9 12.7 %collective-permute-start.3 = (bf16[16,1024]{1,0:T(8,128)(2,1)S(1)}, bf16[16,1024]{1,0:T(8,128)(2,1)S(1)}, u32[]{:S(2)}, u32[]{:S(2)}) collective-permute-start(bf16[16,1024]{1,0:T(8,128)(2,1)S(1)} %get-tuple-element.18), channel_id=1, source_target_pairs={{0,8},{2,10},{4,12},{6,14},{8,0},{10,2},{12,4},{14,6},{1,9},{3,11}... | collective-permute-start | bytes 98312 | tf_op jit(solution)/shard_map/ppermute | solution.py:222
  19.3 11.3 %collective-permute-start.4 = (bf16[16,1024]{1,0:T(8,128)(2,1)S(1)}, bf16[16,1024]{1,0:T(8,128)(2,1)S(1)}, u32[]{:S(2)}, u32[]{:S(2)}) collective-permute-start(bf16[16,1024]{1,0:T(8,128)(2,1)S(1)} %get-tuple-element.19), channel_id=1, source_target_pairs={{0,10},{2,12},{4,14},{6,0},{8,2},{10,4},{12,6},{14,8},{1,11},{3,13... | collective-permute-start | bytes 98312 | tf_op jit(solution)/shard_map/ppermute | solution.py:222
  21.7 8.9 %collective-permute-start.5 = (bf16[16,1024]{1,0:T(8,128)(2,1)S(1)}, bf16[16,1024]{1,0:T(8,128)(2,1)S(1)}, u32[]{:S(2)}, u32[]{:S(2)}) collective-permute-start(bf16[16,1024]{1,0:T(8,128)(2,1)S(1)} %get-tuple-element.20), channel_id=1, source_target_pairs={{0,12},{2,14},{4,0},{6,2},{8,4},{10,6},{12,8},{14,10},{1,13},{3,15... | collective-permute-start | bytes 98312 | tf_op jit(solution)/shard_map/ppermute | solution.py:222
  23.1 7.5 %collective-permute-start.6 = (bf16[16,1024]{1,0:T(8,128)(2,1)S(1)}, bf16[16,1024]{1,0:T(8,128)(2,1)S(1)}, u32[]{:S(2)}, u32[]{:S(2)}) collective-permute-start(bf16[16,1024]{1,0:T(8,128)(2,1)S(1)} %get-tuple-element.21), channel_id=1, source_target_pairs={{0,14},{2,0},{4,2},{6,4},{8,6},{10,8},{12,10},{14,12},{1,15},{3,1}... | collective-permute-start | bytes 98312 | tf_op jit(solution)/shard_map/ppermute | solution.py:222
  24.6 1.6 %copy-start = (f32[16,32768]{1,0:T(8,128)S(1)}, f32[16,32768]{1,0:T(8,128)}, u32[]{:S(2)}) copy-start(f32[16,32768]{1,0:T(8,128)} %tables_ref.1) | copy-start | bytes 6291460
  26.2 0.9 %copy-start.2 = (s32[32768]{0:T(1024)S(1)}, s32[32768]{0:T(1024)}, u32[]{:S(2)}) copy-start(s32[32768]{0:T(1024)} %param.10) | copy-start | bytes 393220
  59.2 4.3 %collective-permute-start.7 = (f32[16,1024]{1,0:T(8,128)S(1)}, f32[16,1024]{1,0:T(8,128)S(1)}, u32[]{:S(2)}, u32[]{:S(2)}) collective-permute-start(f32[16,1024]{1,0:T(8,128)S(1)} %get-tuple-element.23), channel_id=1, source_target_pairs={{0,16},{16,0},{1,17},{17,1},{2,18},{18,2},{3,19},{19,3},{4,20},{20... | collective-permute-start | bytes 196616 | tf_op jit(solution)/shard_map/ppermute | solution.py:265

commit v3 on v2

v3 whole, which is shorter than its diff:
```python
import functools
import math

import jax
import jax.numpy as jnp
import numpy as np
from jax import lax
from jax.experimental import pallas as pl
from jax.experimental.pallas import tpu as pltpu
from jax.sharding import PartitionSpec as P

NT = 5120
NF = 16
LANES = 128
DEGREES = 32
REACH = 1.5
TERMS = 3
VMEM_LIMIT = 48 * 1024 * 1024


def chebyshev_fit(func, degree, low, high):
    fit = np.polynomial.chebyshev.Chebyshev.interpolate(func, degree, domain=[low, high])
    return [float(v) for v in fit.convert(kind=np.polynomial.Polynomial).coef]


SIN_HALF = chebyshev_fit(lambda z: np.pi * np.sinc(np.sqrt(z)), 4, 0.0, 0.25)
COS_HALF = chebyshev_fit(lambda z: np.cos(np.pi * np.sqrt(z)), 4, 0.0, 0.25)


def horner(coefs, arg):
    total = coefs[-1]
    for coef in coefs[-2::-1]:
        total = total * arg + coef
    return total


def turn_parts(rest):
    square = rest * rest
    root = math.sqrt(2.0)
    sine_half = rest * horner([root * c for c in SIN_HALF], square)
    cos_half = horner([root * c for c in COS_HALF], square)
    return sine_half * sine_half, sine_half * cos_half


def cos_sin(turns):
    versine, sine = turn_parts(turns - jnp.round(turns))
    return 1.0 - versine, sine


def bins_column(bins_ref):
    rows = lax.broadcasted_iota(jnp.int32, (NF, NF), 0)
    lanes = lax.broadcasted_iota(jnp.int32, (NF, NF), 1)
    square = jnp.broadcast_to(bins_ref[...].astype(jnp.float32), (NF, NF))
    return jnp.sum(jnp.where(rows == lanes, square, 0.0), axis=1, keepdims=True)


def split_bf16(value, terms):
    pieces = []
    for term in range(terms):
        piece = value.astype(jnp.bfloat16)
        pieces.append(piece)
        if term < terms - 1:
            value = value - piece.astype(jnp.float32)
    return pieces


def send_kernel(nodes, bins_ref, traces_ref, corr_ref, out_ref, *rest):
    sems = rest[-1]
    devices, rows, width = out_ref.shape
    share = width - LANES
    half_length = traces_ref.shape[1]
    copies = []
    if share:
        windows, groups, cores = (lax.axis_size(a) for a in ("win", "sta", "freq"))
        place = lax.axis_index("win") * cores + lax.axis_index("freq")
        for dev in range(devices):
            win, sta, core = dev // (groups * cores), dev // cores % groups, dev % cores
            first = ((sta * cores + core) * windows + win) * nodes
            first = pl.multiple_of(first + place * share, LANES)
            copies.append(
                pltpu.make_async_copy(
                    corr_ref.at[:, pl.ds(first, share)], out_ref.at[dev, :, pl.ds(0, share)], sems.at[dev]
                )
            )
    for copy in copies:
        copy.start()
    start = lax.axis_index("freq") * half_length
    bins = bins_column(bins_ref)
    pos = (start + lax.broadcasted_iota(jnp.int32, (NF, half_length), 1)).astype(jnp.float32)
    product = bins * pos
    turns = jnp.round(product * (1.0 / NT))
    rest = (product - turns * NT) * (1.0 / NT)
    versine, sine = turn_parts(rest)
    scale = 1.0 / math.sqrt(NT)
    table = jnp.concatenate([(1.0 - versine) * scale, sine * -scale], axis=0)
    both = jnp.concatenate(split_bf16(table, 2), axis=0)
    sums = lax.dot_general(
        traces_ref[...], both, (((1,), (1,)), ((), ())), preferred_element_type=jnp.float32
    )
    sums = sums[:, : 2 * NF] + sums[:, 2 * NF :]
    pieces = split_bf16(sums, TERMS) + [jnp.zeros((rows, LANES - 2 * NF * TERMS), jnp.bfloat16)]
    tile = jnp.concatenate([piece.astype(jnp.float32) for piece in pieces], axis=1).astype(jnp.bfloat16)
    for dev in range(devices):
        out_ref[dev, :, share:] = tile
    for copy in copies:
        copy.wait()


def pick_columns(ids_ref, tables_ref, nodes, left_ref, right_ref):
    ntab, grid = tables_ref.shape
    count = nodes // LANES
    wide = right_ref.shape[0] // 3
    blocks = grid // wide
    windows, cores = lax.axis_size("win"), lax.axis_size("freq")
    place = (lax.axis_index("sta") * cores + lax.axis_index("freq")) * windows + lax.axis_index("win")
    ids = ids_ref[pl.ds(place * count, count), :]
    ids = jnp.concatenate([ids[at : at + 1] for at in range(count)], axis=1)
    low, high = ids & (wide - 1), ids >> (wide.bit_length() - 1)
    spots = lax.broadcasted_iota(jnp.int32, (wide, nodes), 0)
    ones = jnp.where(spots == low, 1.0, 0.0).astype(jnp.bfloat16)
    for term in range(3):
        right_ref[term * wide : (term + 1) * wide, :] = ones
    for block in range(blocks):
        pieces = split_bf16(tables_ref[:, block * wide : (block + 1) * wide], 3)
        left_ref[block * ntab : (block + 1) * ntab, :] = jnp.concatenate(pieces, axis=1)
    found = jnp.zeros((ntab, nodes), jnp.float32)
    step = 16
    for first in range(0, blocks, step):
        rows = left_ref[first * ntab : (first + step) * ntab, :]
        picked = jnp.dot(rows, right_ref[...], preferred_element_type=jnp.float32)
        for block in range(step):
            part = picked[block * ntab : (block + 1) * ntab]
            found = jnp.where(high == first + block, part, found)
    return found


def chebyshev_coefs(bins_ref):
    shape = (DEGREES, DEGREES)
    degree = lax.broadcasted_iota(jnp.int32, shape, 0)
    node = lax.broadcasted_iota(jnp.int32, shape, 1)
    period = 4 * DEGREES
    weight, _ = cos_sin((degree * (2 * node + 1) & (period - 1)).astype(jnp.float32) * (1.0 / period))
    weight = weight * jnp.where(degree == 0, 1.0 / DEGREES, 2.0 / DEGREES)
    even = jnp.where(degree % 2 == 0, weight, 0.0)
    odd = jnp.where(degree % 2 == 1, weight, 0.0)
    row = bins_ref[...].astype(jnp.float32)
    bins = jnp.concatenate([row] * (LANES // NF), axis=1)
    at = lax.broadcasted_iota(jnp.int32, (DEGREES, LANES), 0).astype(jnp.float32)
    spot, _ = cos_sin((2.0 * at + 1.0) * (1.0 / period))
    cosine, sine = cos_sin(bins * (spot * (REACH / 256.0)))
    dot = functools.partial(jnp.dot, precision=lax.Precision.HIGHEST, preferred_element_type=jnp.float32)
    return dot(even, cosine) + dot(odd, sine)


def station_order(table_row):
    count = table_row.shape[1]
    shape = (count, count)
    here = lax.broadcasted_iota(jnp.int32, shape, 0)
    there = lax.broadcasted_iota(jnp.int32, shape, 1)
    key_row = table_row * count + there[:1]
    spread = jnp.broadcast_to(key_row, shape)
    key_column = jnp.sum(jnp.where(here == there, spread, 0), axis=1, keepdims=True)
    rank = jnp.sum(jnp.where(key_column < key_row, 1, 0), axis=0, keepdims=True)
    table_column = key_column // count
    bound = lax.broadcasted_iota(jnp.int32, (count, LANES), 1)
    starts = jnp.sum(jnp.where(table_column < bound, 1, 0), axis=0, keepdims=True)
    first = lax.broadcasted_iota(jnp.int32, (count, LANES), 1) * 8
    place_column = jnp.sum(jnp.where(here == there, jnp.broadcast_to(rank, shape), 0), axis=1, keepdims=True)
    low = jnp.sum(jnp.where(place_column == first, table_column, 0), axis=0, keepdims=True)
    high = jnp.sum(jnp.where(place_column == first + 7, table_column, 0), axis=0, keepdims=True)
    plan = jnp.concatenate([starts, low, high, jnp.zeros((5, LANES), jnp.int32)], axis=0)
    return rank, plan


def prepare_kernel(
    bins_ref, table_ref, ids_ref, tables_ref, cos_ref, sin_ref, coef_ref, sorter_ref, plan_ref, left_ref, right_ref
):
    nodes = cos_ref.shape[2]
    coef_ref[...] = chebyshev_coefs(bins_ref)
    rank, plan = station_order(table_ref[...])
    plan_ref[...] = plan
    count = table_ref.shape[1]
    place = lax.broadcasted_iota(jnp.int32, (count, count), 0)
    sorter_ref[...] = jnp.where(place == rank, 1.0, 0.0).astype(jnp.bfloat16)
    turns = pick_columns(ids_ref, tables_ref, nodes, left_ref, right_ref) * (1.0 / 256.0)
    bins = bins_column(bins_ref)
    for table in range(tables_ref.shape[0]):
        cosine, sine = cos_sin(bins * turns[table : table + 1])
        cos_ref[table] = cosine
        sin_ref[table] = sine


def image_kernel(merged, stations_dev, plan_ref, sorter_ref, coef_ref, cos_ref, sin_ref, *rest):
    keep_ref, send_ref, place_ref, weight_ref, sums_ref, basis_a, left_a, basis_b, left_b = rest[-9:]
    stations, nodes = place_ref.shape
    windows, groups, cores = (lax.axis_size(a) for a in ("win", "sta", "freq"))
    ntab = cos_ref.shape[0]
    sorter = sorter_ref[...]
    block_ref = rest[0]
    width = block_ref.shape[2]
    rows_of = lambda win, core: [(win * groups + group) * cores + core for group in range(groups)]

    scale = 1.0 / REACH
    if merged:
        share = width - LANES
        for win in range(windows):
            for core in range(cores):
                part = jnp.concatenate([block_ref[at, :, :share] for at in rows_of(win, core)], axis=0)
                found = jnp.dot(sorter, part, preferred_element_type=jnp.float32)
                first = (win * cores + core) * share
                place_ref[:, first : first + share] = found * scale
    else:
        found = jnp.dot(sorter, rest[1][...], preferred_element_type=jnp.float32)
        place_ref[...] = found * scale

    even, odd = [], []
    for win in range(windows):
        total = None
        for core in range(cores):
            part = jnp.concatenate([block_ref[at, :, width - LANES :] for at in rows_of(win, core)], axis=0)
            part = part.astype(jnp.float32)
            total = part if total is None else total + part
        value = sum(total[:, 2 * NF * term : 2 * NF * (term + 1)] for term in range(TERMS))
        even.append(value)
        odd.append(jnp.concatenate([-value[:, NF:], value[:, :NF]], axis=1))
    both = jnp.concatenate(even + even + odd + odd, axis=1)
    found = None
    for piece in split_bf16(both, 3):
        part = jnp.dot(sorter, piece, preferred_element_type=jnp.float32)
        found = part if found is None else found + part
    weight_ref[...] = found
    sums_ref[...] = jnp.zeros_like(sums_ref)
    chunk = min(256, nodes)
    lanes = 2 * windows * 2 * NF
    slot = lax.broadcasted_iota(jnp.int32, (8, lanes), 1) // (lanes // 2)
    spot = lax.broadcasted_iota(jnp.int32, (8, lanes), 0)

    def make_left(group, table, left_ref):
        here = spot + group * 8
        low = jnp.where(slot == 0, plan_ref[0, table], plan_ref[0, table + 1])
        high = jnp.where(slot == 0, plan_ref[0, table + 1], plan_ref[0, table + 2])
        mask = (here >= low) & (here < high)
        rows = pl.ds(pl.multiple_of(group * 8, 8), 8)
        sides = [
            jnp.where(mask, weight_ref[rows, :lanes], 0.0),
            jnp.where(mask, weight_ref[rows, lanes:], 0.0),
        ]
        for half in range(DEGREES * 8 // LANES):
            per = LANES // 8
            tall = jnp.concatenate(
                [sides[k % 2] * coef_ref[k : k + 1, :lanes] for k in range(half * per, (half + 1) * per)], axis=0
            )
            high, low = split_bf16(tall.T, 2)
            at = half * LANES
            left_ref[:, at : at + LANES] = high
            left_ref[:, DEGREES * 8 + at : DEGREES * 8 + at + LANES] = low

    def make_basis(group, basis_ref):
        arg = place_ref[pl.ds(pl.multiple_of(group * 8, 8), 8), :]
        twice = arg + arg
        before, now = jnp.ones_like(arg), arg
        for degree in range(0, DEGREES, 2):
            pair = jnp.concatenate([before, now], axis=0)
            high, low = split_bf16(pair, 2)
            basis_ref[degree * 8 : degree * 8 + 16, :] = high
            basis_ref[(DEGREES + degree) * 8 : (DEGREES + degree) * 8 + 16, :] = low
            before = twice * now - before
            now = twice * before - now

    def add_tables(table, basis_ref, left_ref):
        depth = DEGREES * 8
        other = jnp.minimum(table + 1, ntab - 1)
        half = lanes // 2
        for first in range(0, nodes, chunk):
            at = slice(first, first + chunk)
            high = left_ref[:, :depth]
            got = jnp.dot(high, basis_ref[:depth, at], preferred_element_type=jnp.float32)
            got = got + jnp.dot(high, basis_ref[depth:, at], preferred_element_type=jnp.float32)
            got = got + jnp.dot(left_ref[:, depth:], basis_ref[:depth, at], preferred_element_type=jnp.float32)
            cos_a, sin_a = cos_ref[table, :, at], sin_ref[table, :, at]
            cos_b, sin_b = cos_ref[other, :, at], sin_ref[other, :, at]
            for win in range(windows):
                row = win * 2 * NF
                real_a, imag_a = got[row : row + NF], got[row + NF : row + 2 * NF]
                real_b, imag_b = got[half + row : half + row + NF], got[half + row + NF : half + row + 2 * NF]
                sums_ref[row : row + NF, at] += (real_a * cos_a - imag_a * sin_a) + (real_b * cos_b - imag_b * sin_b)
                sums_ref[row + NF : row + 2 * NF, at] += (real_a * sin_a + imag_a * cos_a) + (
                    real_b * sin_b + imag_b * cos_b
                )

    def more_tables(group, basis_ref, left_ref):
        first, last = plan_ref[1, group], plan_ref[2, group]

        def step(turn, carry):
            table = first + 2 * turn
            make_left(group, table, left_ref)
            add_tables(table, basis_ref, left_ref)
            return carry

        lax.fori_loop(1, (last - first) // 2 + 1, step, 0)

    total_groups = stations // 8
    make_left(0, plan_ref[1, 0], left_a)
    make_basis(0, basis_a)

    def body(pair, carry):
        group = pair * 2
        make_left(group + 1, plan_ref[1, group + 1], left_b)
        make_basis(group + 1, basis_b)
        add_tables(plan_ref[1, group], basis_a, left_a)
        more_tables(group, basis_a, left_a)
        after = jnp.minimum(group + 2, total_groups - 1)
        make_left(after, plan_ref[1, after], left_a)
        make_basis(after, basis_a)
        add_tables(plan_ref[1, group + 1], basis_b, left_b)
        more_tables(group + 1, basis_b, left_b)
        return carry

    lax.fori_loop(0, total_groups // 2, body, 0)
    powers = []
    for win in range(windows):
        row = win * 2 * NF
        real, imag = sums_ref[row : row + NF, :], sums_ref[row + NF : row + 2 * NF, :]
        powers.append(real * real + imag * imag)
    mine = lax.axis_index("win") == 0
    keep_ref[...] = jnp.where(mine, powers[0], powers[1])
    send_ref[...] = jnp.where(mine, powers[1], powers[0])


def finish_kernel(stations, keep_ref, got_ref, spectrum_ref, beam_ref):
    nodes = keep_ref.shape[1]
    win = lax.axis_index("win")
    for place, ref in ((win, keep_ref), (1 - win, got_ref)):
        power = ref[...]
        total = jnp.sum(power, axis=0, keepdims=True)
        at = pl.ds(pl.multiple_of(place * nodes, LANES), nodes)
        spectrum_ref[:, at] = power * (NF / total)
        beam_ref[:, at] = total * (1.0 / (NF * stations))


def on_device(traces, tables, corrections, station_table, node_ids, freq_bins):
    windows, groups, cores = (lax.axis_size(a) for a in ("win", "sta", "freq"))
    stations_dev, grid = corrections.shape
    stations = stations_dev * groups
    devices = windows * groups * cores
    nodes = grid // devices
    ntab = tables.shape[0]
    params = pltpu.CompilerParams(vmem_limit_bytes=VMEM_LIMIT)
    vmem = pl.BlockSpec(memory_space=pltpu.VMEM)
    smem = pl.BlockSpec(memory_space=pltpu.SMEM)
    anywhere = pl.BlockSpec(memory_space=pl.ANY)
    bins = freq_bins.reshape(1, NF)

    holders = windows * cores
    merged = nodes % (holders * LANES) == 0
    width = LANES + (nodes // holders if merged else 0)
    blocks = pl.pallas_call(
        functools.partial(send_kernel, nodes),
        out_shape=jax.ShapeDtypeStruct((devices, stations_dev, width), jnp.bfloat16),
        in_specs=[vmem, vmem, anywhere],
        out_specs=vmem,
        scratch_shapes=[pltpu.SemaphoreType.DMA((devices,))],
        compiler_params=params,
        name="send",
    )(bins, traces, corrections)
    received = [lax.all_to_all(blocks, ("win", "sta", "freq"), split_axis=0, concat_axis=0, tiled=True)]
    if not merged:
        parts = corrections.reshape(stations_dev, groups, holders, nodes)
        place = lax.axis_index("freq") * windows + lax.axis_index("win")
        mine = lax.dynamic_index_in_dim(parts, place, axis=2, keepdims=False)
        corr = lax.all_to_all(mine.transpose(1, 0, 2), "sta", split_axis=0, concat_axis=0, tiled=True)
        received.append(corr.reshape(stations, nodes))

    wide = 512
    phasors = jax.ShapeDtypeStruct((ntab, NF, nodes), jnp.float32)
    cosine, sine, coefs, sorter, plan = pl.pallas_call(
        prepare_kernel,
        out_shape=[
            phasors,
            phasors,
            jax.ShapeDtypeStruct((DEGREES, LANES), jnp.float32),
            jax.ShapeDtypeStruct((stations, stations), jnp.bfloat16),
            jax.ShapeDtypeStruct((8, LANES), jnp.int32),
        ],
        in_specs=[vmem] * 4,
        out_specs=[vmem] * 5,
        scratch_shapes=[
            pltpu.VMEM((grid // wide * ntab, 3 * wide), jnp.bfloat16),
            pltpu.VMEM((3 * wide, nodes), jnp.bfloat16),
        ],
        compiler_params=params,
        name="prepare",
    )(bins, station_table.reshape(1, stations), node_ids.reshape(grid // LANES, LANES), tables)

    half = jax.ShapeDtypeStruct((NF, nodes), jnp.float32)
    rows = 2 * windows * 2 * NF
    basis = pltpu.VMEM((2 * DEGREES * 8, nodes), jnp.bfloat16)
    left = pltpu.VMEM((rows, 2 * DEGREES * 8), jnp.bfloat16)
    keep, send = pl.pallas_call(
        functools.partial(image_kernel, merged, stations_dev),
        out_shape=[half, half],
        in_specs=[smem] + [vmem] * (4 + len(received)),
        out_specs=[vmem, vmem],
        scratch_shapes=[
            pltpu.VMEM((stations, nodes), jnp.float32),
            pltpu.VMEM((stations, 2 * rows), jnp.float32),
            pltpu.VMEM((rows // 2, nodes), jnp.float32),
            basis,
            left,
            basis,
            left,
        ],
        compiler_params=params,
        name="image",
    )(plan, sorter, coefs, cosine, sine, *received)
    got = lax.ppermute(send, "win", [(0, 1), (1, 0)])
    spectrum, beam_power = pl.pallas_call(
        functools.partial(finish_kernel, stations),
        out_shape=[
            jax.ShapeDtypeStruct((NF, windows * nodes), jnp.float32),
            jax.ShapeDtypeStruct((1, windows * nodes), jnp.float32),
        ],
        in_specs=[vmem, vmem],
        out_specs=[vmem, vmem],
        compiler_params=params,
        name="finish",
    )(keep, got)
    return spectrum, beam_power.reshape(windows * nodes)


def solution(mesh):
    return jax.shard_map(
        on_device,
        mesh=mesh,
        in_specs=(P(("win", "sta"), "freq"), P(), P("sta", None), P(), P(), P()),
        out_specs=(P("win", ("sta", "freq")), P(("win", "sta", "freq"))),
        check_vma=False,
    )
```

time: 64.5 us -> 44.7 us (0.69)
  Pallas kernels: 34.1 us -> 17.8 us
  starting transfers between devices: 21.2 us -> 8.37 us
  waiting for transfers between devices: 2.81 us -> 7.83 us
  local copies, waits for them, and re-layouts: 5.27 us -> 9.97 us
    pallas_call x4 -> x3, Pallas kernels: 33.4 us -> 17.1 us  [the longest x1 11.1 us: on_device(): pl.pallas_call(functools.partial(image_kernel, merged, stations_dev), out...]
    ppermute x7 -> x0, starting transfers between devices: 12.4 us -> none  [on_device(): corr.append(lax.ppermute(blocks[step], 'sta', pairs))]
    unnamed x14 -> x26, local copies, waits for them, and re-layouts: 5.27 us -> 9.97 us
    all_to_all x1, waiting for transfers between devices: 0.01 us -> 4.57 us  [on_device(): lax.all_to_all(blocks, ('win', 'sta', 'freq'), split_axis=0, concat_axis=...]
  transfers between devices with their start and end apart: 9 -> 2, of which waited for: 1 -> 2; matrix products, arithmetic and copies ran while one was open for 0% -> 0% of each run, Pallas kernels for 6% -> 9%
where the time goes in v3:
time: 44.7 us
  Pallas kernels  17.8 us (40%)
  local copies, waits for them, and re-layouts  9.97 us (22%)
  starting transfers between devices  8.37 us (19%)
  waiting for transfers between devices  7.83 us (18%)
  between operations  0.71 us (2%)
    pallas_call x1, Pallas kernels, on_device(): pl.pallas_call(functools.partial(image_kernel, merged, stations_dev), out...  11.1 us
    unnamed x26, local copies, waits for them, and re-layouts  9.97 us
    all_to_all x1, starting transfers between devices, on_device(): lax.all_to_all(blocks, ('win', 'sta', 'freq'), split_axis=0, concat_axis=...  7.3 us
    all_to_all x1, waiting for transfers between devices, on_device(): lax.all_to_all(blocks, ('win', 'sta', 'freq'), split_axis=0, concat_axis=...  4.57 us
    pallas_call x1, Pallas kernels, on_device(): pl.pallas_call(prepare_kernel, out_shape=[phasors, phasors, jax.ShapeDtyp...  4.1 us
    ppermute x1, waiting for transfers between devices, on_device(): got = lax.ppermute(send, 'win', [(0, 1), (1, 0)])  3.26 us
    pallas_call x1, Pallas kernels, on_device(): pl.pallas_call(functools.partial(send_kernel, nodes), out_shape=jax.Shape...  1.87 us
    ppermute x1, starting transfers between devices, on_device(): got = lax.ppermute(send, 'win', [(0, 1), (1, 0)])  1.07 us
  transfers between devices with their start and end apart: 2, of which 2 were waited for; matrix products, arithmetic and copies ran while one was open for 0% of the time, Pallas kernels for 9%

profile of v3, /device:TPU:0, one launch (start us, length us, event | category | flops | bytes accessed | tf_op | source)
XLA Modules:
  0.0 44.7 jit_solution(16112045263717193805)
XLA Ops:
  0.6 0.0 copy-start
  0.6 0.0 copy-start.3
  0.6 1.4 %copy-done.3 = bf16[16,32768]{1,0:T(8,128)(2,1)S(1)} copy-done((bf16[16,32768]{1,0:T(8,128)(2,1)S(1)}, bf16[16,32768]{1,0:T(8,128)(2,1)}, u32[]{:S(2)}) %copy-start.3) | copy-done | bytes 1048600
  2.0 0.9 %copy-done.5 = bf16[16,2560]{1,0:T(8,128)(2,1)S(1)} copy-done((bf16[16,2560]{1,0:T(8,128)(2,1)S(1)}, bf16[16,2560]{1,0:T(8,128)(2,1)}, u32[]{:S(2)}) %copy-start.5) | copy-done | bytes 81944
  2.9 0.7 %copy-done.10 = s32[16]{0:T(128)S(1)} copy-done((s32[16]{0:T(128)S(1)}, s32[16]{0:T(128)}, u32[]{:S(2)}) %copy-start.10) | copy-done | bytes 88
  3.6 1.9 %send.1 = bf16[32,16,384]{2,1,0:T(8,128)(2,1)} custom-call(s32[1,16]{1,0:T(1,128)S(1)} %bitcast.5, bf16[16,2560]{1,0:T(8,128)(2,1)S(1)} %copy-done.5, bf16[16,32768]{1,0:T(8,128)(2,1)S(1)} %copy-done.3), custom_call_target="tpu_custom_call" | custom-call | tf_op jit(solution)/shard_map/send/pallas_call | solution.py:357
  5.4 7.3 %all-to-all-start = ((bf16[32,16,384]{2,1,0:T(8,128)(2,1)}), bf16[32,16,384]{2,1,0:T(8,128)(2,1)S(1)}, u32[]{:S(2)}, u32[]{:S(2)}) async-start(bf16[32,16,384]{2,1,0:T(8,128)(2,1)} %send.1), calls=%async_computation | async-start | bytes 786432 | tf_op jit(solution)/shard_map/all_to_all | solution.py:366
  12.7 0.0 copy-done
  12.8 0.0 copy-start.4
  12.8 0.9 %copy-done.4 = s32[32768]{0:T(1024)S(1)} copy-done((s32[32768]{0:T(1024)S(1)}, s32[32768]{0:T(1024)}, u32[]{:S(2)}) %copy-start.4) | copy-done | bytes 131096
  13.7 0.7 %copy-done.11 = s32[16]{0:T(128)S(1)} copy-done((s32[16]{0:T(128)S(1)}, s32[16]{0:T(128)}, u32[]{:S(2)}) %copy-start.11) | copy-done | bytes 88
  14.3 0.7 %copy-done.12 = s32[128]{0:T(128)S(1)} copy-done((s32[128]{0:T(128)S(1)}, s32[128]{0:T(128)}, u32[]{:S(2)}) %copy-start.12) | copy-done | bytes 536
  15.0 4.1 %prepare.1 = (f32[16,16,1024]{2,1,0:T(8,128)S(1)}, f32[16,16,1024]{2,1,0:T(8,128)S(1)}, f32[32,128]{1,0:T(8,128)S(1)}, bf16[128,128]{1,0:T(8,128)(2,1)S(1)}, s32[8,128]{1,0:T(8,128)S(1)}) custom-call(s32[1,16]{1,0:T(1,128)S(1)} %bitcast.6, s32[1,128]{1,0:T(1,128)S(1)} %bitcast.7, s32[256,128]{1,0:T(8,128)S(1)} %bitcast.4, f32[16,32768]{1,0:T(8,128)S(1)} %copy-done), custom_call_target="tpu_custom_call" | custom-call | tf_op jit(solution)/shard_map/prepare/pallas_call | solution.py:376
  19.1 1.0 %copy-done.1 = f32[16,16,1024]{2,1,0:T(8,128)} copy-done((f32[16,16,1024]{2,1,0:T(8,128)}, f32[16,16,1024]{2,1,0:T(8,128)S(1)}, u32[]{:S(2)}) %copy-start.1) | copy-done | bytes 1048600
  20.1 0.6 %copy-done.6 = bf16[128,128]{1,0:T(8,128)(2,1)} copy-done((bf16[128,128]{1,0:T(8,128)(2,1)}, bf16[128,128]{1,0:T(8,128)(2,1)S(1)}, u32[]{:S(2)}) %copy-start.6) | copy-done | bytes 32792
  20.7 0.6 %copy-done.8 = s32[8,128]{1,0:T(8,128)} copy-done((s32[8,128]{1,0:T(8,128)}, s32[8,128]{1,0:T(8,128)S(1)}, u32[]{:S(2)}) %copy-start.8) | copy-done | bytes 4120
  21.3 4.6 %all-to-all-done.rest_0_ = bf16[32,16,384]{2,1,0:T(8,128)(2,1)S(1)} async-done(((bf16[32,16,384]{2,1,0:T(8,128)(2,1)}), bf16[32,16,384]{2,1,0:T(8,128)(2,1)S(1)}, u32[]{:S(2)}, u32[]{:S(2)}) %all-to-all-start) | async-done | bytes 393248 | tf_op jit(solution)/shard_map/all_to_all | solution.py:366
  25.9 1.2 %copy-done.2 = f32[16,16,1024]{2,1,0:T(8,128)S(1)} copy-done((f32[16,16,1024]{2,1,0:T(8,128)S(1)}, f32[16,16,1024]{2,1,0:T(8,128)}, u32[]{:S(2)}) %copy-start.2) | copy-done | bytes 1048600
  27.1 0.8 %copy-done.7 = bf16[128,128]{1,0:T(8,128)(2,1)S(1)} copy-done((bf16[128,128]{1,0:T(8,128)(2,1)S(1)}, bf16[128,128]{1,0:T(8,128)(2,1)}, u32[]{:S(2)}) %copy-start.7) | copy-done | bytes 32792
  27.8 0.7 %copy-done.9 = s32[8,128]{1,0:T(8,128)S(1)} copy-done((s32[8,128]{1,0:T(8,128)S(1)}, s32[8,128]{1,0:T(8,128)}, u32[]{:S(2)}) %copy-start.9) | copy-done | bytes 4120
  28.5 11.1 %image.1 = (f32[16,1024]{1,0:T(8,128)S(1)}, f32[16,1024]{1,0:T(8,128)S(1)}) custom-call(s32[8,128]{1,0:T(8,128)S(1)} %copy-done.9, bf16[128,128]{1,0:T(8,128)(2,1)S(1)} %copy-done.7, f32[32,128]{1,0:T(8,128)S(1)} %get-tuple-element.13.coef_ref, f32[16,16,1024]{2,1,0:T(8,128)S(1)} %get-tuple-element.14.cos_ref, f32[16,16,1024]{2,1,0:T(8,128)S(1)} %copy-done.2, ...), custom_call_target="tpu_custom_call" | custom-call | tf_op jit(solution)/shard_map/image/pallas_call | solution.py:399
  39.7 1.1 %collective-permute-start = (f32[16,1024]{1,0:T(8,128)S(1)}, f32[16,1024]{1,0:T(8,128)S(1)}, u32[]{:S(2)}, u32[]{:S(2)}) collective-permute-start(f32[16,1024]{1,0:T(8,128)S(1)} %get-tuple-element.17), channel_id=1, source_target_pairs={{0,16},{16,0},{1,17},{17,1},{2,18},{18,2},{3,19},{19,3},{4,20},{20... | collective-permute-start | bytes 196616 | tf_op jit(solution)/shard_map/ppermute | solution.py:416
  40.7 3.3 %collective-permute-done.got_ref = f32[16,1024]{1,0:T(8,128)S(1)} collective-permute-done((f32[16,1024]{1,0:T(8,128)S(1)}, f32[16,1024]{1,0:T(8,128)S(1)}, u32[]{:S(2)}, u32[]{:S(2)}) %collective-permute-start) | collective-permute-done | bytes 65568 | tf_op jit(solution)/shard_map/ppermute | solution.py:416
  44.0 0.7 %finish.1 = (f32[16,2048]{1,0:T(8,128)}, f32[1,2048]{1,0:T(1,128)}) custom-call(f32[16,1024]{1,0:T(8,128)S(1)} %get-tuple-element.16.keep_ref, f32[16,1024]{1,0:T(8,128)S(1)} %collective-permute-done.got_ref), custom_call_target="tpu_custom_call" | custom-call | tf_op jit(solution)/shard_map/finish/pallas_call | solution.py:417
  (10 shorter events, 0.0 us)
Async XLA Ops:
  0.6 12.1 %copy-start = (f32[16,32768]{1,0:T(8,128)S(1)}, f32[16,32768]{1,0:T(8,128)}, u32[]{:S(2)}) copy-start(f32[16,32768]{1,0:T(8,128)} %tables_ref.1) | copy-start | bytes 6291460
  0.6 1.4 %copy-start.3 = (bf16[16,32768]{1,0:T(8,128)(2,1)S(1)}, bf16[16,32768]{1,0:T(8,128)(2,1)}, u32[]{:S(2)}) copy-start(bf16[16,32768]{1,0:T(8,128)(2,1)} %corr_ref.1) | copy-start | bytes 3145732
  2.0 0.9 %copy-start.5 = (bf16[16,2560]{1,0:T(8,128)(2,1)S(1)}, bf16[16,2560]{1,0:T(8,128)(2,1)}, u32[]{:S(2)}) copy-start(bf16[16,2560]{1,0:T(8,128)(2,1)} %traces_ref.1) | copy-start | bytes 245764
  2.9 0.7 %copy-start.10 = (s32[16]{0:T(128)S(1)}, s32[16]{0:T(128)}, u32[]{:S(2)}) copy-start(s32[16]{0:T(128)} %param.11) | copy-start | bytes 196
  5.4 20.4 %all-to-all-start = ((bf16[32,16,384]{2,1,0:T(8,128)(2,1)}), bf16[32,16,384]{2,1,0:T(8,128)(2,1)S(1)}, u32[]{:S(2)}, u32[]{:S(2)}) async-start(bf16[32,16,384]{2,1,0:T(8,128)(2,1)} %send.1), calls=%async_computation | async-start | bytes 786432 | tf_op jit(solution)/shard_map/all_to_all | solution.py:366
  12.8 0.9 %copy-start.4 = (s32[32768]{0:T(1024)S(1)}, s32[32768]{0:T(1024)}, u32[]{:S(2)}) copy-start(s32[32768]{0:T(1024)} %param.10) | copy-start | bytes 393220
  13.7 0.7 %copy-start.11 = (s32[16]{0:T(128)S(1)}, s32[16]{0:T(128)}, u32[]{:S(2)}) copy-start(s32[16]{0:T(128)} %param.11) | copy-start | bytes 196
  14.3 0.7 %copy-start.12 = (s32[128]{0:T(128)S(1)}, s32[128]{0:T(128)}, u32[]{:S(2)}) copy-start(s32[128]{0:T(128)} %param.9) | copy-start | bytes 1540
  19.1 1.0 %copy-start.1 = (f32[16,16,1024]{2,1,0:T(8,128)}, f32[16,16,1024]{2,1,0:T(8,128)S(1)}, u32[]{:S(2)}) copy-start(f32[16,16,1024]{2,1,0:T(8,128)S(1)} %get-tuple-element.15.sin_ref) | copy-start | bytes 3145732
  20.1 0.6 %copy-start.6 = (bf16[128,128]{1,0:T(8,128)(2,1)}, bf16[128,128]{1,0:T(8,128)(2,1)S(1)}, u32[]{:S(2)}) copy-start(bf16[128,128]{1,0:T(8,128)(2,1)S(1)} %get-tuple-element.12.sorter_ref) | copy-start | bytes 98308
  20.7 0.6 %copy-start.8 = (s32[8,128]{1,0:T(8,128)}, s32[8,128]{1,0:T(8,128)S(1)}, u32[]{:S(2)}) copy-start(s32[8,128]{1,0:T(8,128)S(1)} %get-tuple-element.11.plan_ref) | copy-start | bytes 12292
  25.8 1.2 %copy-start.2 = (f32[16,16,1024]{2,1,0:T(8,128)S(1)}, f32[16,16,1024]{2,1,0:T(8,128)}, u32[]{:S(2)}) copy-start(f32[16,16,1024]{2,1,0:T(8,128)} %copy-done.1) | copy-start | bytes 3145732
  27.1 0.8 %copy-start.7 = (bf16[128,128]{1,0:T(8,128)(2,1)S(1)}, bf16[128,128]{1,0:T(8,128)(2,1)}, u32[]{:S(2)}) copy-start(bf16[128,128]{1,0:T(8,128)(2,1)} %copy-done.6) | copy-start | bytes 98308
  27.8 0.7 %copy-start.9 = (s32[8,128]{1,0:T(8,128)S(1)}, s32[8,128]{1,0:T(8,128)}, u32[]{:S(2)}) copy-start(s32[8,128]{1,0:T(8,128)} %copy-done.8) | copy-start | bytes 12292
  39.7 4.3 %collective-permute-start = (f32[16,1024]{1,0:T(8,128)S(1)}, f32[16,1024]{1,0:T(8,128)S(1)}, u32[]{:S(2)}, u32[]{:S(2)}) collective-permute-start(f32[16,1024]{1,0:T(8,128)S(1)} %get-tuple-element.17), channel_id=1, source_target_pairs={{0,16},{16,0},{1,17},{17,1},{2,18},{18,2},{3,19},{19,3},{4,20},{20... | collective-permute-start | bytes 196616 | tf_op jit(solution)/shard_map/ppermute | solution.py:416

commit v4 on v3

--- a/solution.py
+++ b/solution.py
@@ -14,8 +14,8 @@
 LANES = 128
 DEGREES = 32
 REACH = 1.5
-TERMS = 3
-VMEM_LIMIT = 48 * 1024 * 1024
+TABLE_PIECES = 8
+VMEM_LIMIT = 64 * 1024 * 1024 - 64 * 1024
 
 
 def chebyshev_fit(func, degree, low, high):
@@ -64,27 +64,32 @@
     return pieces
 
 
-def send_kernel(nodes, bins_ref, traces_ref, corr_ref, out_ref, *rest):
-    sems = rest[-1]
-    devices, rows, width = out_ref.shape
-    share = width - LANES
-    half_length = traces_ref.shape[1]
-    copies = []
-    if share:
-        windows, groups, cores = (lax.axis_size(a) for a in ("win", "sta", "freq"))
-        place = lax.axis_index("win") * cores + lax.axis_index("freq")
-        for dev in range(devices):
-            win, sta, core = dev // (groups * cores), dev // cores % groups, dev % cores
-            first = ((sta * cores + core) * windows + win) * nodes
-            first = pl.multiple_of(first + place * share, LANES)
-            copies.append(
-                pltpu.make_async_copy(
-                    corr_ref.at[:, pl.ds(first, share)], out_ref.at[dev, :, pl.ds(0, share)], sems.at[dev]
-                )
-            )
+def start_all(copies):
     for copy in copies:
         copy.start()
+    return copies
+
+
+def send_kernel(nodes, bins_hbm, traces_hbm, corr_hbm, corr_out, spectra_out, bins_ref, traces_ref, sems):
+    groups, _, _ = corr_out.shape
+    windows, cores = lax.axis_size("win"), lax.axis_size("freq")
+    place = lax.axis_index("freq") * windows + lax.axis_index("win")
+    half_length = traces_ref.shape[1]
+    small = start_all(
+        [
+            pltpu.make_async_copy(bins_hbm, bins_ref, sems.at[groups]),
+            pltpu.make_async_copy(traces_hbm, traces_ref, sems.at[groups + 1]),
+        ]
+    )
+    copies = []
+    for group in range(groups):
+        first = pl.multiple_of((group * cores * windows + place) * nodes, LANES)
+        copies.append(
+            pltpu.make_async_copy(corr_hbm.at[:, pl.ds(first, nodes)], corr_out.at[group], sems.at[group])
+        )
+    start_all(copies)
     start = lax.axis_index("freq") * half_length
+    small[0].wait()
     bins = bins_column(bins_ref)
     pos = (start + lax.broadcasted_iota(jnp.int32, (NF, half_length), 1)).astype(jnp.float32)
     product = bins * pos
@@ -94,26 +99,30 @@
     scale = 1.0 / math.sqrt(NT)
     table = jnp.concatenate([(1.0 - versine) * scale, sine * -scale], axis=0)
     both = jnp.concatenate(split_bf16(table, 2), axis=0)
+    small[1].wait()
     sums = lax.dot_general(
         traces_ref[...], both, (((1,), (1,)), ((), ())), preferred_element_type=jnp.float32
     )
     sums = sums[:, : 2 * NF] + sums[:, 2 * NF :]
-    pieces = split_bf16(sums, TERMS) + [jnp.zeros((rows, LANES - 2 * NF * TERMS), jnp.bfloat16)]
-    tile = jnp.concatenate([piece.astype(jnp.float32) for piece in pieces], axis=1).astype(jnp.bfloat16)
-    for dev in range(devices):
-        out_ref[dev, :, share:] = tile
+    rows = spectra_out.shape[1]
+    tile = jnp.concatenate([sums[at : at + rows] for at in range(0, sums.shape[0], rows)], axis=1)
+    for dev in range(spectra_out.shape[0]):
+        spectra_out[dev] = tile
     for copy in copies:
         copy.wait()
 
 
-def pick_columns(ids_ref, tables_ref, nodes, left_ref, right_ref):
+def own_place():
+    windows, cores = lax.axis_size("win"), lax.axis_size("freq")
+    return (lax.axis_index("sta") * cores + lax.axis_index("freq")) * windows + lax.axis_index("win")
+
+
+def pick_columns(ids_ref, tables_ref, table_copies, nodes, left_ref, right_ref):
     ntab, grid = tables_ref.shape
     count = nodes // LANES
     wide = right_ref.shape[0] // 3
     blocks = grid // wide
-    windows, cores = lax.axis_size("win"), lax.axis_size("freq")
-    place = (lax.axis_index("sta") * cores + lax.axis_index("freq")) * windows + lax.axis_index("win")
-    ids = ids_ref[pl.ds(place * count, count), :]
+    ids = ids_ref[pl.ds(own_place() * count % ids_ref.shape[0], count), :]
     ids = jnp.concatenate([ids[at : at + 1] for at in range(count)], axis=1)
     low, high = ids & (wide - 1), ids >> (wide.bit_length() - 1)
     spots = lax.broadcasted_iota(jnp.int32, (wide, nodes), 0)
@@ -121,6 +130,8 @@
     for term in range(3):
         right_ref[term * wide : (term + 1) * wide, :] = ones
     for block in range(blocks):
+        if block % (blocks // len(table_copies)) == 0:
+            table_copies[block // (blocks // len(table_copies))].wait()
         pieces = split_bf16(tables_ref[:, block * wide : (block + 1) * wide], 3)
         left_ref[block * ntab : (block + 1) * ntab, :] = jnp.concatenate(pieces, axis=1)
     found = jnp.zeros((ntab, nodes), jnp.float32)
@@ -173,54 +184,90 @@
 
 
 def prepare_kernel(
-    bins_ref, table_ref, ids_ref, tables_ref, cos_ref, sin_ref, coef_ref, sorter_ref, plan_ref, left_ref, right_ref
+    bins_hbm, table_hbm, ids_hbm, tables_hbm, cos_hbm, sin_hbm, coef_hbm, sorter_hbm, plan_hbm, *rest
 ):
-    nodes = cos_ref.shape[2]
+    bins_ref, table_ref, ids_ref, tables_ref, cos_ref, sin_ref, coef_ref, sorter_ref, plan_ref = rest[:9]
+    left_ref, right_ref, sems, table_sems = rest[9:]
+    ntab, _, nodes = cos_ref.shape
+    near = ids_ref.shape[0]
+    first = pl.multiple_of(own_place() * (nodes // LANES) // near * near, 8)
+    ins = start_all(
+        [
+            pltpu.make_async_copy(ids_hbm.at[pl.ds(first, near), :], ids_ref, sems.at[0]),
+            pltpu.make_async_copy(bins_hbm, bins_ref, sems.at[1]),
+            pltpu.make_async_copy(table_hbm, table_ref, sems.at[2]),
+        ]
+    )
+    piece = tables_ref.shape[1] // TABLE_PIECES
+    table_copies = []
+    for at in range(TABLE_PIECES):
+        part = (slice(None), pl.ds(at * piece, piece))
+        table_copies.append(pltpu.make_async_copy(tables_hbm.at[part], tables_ref.at[part], table_sems.at[at]))
+    start_all(table_copies)
+    for copy in ins:
+        copy.wait()
     coef_ref[...] = chebyshev_coefs(bins_ref)
     rank, plan = station_order(table_ref[...])
     plan_ref[...] = plan
     count = table_ref.shape[1]
     place = lax.broadcasted_iota(jnp.int32, (count, count), 0)
     sorter_ref[...] = jnp.where(place == rank, 1.0, 0.0).astype(jnp.bfloat16)
-    turns = pick_columns(ids_ref, tables_ref, nodes, left_ref, right_ref) * (1.0 / 256.0)
+    outs = start_all(
+        [
+            pltpu.make_async_copy(coef_ref, coef_hbm, sems.at[0]),
+            pltpu.make_async_copy(plan_ref, plan_hbm, sems.at[1]),
+            pltpu.make_async_copy(sorter_ref, sorter_hbm, sems.at[2]),
+        ]
+    )
+    turns = pick_columns(ids_ref, tables_ref, table_copies, nodes, left_ref, right_ref) * (1.0 / 256.0)
     bins = bins_column(bins_ref)
-    for table in range(tables_ref.shape[0]):
+    for table in range(ntab):
         cosine, sine = cos_sin(bins * turns[table : table + 1])
         cos_ref[table] = cosine
         sin_ref[table] = sine
-
-
-def image_kernel(merged, stations_dev, plan_ref, sorter_ref, coef_ref, cos_ref, sin_ref, *rest):
-    keep_ref, send_ref, place_ref, weight_ref, sums_ref, basis_a, left_a, basis_b, left_b = rest[-9:]
+        outs += start_all(
+            [
+                pltpu.make_async_copy(cos_ref.at[table], cos_hbm.at[table], sems.at[3 + 2 * table]),
+                pltpu.make_async_copy(sin_ref.at[table], sin_hbm.at[table], sems.at[4 + 2 * table]),
+            ]
+        )
+    for copy in outs:
+        copy.wait()
+
+
+def image_kernel(
+    stations_dev, plan_hbm, sorter_hbm, coef_hbm, spectra_hbm, corr_hbm, cos_hbm, sin_hbm, keep_ref, send_ref, *rest
+):
+    plan_ref, sorter_ref, coef_ref, spectra_ref, corr_ref, cos_ref, sin_ref, sems = rest[:8]
+    place_ref, weight_ref, sums_ref, basis_a, left_a, basis_b, left_b = rest[8:]
+    pairs = [
+        (sorter_hbm, sorter_ref), (corr_hbm, corr_ref), (spectra_hbm, spectra_ref), (plan_hbm, plan_ref),
+        (coef_hbm, coef_ref), (cos_hbm, cos_ref), (sin_hbm, sin_ref),
+    ]
+    copies = [pltpu.make_async_copy(src, dst, sems.at[at]) for at, (src, dst) in enumerate(pairs)]
+    start_all(copies)
     stations, nodes = place_ref.shape
     windows, groups, cores = (lax.axis_size(a) for a in ("win", "sta", "freq"))
     ntab = cos_ref.shape[0]
+    for copy in copies[:2]:
+        copy.wait()
     sorter = sorter_ref[...]
-    block_ref = rest[0]
-    width = block_ref.shape[2]
-    rows_of = lambda win, core: [(win * groups + group) * cores + core for group in range(groups)]
-
-    scale = 1.0 / REACH
-    if merged:
-        share = width - LANES
-        for win in range(windows):
-            for core in range(cores):
-                part = jnp.concatenate([block_ref[at, :, :share] for at in rows_of(win, core)], axis=0)
-                found = jnp.dot(sorter, part, preferred_element_type=jnp.float32)
-                first = (win * cores + core) * share
-                place_ref[:, first : first + share] = found * scale
-    else:
-        found = jnp.dot(sorter, rest[1][...], preferred_element_type=jnp.float32)
-        place_ref[...] = found * scale
-
+
+    place_ref[...] = jnp.dot(sorter, corr_ref[...], preferred_element_type=jnp.float32) * (1.0 / REACH)
+
+    for copy in copies[2:5]:
+        copy.wait()
     even, odd = [], []
+    rows = spectra_ref.shape[1]
     for win in range(windows):
-        total = None
-        for core in range(cores):
-            part = jnp.concatenate([block_ref[at, :, width - LANES :] for at in rows_of(win, core)], axis=0)
-            part = part.astype(jnp.float32)
-            total = part if total is None else total + part
-        value = sum(total[:, 2 * NF * term : 2 * NF * (term + 1)] for term in range(TERMS))
+        value = []
+        for group in range(groups):
+            at = (win * groups + group) * cores
+            tile = spectra_ref[at]
+            for core in range(1, cores):
+                tile = tile + spectra_ref[at + core]
+            value += [tile[:, 2 * NF * piece : 2 * NF * (piece + 1)] for piece in range(stations_dev // rows)]
+        value = jnp.concatenate(value, axis=0)
         even.append(value)
         odd.append(jnp.concatenate([-value[:, NF:], value[:, :NF]], axis=1))
     both = jnp.concatenate(even + even + odd + odd, axis=1)
@@ -231,11 +278,12 @@
     weight_ref[...] = found
     sums_ref[...] = jnp.zeros_like(sums_ref)
     chunk = min(256, nodes)
+    depth = DEGREES * 8
     lanes = 2 * windows * 2 * NF
     slot = lax.broadcasted_iota(jnp.int32, (8, lanes), 1) // (lanes // 2)
     spot = lax.broadcasted_iota(jnp.int32, (8, lanes), 0)
 
-    def make_left(group, table, left_ref):
+    def left_steps(group, table, left_ref):
         here = spot + group * 8
         low = jnp.where(slot == 0, plan_ref[0, table], plan_ref[0, table + 1])
         high = jnp.where(slot == 0, plan_ref[0, table + 1], plan_ref[0, table + 2])
@@ -245,17 +293,19 @@
             jnp.where(mask, weight_ref[rows, :lanes], 0.0),
             jnp.where(mask, weight_ref[rows, lanes:], 0.0),
         ]
-        for half in range(DEGREES * 8 // LANES):
-            per = LANES // 8
+        per = LANES // 8
+        for half in range(DEGREES // per):
             tall = jnp.concatenate(
                 [sides[k % 2] * coef_ref[k : k + 1, :lanes] for k in range(half * per, (half + 1) * per)], axis=0
             )
             high, low = split_bf16(tall.T, 2)
             at = half * LANES
             left_ref[:, at : at + LANES] = high
-            left_ref[:, DEGREES * 8 + at : DEGREES * 8 + at + LANES] = low
-
-    def make_basis(group, basis_ref):
+            left_ref[:, depth + at : depth + at + LANES] = high
+            left_ref[:, 2 * depth + at : 2 * depth + at + LANES] = low
+            yield
+
+    def basis_steps(group, basis_ref):
         arg = place_ref[pl.ds(pl.multiple_of(group * 8, 8), 8), :]
         twice = arg + arg
         before, now = jnp.ones_like(arg), arg
@@ -263,20 +313,25 @@
             pair = jnp.concatenate([before, now], axis=0)
             high, low = split_bf16(pair, 2)
             basis_ref[degree * 8 : degree * 8 + 16, :] = high
-            basis_ref[(DEGREES + degree) * 8 : (DEGREES + degree) * 8 + 16, :] = low
+            basis_ref[depth + degree * 8 : depth + degree * 8 + 16, :] = low
             before = twice * now - before
             now = twice * before - now
-
-    def add_tables(table, basis_ref, left_ref):
-        depth = DEGREES * 8
+            if degree % 8 == 6:
+                yield
+
+    def run(steps):
+        for _ in steps:
+            pass
+
+    def add_tables(table, basis_ref, left_ref, steps):
         other = jnp.minimum(table + 1, ntab - 1)
         half = lanes // 2
         for first in range(0, nodes, chunk):
             at = slice(first, first + chunk)
-            high = left_ref[:, :depth]
-            got = jnp.dot(high, basis_ref[:depth, at], preferred_element_type=jnp.float32)
-            got = got + jnp.dot(high, basis_ref[depth:, at], preferred_element_type=jnp.float32)
-            got = got + jnp.dot(left_ref[:, depth:], basis_ref[:depth, at], preferred_element_type=jnp.float32)
+            right = jnp.concatenate([basis_ref[:, at], basis_ref[:depth, at]], axis=0)
+            got = jnp.dot(left_ref[...], right, preferred_element_type=jnp.float32)
+            for step in steps:
+                next(step, None)
             cos_a, sin_a = cos_ref[table, :, at], sin_ref[table, :, at]
             cos_b, sin_b = cos_ref[other, :, at], sin_ref[other, :, at]
             for win in range(windows):
@@ -287,33 +342,36 @@
                 sums_ref[row + NF : row + 2 * NF, at] += (real_a * sin_a + imag_a * cos_a) + (
                     real_b * sin_b + imag_b * cos_b
                 )
+        for step in steps:
+            run(step)
 
     def more_tables(group, basis_ref, left_ref):
         first, last = plan_ref[1, group], plan_ref[2, group]
 
         def step(turn, carry):
             table = first + 2 * turn
-            make_left(group, table, left_ref)
-            add_tables(table, basis_ref, left_ref)
+            run(left_steps(group, table, left_ref))
+            add_tables(table, basis_ref, left_ref, [])
             return carry
 
         lax.fori_loop(1, (last - first) // 2 + 1, step, 0)
 
     total_groups = stations // 8
-    make_left(0, plan_ref[1, 0], left_a)
-    make_basis(0, basis_a)
+    run(left_steps(0, plan_ref[1, 0], left_a))
+    run(basis_steps(0, basis_a))
+    for copy in copies[5:]:
+        copy.wait()
+
+    def stage(group, after, basis_ref, left_ref, next_basis, next_left):
+        steps = [left_steps(after, plan_ref[1, after], next_left), basis_steps(after, next_basis)]
+        add_tables(plan_ref[1, group], basis_ref, left_ref, steps)
+        more_tables(group, basis_ref, left_ref)
 
     def body(pair, carry):
         group = pair * 2
-        make_left(group + 1, plan_ref[1, group + 1], left_b)
-        make_basis(group + 1, basis_b)
-        add_tables(plan_ref[1, group], basis_a, left_a)
-        more_tables(group, basis_a, left_a)
         after = jnp.minimum(group + 2, total_groups - 1)
-        make_left(after, plan_ref[1, after], left_a)
-        make_basis(after, basis_a)
-        add_tables(plan_ref[1, group + 1], basis_b, left_b)
-        more_tables(group + 1, basis_b, left_b)
+        stage(group, group + 1, basis_a, left_a, basis_b, left_b)
+        stage(group + 1, after, basis_b, left_b, basis_a, left_a)
         return carry
 
     lax.fori_loop(0, total_groups // 2, body, 0)
@@ -347,46 +405,54 @@
     ntab = tables.shape[0]
     params = pltpu.CompilerParams(vmem_limit_bytes=VMEM_LIMIT)
     vmem = pl.BlockSpec(memory_space=pltpu.VMEM)
-    smem = pl.BlockSpec(memory_space=pltpu.SMEM)
-    anywhere = pl.BlockSpec(memory_space=pl.ANY)
+    hbm = pl.BlockSpec(memory_space=pltpu.HBM)
     bins = freq_bins.reshape(1, NF)
-
-    holders = windows * cores
-    merged = nodes % (holders * LANES) == 0
-    width = LANES + (nodes // holders if merged else 0)
-    blocks = pl.pallas_call(
+    bins_scratch = pltpu.VMEM((1, NF), jnp.int32)
+
+    corr, copies = pl.pallas_call(
         functools.partial(send_kernel, nodes),
-        out_shape=jax.ShapeDtypeStruct((devices, stations_dev, width), jnp.bfloat16),
-        in_specs=[vmem, vmem, anywhere],
-        out_specs=vmem,
-        scratch_shapes=[pltpu.SemaphoreType.DMA((devices,))],
+        out_shape=[
+            jax.ShapeDtypeStruct((groups, stations_dev, nodes), jnp.bfloat16),
+            jax.ShapeDtypeStruct((devices, stations_dev * 2 * NF // LANES, LANES), jnp.float32),
+        ],
+        in_specs=[hbm] * 3,
+        out_specs=[hbm, vmem],
+        scratch_shapes=[
+            bins_scratch,
+            pltpu.VMEM(traces.shape, traces.dtype),
+            pltpu.SemaphoreType.DMA((groups + 2,)),
+        ],
         compiler_params=params,
         name="send",
     )(bins, traces, corrections)
-    received = [lax.all_to_all(blocks, ("win", "sta", "freq"), split_axis=0, concat_axis=0, tiled=True)]
-    if not merged:
-        parts = corrections.reshape(stations_dev, groups, holders, nodes)
-        place = lax.axis_index("freq") * windows + lax.axis_index("win")
-        mine = lax.dynamic_index_in_dim(parts, place, axis=2, keepdims=False)
-        corr = lax.all_to_all(mine.transpose(1, 0, 2), "sta", split_axis=0, concat_axis=0, tiled=True)
-        received.append(corr.reshape(stations, nodes))
+    corr = lax.all_to_all(corr, "sta", split_axis=0, concat_axis=0, tiled=True)
+    spectra = lax.all_to_all(copies, ("win", "sta", "freq"), split_axis=0, concat_axis=0, tiled=True)
 
     wide = 512
-    phasors = jax.ShapeDtypeStruct((ntab, NF, nodes), jnp.float32)
+    products = [
+        ((ntab, NF, nodes), jnp.float32),
+        ((ntab, NF, nodes), jnp.float32),
+        ((DEGREES, LANES), jnp.float32),
+        ((stations, stations), jnp.bfloat16),
+        ((8, LANES), jnp.int32),
+    ]
     cosine, sine, coefs, sorter, plan = pl.pallas_call(
         prepare_kernel,
-        out_shape=[
-            phasors,
-            phasors,
-            jax.ShapeDtypeStruct((DEGREES, LANES), jnp.float32),
-            jax.ShapeDtypeStruct((stations, stations), jnp.bfloat16),
-            jax.ShapeDtypeStruct((8, LANES), jnp.int32),
-        ],
-        in_specs=[vmem] * 4,
-        out_specs=[vmem] * 5,
+        out_shape=[jax.ShapeDtypeStruct(*product) for product in products],
+        in_specs=[hbm] * 4,
+        out_specs=[hbm] * 5,
         scratch_shapes=[
+            bins_scratch,
+            pltpu.VMEM((1, stations), jnp.int32),
+            pltpu.VMEM((max(nodes // LANES, 8), LANES), jnp.int32),
+            pltpu.VMEM(tables.shape, tables.dtype),
+        ]
+        + [pltpu.VMEM(*product) for product in products]
+        + [
             pltpu.VMEM((grid // wide * ntab, 3 * wide), jnp.bfloat16),
             pltpu.VMEM((3 * wide, nodes), jnp.bfloat16),
+            pltpu.SemaphoreType.DMA((3 + 2 * ntab,)),
+            pltpu.SemaphoreType.DMA((TABLE_PIECES,)),
         ],
         compiler_params=params,
         name="prepare",
@@ -395,13 +461,21 @@
     half = jax.ShapeDtypeStruct((NF, nodes), jnp.float32)
     rows = 2 * windows * 2 * NF
     basis = pltpu.VMEM((2 * DEGREES * 8, nodes), jnp.bfloat16)
-    left = pltpu.VMEM((rows, 2 * DEGREES * 8), jnp.bfloat16)
+    left = pltpu.VMEM((rows, 3 * DEGREES * 8), jnp.bfloat16)
     keep, send = pl.pallas_call(
-        functools.partial(image_kernel, merged, stations_dev),
+        functools.partial(image_kernel, stations_dev),
         out_shape=[half, half],
-        in_specs=[smem] + [vmem] * (4 + len(received)),
+        in_specs=[hbm] * 7,
         out_specs=[vmem, vmem],
         scratch_shapes=[
+            pltpu.SMEM(*products[4]),
+            pltpu.VMEM(*products[3]),
+            pltpu.VMEM(*products[2]),
+            pltpu.VMEM(spectra.shape, spectra.dtype),
+            pltpu.VMEM((stations, nodes), corr.dtype),
+            pltpu.VMEM(*products[0]),
+            pltpu.VMEM(*products[1]),
+            pltpu.SemaphoreType.DMA((7,)),
             pltpu.VMEM((stations, nodes), jnp.float32),
             pltpu.VMEM((stations, 2 * rows), jnp.float32),
             pltpu.VMEM((rows // 2, nodes), jnp.float32),
@@ -412,7 +486,7 @@
         ],
         compiler_params=params,
         name="image",
-    )(plan, sorter, coefs, cosine, sine, *received)
+    )(plan, sorter, coefs, spectra, corr.reshape(stations, nodes), cosine, sine)
     got = lax.ppermute(send, "win", [(0, 1), (1, 0)])
     spectrum, beam_power = pl.pallas_call(
         functools.partial(finish_kernel, stations),

time: 44.7 us -> 57.6 us (1.29)
  blocking collectives: 0 us -> 14.8 us
  Pallas kernels: 17.8 us -> 31.2 us
  local copies, waits for them, and re-layouts: 9.97 us -> 0 us
  starting transfers between devices: 8.37 us -> 4.73 us
  waiting for transfers between devices: 7.83 us -> 5.77 us
    all_to_all x0 -> x1, blocking collectives: none -> 14.8 us  [on_device(): lax.all_to_all(copies, ('win', 'sta', 'freq'), split_axis=0, concat_axis=...]
    pallas_call x3, Pallas kernels: 17.1 us -> 29.7 us  [the longest x1 12.2 us: on_device(): pl.pallas_call(functools.partial(image_kernel, stations_dev), out_shape=[...]
    unnamed x26 -> x0, local copies, waits for them, and re-layouts: 9.97 us -> none
    all_to_all x1, starting transfers between devices: 7.3 us -> 4.05 us  [on_device(): corr = lax.all_to_all(corr, 'sta', split_axis=0, concat_axis=0, tiled=True)]
    all_to_all x1, waiting for transfers between devices: 4.57 us -> 1.79 us  [on_device(): corr = lax.all_to_all(corr, 'sta', split_axis=0, concat_axis=0, tiled=True)]
    pallas_call x1, Pallas kernels: 0.69 us -> 1.57 us  [on_device(): pl.pallas_call(functools.partial(finish_kernel, stations), out_shape=[jax...]
    ppermute x1, waiting for transfers between devices: 3.26 us -> 3.97 us  [on_device(): got = lax.ppermute(send, 'win', [(0, 1), (1, 0)])]
  transfers between devices with their start and end apart: 2 -> 2, of which waited for: 2 -> 2; matrix products, arithmetic and copies ran while one was open for 0% -> 0% of each run, Pallas kernels for 9% -> 13%
where the time goes in v4:
time: 57.6 us; the launch traced here: 57.2 us
  Pallas kernels  31.2 us (54%)
  blocking collectives  14.8 us (26%)
  waiting for transfers between devices  5.77 us (10%)
  starting transfers between devices  4.73 us (8%)
  between operations  0.66 us (1%)
    all_to_all x1, blocking collectives, on_device(): lax.all_to_all(copies, ('win', 'sta', 'freq'), split_axis=0, concat_axis=...  14.8 us
    pallas_call x1, Pallas kernels, on_device(): pl.pallas_call(functools.partial(image_kernel, stations_dev), out_shape=[...  12.2 us
    pallas_call x1, Pallas kernels, on_device(): pl.pallas_call(functools.partial(send_kernel, nodes), out_shape=[jax.Shap...  9.77 us
    pallas_call x1, Pallas kernels, on_device(): pl.pallas_call(prepare_kernel, out_shape=[jax.ShapeDtypeStruct(*product)...  7.69 us
    all_to_all x1, starting transfers between devices, on_device(): corr = lax.all_to_all(corr, 'sta', split_axis=0, concat_axis=0, tiled=True)  4.05 us
    ppermute x1, waiting for transfers between devices, on_device(): got = lax.ppermute(send, 'win', [(0, 1), (1, 0)])  3.97 us
    all_to_all x1, waiting for transfers between devices, on_device(): corr = lax.all_to_all(corr, 'sta', split_axis=0, concat_axis=0, tiled=True)  1.79 us
    pallas_call x1, Pallas kernels, on_device(): pl.pallas_call(functools.partial(finish_kernel, stations), out_shape=[jax...  1.57 us
  transfers between devices with their start and end apart: 2, of which 2 were waited for; matrix products, arithmetic and copies ran while one was open for 0% of the time, Pallas kernels for 13%

profile of v4, /device:TPU:0, one launch (start us, length us, event | category | flops | bytes accessed | tf_op | source)
XLA Modules:
  0.0 57.2 jit_solution(5121773051954104730)
XLA Ops:
  0.6 9.8 %send.1 = (bf16[8,16,1024]{2,1,0:T(8,128)(2,1)}, f32[32,4,128]{2,1,0:T(4,128)}) custom-call(s32[1,16]{1,0:T(1,128)} %bitcast.6, bf16[16,2560]{1,0:T(8,128)(2,1)} %traces_hbm.1, bf16[16,32768]{1,0:T(8,128)(2,1)} %corr_hbm.1), custom_call_target="tpu_custom_call" | custom-call | tf_op jit(solution)/shard_map/send/pallas_call | solution.py:412
  10.4 14.8 %all_to_all.10.spectra_hbm = f32[32,4,128]{2,1,0:T(4,128)} all-to-all(f32[32,4,128]{2,1,0:T(4,128)} %get-tuple-element.16), channel_id=1, replica_groups=mesh['win'=2,'sta'=8,'freq'=2] {'win','sta','freq'}, dimensions={0} | all-to-all | bytes 131072 | tf_op jit(solution)/shard_map/all_to_all | solution.py:429
  25.2 4.1 %all-to-all-start.1 = ((bf16[8,16,1024]{2,1,0:T(8,128)(2,1)}), bf16[8,16,1024]{2,1,0:T(8,128)(2,1)}, u32[]{:S(2)}, u32[]{:S(2)}) async-start(bf16[8,16,1024]{2,1,0:T(8,128)(2,1)} %get-tuple-element.17), calls=%async_computation.1 | async-start | bytes 524288 | tf_op jit(solution)/shard_map/all_to_all | solution.py:428
  29.3 7.7 %prepare.1 = (f32[16,16,1024]{2,1,0:T(8,128)}, f32[16,16,1024]{2,1,0:T(8,128)}, f32[32,128]{1,0:T(8,128)}, bf16[128,128]{1,0:T(8,128)(2,1)}, s32[8,128]{1,0:T(8,128)}) custom-call(s32[1,16]{1,0:T(1,128)} %bitcast.7, s32[1,128]{1,0:T(1,128)} %bitcast.8, s32[256,128]{1,0:T(8,128)} %bitcast.5, f32[16,32768]{1,0:T(8,128)} %tables_hbm.1), custom_call_target="tpu_custom_call" | custom-call | tf_op jit(solution)/shard_map/prepare/pallas_call | solution.py:439
  37.0 1.8 %all-to-all-done.1 = bf16[8,16,1024]{2,1,0:T(8,128)(2,1)} async-done(((bf16[8,16,1024]{2,1,0:T(8,128)(2,1)}), bf16[8,16,1024]{2,1,0:T(8,128)(2,1)}, u32[]{:S(2)}, u32[]{:S(2)}) %all-to-all-start.1) | async-done | bytes 262176 | tf_op jit(solution)/shard_map/all_to_all | solution.py:428
  38.8 12.2 %image.1 = (f32[16,1024]{1,0:T(8,128)}, f32[16,1024]{1,0:T(8,128)}) custom-call(s32[8,128]{1,0:T(8,128)} %get-tuple-element.13.plan_hbm, bf16[128,128]{1,0:T(8,128)(2,1)} %get-tuple-element.14.sorter_hbm, f32[32,128]{1,0:T(8,128)} %get-tuple-element.15.coef_hbm, f32[32,4,128]{2,1,0:T(4,128)} %all_to_all.10.spectra_hbm, bf16[128,1024]{1,0:T(8,128)(2,1)} %bitcast.3.corr_hbm, ...), custom_call_target="tpu_custom_call" | custom-call | tf_op jit(solution)/shard_map/image/pallas_call | solution.py:465
  51.0 0.7 %collective-permute-start = (f32[16,1024]{1,0:T(8,128)}, f32[16,1024]{1,0:T(8,128)}, u32[]{:S(2)}, u32[]{:S(2)}) collective-permute-start(f32[16,1024]{1,0:T(8,128)} %get-tuple-element.21), channel_id=1, source_target_pairs={{0,16},{16,0},{1,17},{17,1},{2,18},{18,2},{3,19},{19,3},{4,20},{20... | collective-permute-start | bytes 196616 | tf_op jit(solution)/shard_map/ppermute | solution.py:490
  51.7 4.0 %collective-permute-done.got_ref = f32[16,1024]{1,0:T(8,128)} collective-permute-done((f32[16,1024]{1,0:T(8,128)}, f32[16,1024]{1,0:T(8,128)}, u32[]{:S(2)}, u32[]{:S(2)}) %collective-permute-start) | collective-permute-done | bytes 65568 | tf_op jit(solution)/shard_map/ppermute | solution.py:490
  55.7 1.6 %finish.1 = (f32[16,2048]{1,0:T(8,128)}, f32[1,2048]{1,0:T(1,128)}) custom-call(f32[16,1024]{1,0:T(8,128)} %get-tuple-element.20.keep_ref, f32[16,1024]{1,0:T(8,128)} %collective-permute-done.got_ref), custom_call_target="tpu_custom_call" | custom-call | tf_op jit(solution)/shard_map/finish/pallas_call | solution.py:491
Async XLA Ops:
  25.2 13.6 %all-to-all-start.1 = ((bf16[8,16,1024]{2,1,0:T(8,128)(2,1)}), bf16[8,16,1024]{2,1,0:T(8,128)(2,1)}, u32[]{:S(2)}, u32[]{:S(2)}) async-start(bf16[8,16,1024]{2,1,0:T(8,128)(2,1)} %get-tuple-element.17), calls=%async_computation.1 | async-start | bytes 524288 | tf_op jit(solution)/shard_map/all_to_all | solution.py:428
  51.0 4.6 %collective-permute-start = (f32[16,1024]{1,0:T(8,128)}, f32[16,1024]{1,0:T(8,128)}, u32[]{:S(2)}, u32[]{:S(2)}) collective-permute-start(f32[16,1024]{1,0:T(8,128)} %get-tuple-element.21), channel_id=1, source_target_pairs={{0,16},{16,0},{1,17},{17,1},{2,18},{18,2},{3,19},{19,3},{4,20},{20... | collective-permute-start | bytes 196616 | tf_op jit(solution)/shard_map/ppermute | solution.py:490

commit v5 on v4

--- a/solution.py
+++ b/solution.py
@@ -14,7 +14,7 @@
 LANES = 128
 DEGREES = 32
 REACH = 1.5
-TABLE_PIECES = 8
+TABLE_PIECES = 4
 VMEM_LIMIT = 64 * 1024 * 1024 - 64 * 1024
 
 
@@ -70,23 +70,27 @@
     return copies
 
 
-def send_kernel(nodes, bins_hbm, traces_hbm, corr_hbm, corr_out, spectra_out, bins_ref, traces_ref, sems):
-    groups, _, _ = corr_out.shape
-    windows, cores = lax.axis_size("win"), lax.axis_size("freq")
-    place = lax.axis_index("freq") * windows + lax.axis_index("win")
-    half_length = traces_ref.shape[1]
+def send_kernel(nodes, bins_hbm, traces_hbm, corr_hbm, out_ref, bins_ref, traces_ref, sems):
+    devices, height, _ = out_ref.shape
+    stations_dev, half_length = traces_ref.shape
+    pieces = (height - 8) // stations_dev
+    windows, groups, cores = (lax.axis_size(a) for a in ("win", "sta", "freq"))
+    place = lax.axis_index("win") * cores + lax.axis_index("freq")
     small = start_all(
         [
-            pltpu.make_async_copy(bins_hbm, bins_ref, sems.at[groups]),
-            pltpu.make_async_copy(traces_hbm, traces_ref, sems.at[groups + 1]),
+            pltpu.make_async_copy(bins_hbm, bins_ref, sems.at[0]),
+            pltpu.make_async_copy(traces_hbm, traces_ref, sems.at[1]),
         ]
     )
     copies = []
-    for group in range(groups):
-        first = pl.multiple_of((group * cores * windows + place) * nodes, LANES)
-        copies.append(
-            pltpu.make_async_copy(corr_hbm.at[:, pl.ds(first, nodes)], corr_out.at[group], sems.at[group])
-        )
+    for dev in range(devices):
+        win, sta, core = dev // (groups * cores), dev // cores % groups, dev % cores
+        first = ((sta * cores + core) * windows + win) * nodes
+        for piece in range(pieces):
+            at = pl.multiple_of(first + (place * pieces + piece) * LANES, LANES)
+            to = out_ref.at[dev, pl.ds(piece * stations_dev, stations_dev), :]
+            sem = sems.at[2 + dev * pieces + piece]
+            copies.append(pltpu.make_async_copy(corr_hbm.at[:, pl.ds(at, LANES)], to, sem))
     start_all(copies)
     start = lax.axis_index("freq") * half_length
     small[0].wait()
@@ -104,10 +108,11 @@
         traces_ref[...], both, (((1,), (1,)), ((), ())), preferred_element_type=jnp.float32
     )
     sums = sums[:, : 2 * NF] + sums[:, 2 * NF :]
-    rows = spectra_out.shape[1]
-    tile = jnp.concatenate([sums[at : at + rows] for at in range(0, sums.shape[0], rows)], axis=1)
-    for dev in range(spectra_out.shape[0]):
-        spectra_out[dev] = tile
+    terms = [term.astype(jnp.float32) for term in split_bf16(sums, 2)]
+    tile = jnp.concatenate([term[at : at + 8] for term in terms for at in range(0, stations_dev, 8)], axis=1)
+    tile = tile.astype(jnp.bfloat16)
+    for dev in range(devices):
+        out_ref[dev, height - 8 :, :] = tile
     for copy in copies:
         copy.wait()
 
@@ -129,19 +134,18 @@
     ones = jnp.where(spots == low, 1.0, 0.0).astype(jnp.bfloat16)
     for term in range(3):
         right_ref[term * wide : (term + 1) * wide, :] = ones
-    for block in range(blocks):
-        if block % (blocks // len(table_copies)) == 0:
-            table_copies[block // (blocks // len(table_copies))].wait()
-        pieces = split_bf16(tables_ref[:, block * wide : (block + 1) * wide], 3)
-        left_ref[block * ntab : (block + 1) * ntab, :] = jnp.concatenate(pieces, axis=1)
     found = jnp.zeros((ntab, nodes), jnp.float32)
-    step = 16
-    for first in range(0, blocks, step):
-        rows = left_ref[first * ntab : (first + step) * ntab, :]
+    step = blocks // len(table_copies)
+    for at, copy in enumerate(table_copies):
+        copy.wait()
+        for block in range(at * step, (at + 1) * step):
+            pieces = split_bf16(tables_ref[:, block * wide : (block + 1) * wide], 3)
+            left_ref[block * ntab : (block + 1) * ntab, :] = jnp.concatenate(pieces, axis=1)
+        rows = left_ref[at * step * ntab : (at + 1) * step * ntab, :]
         picked = jnp.dot(rows, right_ref[...], preferred_element_type=jnp.float32)
         for block in range(step):
             part = picked[block * ntab : (block + 1) * ntab]
-            found = jnp.where(high == first + block, part, found)
+            found = jnp.where(high == at * step + block, part, found)
     return found
 
 
@@ -235,75 +239,89 @@
         copy.wait()
 
 
-def image_kernel(
-    stations_dev, plan_hbm, sorter_hbm, coef_hbm, spectra_hbm, corr_hbm, cos_hbm, sin_hbm, keep_ref, send_ref, *rest
-):
-    plan_ref, sorter_ref, coef_ref, spectra_ref, corr_ref, cos_ref, sin_ref, sems = rest[:8]
-    place_ref, weight_ref, sums_ref, basis_a, left_a, basis_b, left_b = rest[8:]
+def image_kernel(merged, stations_dev, plan_hbm, sorter_hbm, coef_hbm, cos_hbm, sin_hbm, block_hbm, *rest):
+    corr_hbm, rest = (None, rest) if merged else (rest[0], rest[1:])
+    keep_ref, send_ref, plan_ref, sorter_ref, coef_ref, block_ref, corr_ref, cos_ref, sin_ref, sems = rest[:10]
+    place_ref, weight_ref, left_ref, sums_ref, basis_a, basis_b = rest[10:]
     pairs = [
-        (sorter_hbm, sorter_ref), (corr_hbm, corr_ref), (spectra_hbm, spectra_ref), (plan_hbm, plan_ref),
-        (coef_hbm, coef_ref), (cos_hbm, cos_ref), (sin_hbm, sin_ref),
+        (sorter_hbm, sorter_ref), (block_hbm, block_ref), (plan_hbm, plan_ref), (coef_hbm, coef_ref),
+        (cos_hbm, cos_ref), (sin_hbm, sin_ref),
     ]
+    if not merged:
+        pairs.append((corr_hbm, corr_ref))
     copies = [pltpu.make_async_copy(src, dst, sems.at[at]) for at, (src, dst) in enumerate(pairs)]
     start_all(copies)
     stations, nodes = place_ref.shape
     windows, groups, cores = (lax.axis_size(a) for a in ("win", "sta", "freq"))
     ntab = cos_ref.shape[0]
-    for copy in copies[:2]:
+    for copy in copies[:4] + copies[6:]:
         copy.wait()
     sorter = sorter_ref[...]
-
-    place_ref[...] = jnp.dot(sorter, corr_ref[...], preferred_element_type=jnp.float32) * (1.0 / REACH)
-
-    for copy in copies[2:5]:
-        copy.wait()
+    height = block_ref.shape[1]
+    rows_of = lambda win, core: [(win * groups + group) * cores + core for group in range(groups)]
+
+    if merged:
+        parts = []
+        for win in range(windows):
+            for core in range(cores):
+                for first in range(0, height - 8, stations_dev):
+                    rows = [block_ref[at, first : first + stations_dev, :] for at in rows_of(win, core)]
+                    parts.append(jnp.concatenate(rows, axis=0))
+        corr = jnp.concatenate(parts, axis=1)
+    else:
+        corr = corr_ref[...]
+    place_ref[...] = jnp.dot(sorter, corr, preferred_element_type=jnp.float32) * (1.0 / REACH)
+
     even, odd = [], []
-    rows = spectra_ref.shape[1]
     for win in range(windows):
         value = []
         for group in range(groups):
-            at = (win * groups + group) * cores
-            tile = spectra_ref[at]
-            for core in range(1, cores):
-                tile = tile + spectra_ref[at + core]
-            value += [tile[:, 2 * NF * piece : 2 * NF * (piece + 1)] for piece in range(stations_dev // rows)]
+            tile = None
+            for core in range(cores):
+                part = block_ref[(win * groups + group) * cores + core, height - 8 :, :].astype(jnp.float32)
+                tile = part if tile is None else tile + part
+            tile = tile[:, : LANES // 2] + tile[:, LANES // 2 :]
+            value += [tile[:, 2 * NF * piece : 2 * NF * (piece + 1)] for piece in range(stations_dev // 8)]
         value = jnp.concatenate(value, axis=0)
         even.append(value)
         odd.append(jnp.concatenate([-value[:, NF:], value[:, :NF]], axis=1))
-    both = jnp.concatenate(even + even + odd + odd, axis=1)
     found = None
-    for piece in split_bf16(both, 3):
+    for piece in split_bf16(jnp.concatenate(even + odd, axis=1), 3):
         part = jnp.dot(sorter, piece, preferred_element_type=jnp.float32)
         found = part if found is None else found + part
     weight_ref[...] = found
     sums_ref[...] = jnp.zeros_like(sums_ref)
     chunk = min(256, nodes)
     depth = DEGREES * 8
-    lanes = 2 * windows * 2 * NF
-    slot = lax.broadcasted_iota(jnp.int32, (8, lanes), 1) // (lanes // 2)
-    spot = lax.broadcasted_iota(jnp.int32, (8, lanes), 0)
-
-    def left_steps(group, table, left_ref):
-        here = spot + group * 8
-        low = jnp.where(slot == 0, plan_ref[0, table], plan_ref[0, table + 1])
-        high = jnp.where(slot == 0, plan_ref[0, table + 1], plan_ref[0, table + 2])
-        mask = (here >= low) & (here < high)
-        rows = pl.ds(pl.multiple_of(group * 8, 8), 8)
+    lanes = windows * 2 * NF
+    total_groups = stations // 8
+
+    def make_left(pair, carry):
+        top = weight_ref[pl.ds(pl.multiple_of(pair * 16, 16), 8), :]
+        bottom = weight_ref[pl.ds(pl.multiple_of(pair * 16 + 8, 8), 8), :]
         sides = [
-            jnp.where(mask, weight_ref[rows, :lanes], 0.0),
-            jnp.where(mask, weight_ref[rows, lanes:], 0.0),
+            jnp.concatenate([top[:, :lanes], bottom[:, :lanes]], axis=1),
+            jnp.concatenate([top[:, lanes:], bottom[:, lanes:]], axis=1),
         ]
         per = LANES // 8
         for half in range(DEGREES // per):
             tall = jnp.concatenate(
-                [sides[k % 2] * coef_ref[k : k + 1, :lanes] for k in range(half * per, (half + 1) * per)], axis=0
+                [sides[k % 2] * coef_ref[k : k + 1, :] for k in range(half * per, (half + 1) * per)], axis=0
             )
-            high, low = split_bf16(tall.T, 2)
-            at = half * LANES
-            left_ref[:, at : at + LANES] = high
-            left_ref[:, depth + at : depth + at + LANES] = high
-            left_ref[:, 2 * depth + at : 2 * depth + at + LANES] = low
-            yield
+            at = slice(half * LANES, (half + 1) * LANES)
+            for term, value in enumerate(split_bf16(tall.T, 2)):
+                left_ref[2 * pair, term * lanes : (term + 1) * lanes, at] = value[:lanes]
+                left_ref[2 * pair + 1, term * lanes : (term + 1) * lanes, at] = value[lanes:]
+        return carry
+
+    lax.fori_loop(0, total_groups // 2, make_left, 0)
+    spot = lax.broadcasted_iota(jnp.int32, (16, depth), 1) % 8
+
+    def left_of(group, table):
+        here = spot + group * 8
+        mask = (here >= plan_ref[0, table]) & (here < plan_ref[0, table + 1])
+        mask = jnp.where(mask, 1.0, 0.0).astype(jnp.bfloat16)
+        return left_ref[group] * jnp.concatenate([mask] * (2 * lanes // 16), axis=0)
 
     def basis_steps(group, basis_ref):
         arg = place_ref[pl.ds(pl.multiple_of(group * 8, 8), 8), :]
@@ -323,55 +341,50 @@
         for _ in steps:
             pass
 
-    def add_tables(table, basis_ref, left_ref, steps):
+    def add_tables(group, table, basis_ref, steps):
         other = jnp.minimum(table + 1, ntab - 1)
-        half = lanes // 2
+        left_a, left_b = left_of(group, table), left_of(group, table + 1)
+        both = jnp.concatenate([left_a, left_b], axis=0)
+        high = jnp.concatenate([left_a[:lanes], left_b[:lanes]], axis=0)
         for first in range(0, nodes, chunk):
             at = slice(first, first + chunk)
-            right = jnp.concatenate([basis_ref[:, at], basis_ref[:depth, at]], axis=0)
-            got = jnp.dot(left_ref[...], right, preferred_element_type=jnp.float32)
-            for step in steps:
-                next(step, None)
-            cos_a, sin_a = cos_ref[table, :, at], sin_ref[table, :, at]
-            cos_b, sin_b = cos_ref[other, :, at], sin_ref[other, :, at]
-            for win in range(windows):
-                row = win * 2 * NF
-                real_a, imag_a = got[row : row + NF], got[row + NF : row + 2 * NF]
-                real_b, imag_b = got[half + row : half + row + NF], got[half + row + NF : half + row + 2 * NF]
-                sums_ref[row : row + NF, at] += (real_a * cos_a - imag_a * sin_a) + (real_b * cos_b - imag_b * sin_b)
-                sums_ref[row + NF : row + 2 * NF, at] += (real_a * sin_a + imag_a * cos_a) + (
-                    real_b * sin_b + imag_b * cos_b
-                )
-        for step in steps:
-            run(step)
-
-    def more_tables(group, basis_ref, left_ref):
+            got = jnp.dot(both, basis_ref[:depth, at], preferred_element_type=jnp.float32)
+            more = jnp.dot(high, basis_ref[depth:, at], preferred_element_type=jnp.float32)
+            next(steps, None)
+            for slot, place in enumerate((table, other)):
+                row = slot * 2 * lanes
+                value = got[row : row + lanes] + got[row + lanes : row + 2 * lanes]
+                value = value + more[slot * lanes : (slot + 1) * lanes]
+                cosine, sine = cos_ref[place, :, at], sin_ref[place, :, at]
+                for win in range(windows):
+                    row = win * 2 * NF
+                    real, imag = value[row : row + NF], value[row + NF : row + 2 * NF]
+                    sums_ref[row : row + NF, at] += real * cosine - imag * sine
+                    sums_ref[row + NF : row + 2 * NF, at] += real * sine + imag * cosine
+        run(steps)
+
+    def more_tables(group, basis_ref):
         first, last = plan_ref[1, group], plan_ref[2, group]
 
         def step(turn, carry):
-            table = first + 2 * turn
-            run(left_steps(group, table, left_ref))
-            add_tables(table, basis_ref, left_ref, [])
+            add_tables(group, first + 2 * turn, basis_ref, iter(()))
             return carry
 
         lax.fori_loop(1, (last - first) // 2 + 1, step, 0)
 
-    total_groups = stations // 8
-    run(left_steps(0, plan_ref[1, 0], left_a))
     run(basis_steps(0, basis_a))
-    for copy in copies[5:]:
+    for copy in copies[4:6]:
         copy.wait()
 
-    def stage(group, after, basis_ref, left_ref, next_basis, next_left):
-        steps = [left_steps(after, plan_ref[1, after], next_left), basis_steps(after, next_basis)]
-        add_tables(plan_ref[1, group], basis_ref, left_ref, steps)
-        more_tables(group, basis_ref, left_ref)
+    def stage(group, after, basis_ref, next_basis):
+        add_tables(group, plan_ref[1, group], basis_ref, basis_steps(after, next_basis))
+        more_tables(group, basis_ref)
 
     def body(pair, carry):
         group = pair * 2
         after = jnp.minimum(group + 2, total_groups - 1)
-        stage(group, group + 1, basis_a, left_a, basis_b, left_b)
-        stage(group + 1, after, basis_b, left_b, basis_a, left_a)
+        stage(group, group + 1, basis_a, basis_b)
+        stage(group + 1, after, basis_b, basis_a)
         return carry
 
     lax.fori_loop(0, total_groups // 2, body, 0)
@@ -409,24 +422,30 @@
     bins = freq_bins.reshape(1, NF)
     bins_scratch = pltpu.VMEM((1, NF), jnp.int32)
 
-    corr, copies = pl.pallas_call(
+    holders = windows * cores
+    merged = nodes % (holders * LANES) == 0
+    pieces = nodes // (holders * LANES) if merged else 0
+    height = pieces * stations_dev + 8
+    blocks = pl.pallas_call(
         functools.partial(send_kernel, nodes),
-        out_shape=[
-            jax.ShapeDtypeStruct((groups, stations_dev, nodes), jnp.bfloat16),
-            jax.ShapeDtypeStruct((devices, stations_dev * 2 * NF // LANES, LANES), jnp.float32),
-        ],
+        out_shape=jax.ShapeDtypeStruct((devices, height, LANES), jnp.bfloat16),
         in_specs=[hbm] * 3,
-        out_specs=[hbm, vmem],
+        out_specs=vmem,
         scratch_shapes=[
             bins_scratch,
             pltpu.VMEM(traces.shape, traces.dtype),
-            pltpu.SemaphoreType.DMA((groups + 2,)),
+            pltpu.SemaphoreType.DMA((2 + devices * max(pieces, 1),)),
         ],
         compiler_params=params,
         name="send",
     )(bins, traces, corrections)
-    corr = lax.all_to_all(corr, "sta", split_axis=0, concat_axis=0, tiled=True)
-    spectra = lax.all_to_all(copies, ("win", "sta", "freq"), split_axis=0, concat_axis=0, tiled=True)
+    received = [lax.all_to_all(blocks, ("win", "sta", "freq"), split_axis=0, concat_axis=0, tiled=True)]
+    if not merged:
+        parts = corrections.reshape(stations_dev, groups, holders, nodes)
+        place = lax.axis_index("freq") * windows + lax.axis_index("win")
+        mine = lax.dynamic_index_in_dim(parts, place, axis=2, keepdims=False)
+        corr = lax.all_to_all(mine.transpose(1, 0, 2), "sta", split_axis=0, concat_axis=0, tiled=True)
+        received.append(corr.reshape(stations, nodes))
 
     wide = 512
     products = [
@@ -461,32 +480,30 @@
     half = jax.ShapeDtypeStruct((NF, nodes), jnp.float32)
     rows = 2 * windows * 2 * NF
     basis = pltpu.VMEM((2 * DEGREES * 8, nodes), jnp.bfloat16)
-    left = pltpu.VMEM((rows, 3 * DEGREES * 8), jnp.bfloat16)
     keep, send = pl.pallas_call(
-        functools.partial(image_kernel, stations_dev),
+        functools.partial(image_kernel, merged, stations_dev),
         out_shape=[half, half],
-        in_specs=[hbm] * 7,
+        in_specs=[hbm] * (5 + len(received)),
         out_specs=[vmem, vmem],
         scratch_shapes=[
             pltpu.SMEM(*products[4]),
             pltpu.VMEM(*products[3]),
             pltpu.VMEM(*products[2]),
-            pltpu.VMEM(spectra.shape, spectra.dtype),
-            pltpu.VMEM((stations, nodes), corr.dtype),
+            pltpu.VMEM((devices, height, LANES), jnp.bfloat16),
+            pltpu.VMEM((16, LANES) if merged else (stations, nodes), jnp.bfloat16),
             pltpu.VMEM(*products[0]),
             pltpu.VMEM(*products[1]),
             pltpu.SemaphoreType.DMA((7,)),
             pltpu.VMEM((stations, nodes), jnp.float32),
-            pltpu.VMEM((stations, 2 * rows), jnp.float32),
+            pltpu.VMEM((stations, rows), jnp.float32),
+            pltpu.VMEM((stations // 8, rows, DEGREES * 8), jnp.bfloat16),
             pltpu.VMEM((rows // 2, nodes), jnp.float32),
             basis,
-            left,
             basis,
-            left,
         ],
         compiler_params=params,
         name="image",
-    )(plan, sorter, coefs, spectra, corr.reshape(stations, nodes), cosine, sine)
+    )(plan, sorter, coefs, cosine, sine, *received)
     got = lax.ppermute(send, "win", [(0, 1), (1, 0)])
     spectrum, beam_power = pl.pallas_call(
         functools.partial(finish_kernel, stations),

time: 57.6 us -> 41.8 us (0.73)
  blocking collectives: 14.8 us -> 0 us
  Pallas kernels: 31.2 us -> 24.5 us
  starting transfers between devices: 4.73 us -> 8.48 us
  waiting for transfers between devices: 5.77 us -> 7.46 us
    all_to_all x1 -> x0, blocking collectives: 14.8 us -> none  [on_device(): lax.all_to_all(copies, ('win', 'sta', 'freq'), split_axis=0, concat_axis=...]
    pallas_call x2, Pallas kernels: 22 us -> 15.1 us  [the longest x1 12.4 us: on_device(): pl.pallas_call(functools.partial(image_kernel, merged, stations_dev), out...]
    all_to_all x1, starting transfers between devices: 4.05 us -> 7.42 us  [on_device(): lax.all_to_all(blocks, ('win', 'sta', 'freq'), split_axis=0, concat_axis=...]
    all_to_all x1, waiting for transfers between devices: 1.79 us -> 3.88 us  [on_device(): lax.all_to_all(blocks, ('win', 'sta', 'freq'), split_axis=0, concat_axis=...]
  transfers between devices with their start and end apart: 2 -> 2, of which waited for: 2 -> 2; matrix products, arithmetic and copies ran while one was open for 0% -> 0% of each run, Pallas kernels for 13% -> 19%
where the time goes in v5:
time: 41.8 us; the launch traced here: 41.1 us
  Pallas kernels  24.5 us (59%)
  starting transfers between devices  8.48 us (20%)
  waiting for transfers between devices  7.46 us (18%)
  between operations  0.66 us (2%)
    pallas_call x1, Pallas kernels, on_device(): pl.pallas_call(functools.partial(image_kernel, merged, stations_dev), out...  12.4 us
    pallas_call x1, Pallas kernels, on_device(): pl.pallas_call(prepare_kernel, out_shape=[jax.ShapeDtypeStruct(*product)...  7.8 us
    all_to_all x1, starting transfers between devices, on_device(): lax.all_to_all(blocks, ('win', 'sta', 'freq'), split_axis=0, concat_axis=...  7.42 us
    all_to_all x1, waiting for transfers between devices, on_device(): lax.all_to_all(blocks, ('win', 'sta', 'freq'), split_axis=0, concat_axis=...  3.88 us
    ppermute x1, waiting for transfers between devices, on_device(): got = lax.ppermute(send, 'win', [(0, 1), (1, 0)])  3.58 us
    pallas_call x1, Pallas kernels, on_device(): pl.pallas_call(functools.partial(send_kernel, nodes), out_shape=jax.Shape...  2.73 us
    pallas_call x1, Pallas kernels, on_device(): pl.pallas_call(functools.partial(finish_kernel, stations), out_shape=[jax...  1.57 us
    ppermute x1, starting transfers between devices, on_device(): got = lax.ppermute(send, 'win', [(0, 1), (1, 0)])  1.07 us
  transfers between devices with their start and end apart: 2, of which 2 were waited for; matrix products, arithmetic and copies ran while one was open for 0% of the time, Pallas kernels for 19%

profile of v5, /device:TPU:0, one launch (start us, length us, event | category | flops | bytes accessed | tf_op | source)
XLA Modules:
  0.0 41.1 jit_solution(8135186826223884845)
XLA Ops:
  0.6 2.7 %send.1 = bf16[32,40,128]{2,1,0:T(8,128)(2,1)} custom-call(s32[1,16]{1,0:T(1,128)} %bitcast.5, bf16[16,2560]{1,0:T(8,128)(2,1)} %traces_hbm.1, bf16[16,32768]{1,0:T(8,128)(2,1)} %corr_hbm.1), custom_call_target="tpu_custom_call" | custom-call | tf_op jit(solution)/shard_map/send/pallas_call | solution.py:429
  3.4 7.4 %all-to-all-start = ((bf16[32,40,128]{2,1,0:T(8,128)(2,1)}), bf16[32,40,128]{2,1,0:T(8,128)(2,1)}, u32[]{:S(2)}, u32[]{:S(2)}) async-start(bf16[32,40,128]{2,1,0:T(8,128)(2,1)} %send.1), calls=%async_computation | async-start | bytes 655360 | tf_op jit(solution)/shard_map/all_to_all | solution.py:442
  10.8 7.8 %prepare.1 = (f32[16,16,1024]{2,1,0:T(8,128)}, f32[16,16,1024]{2,1,0:T(8,128)}, f32[32,128]{1,0:T(8,128)}, bf16[128,128]{1,0:T(8,128)(2,1)}, s32[8,128]{1,0:T(8,128)}) custom-call(s32[1,16]{1,0:T(1,128)} %bitcast.6, s32[1,128]{1,0:T(1,128)} %bitcast.7, s32[256,128]{1,0:T(8,128)} %bitcast.4, f32[16,32768]{1,0:T(8,128)} %tables_hbm.1), custom_call_target="tpu_custom_call" | custom-call | tf_op jit(solution)/shard_map/prepare/pallas_call | solution.py:458
  18.6 3.9 %all-to-all-done.block_hbm = bf16[32,40,128]{2,1,0:T(8,128)(2,1)} async-done(((bf16[32,40,128]{2,1,0:T(8,128)(2,1)}), bf16[32,40,128]{2,1,0:T(8,128)(2,1)}, u32[]{:S(2)}, u32[]{:S(2)}) %all-to-all-start) | async-done | bytes 327712 | tf_op jit(solution)/shard_map/all_to_all | solution.py:442
  22.5 12.4 %image.1 = (f32[16,1024]{1,0:T(8,128)}, f32[16,1024]{1,0:T(8,128)}) custom-call(s32[8,128]{1,0:T(8,128)} %get-tuple-element.11.plan_hbm, bf16[128,128]{1,0:T(8,128)(2,1)} %get-tuple-element.12.sorter_hbm, f32[32,128]{1,0:T(8,128)} %get-tuple-element.13.coef_hbm, f32[16,16,1024]{2,1,0:T(8,128)} %get-tuple-element.14.cos_hbm, ...), custom_call_target="tpu_custom_call" | custom-call | tf_op jit(solution)/shard_map/image/pallas_call | solution.py:483
  34.9 1.1 %collective-permute-start = (f32[16,1024]{1,0:T(8,128)}, f32[16,1024]{1,0:T(8,128)}, u32[]{:S(2)}, u32[]{:S(2)}) collective-permute-start(f32[16,1024]{1,0:T(8,128)} %get-tuple-element.17), channel_id=1, source_target_pairs={{0,16},{16,0},{1,17},{17,1},{2,18},{18,2},{3,19},{19,3},{4,20},{20... | collective-permute-start | bytes 196616 | tf_op jit(solution)/shard_map/ppermute | solution.py:507
  36.0 3.6 %collective-permute-done.got_ref = f32[16,1024]{1,0:T(8,128)} collective-permute-done((f32[16,1024]{1,0:T(8,128)}, f32[16,1024]{1,0:T(8,128)}, u32[]{:S(2)}, u32[]{:S(2)}) %collective-permute-start) | collective-permute-done | bytes 65568 | tf_op jit(solution)/shard_map/ppermute | solution.py:507
  39.6 1.6 %finish.1 = (f32[16,2048]{1,0:T(8,128)}, f32[1,2048]{1,0:T(1,128)}) custom-call(f32[16,1024]{1,0:T(8,128)} %get-tuple-element.16.keep_ref, f32[16,1024]{1,0:T(8,128)} %collective-permute-done.got_ref), custom_call_target="tpu_custom_call" | custom-call | tf_op jit(solution)/shard_map/finish/pallas_call | solution.py:508
Async XLA Ops:
  3.4 19.1 %all-to-all-start = ((bf16[32,40,128]{2,1,0:T(8,128)(2,1)}), bf16[32,40,128]{2,1,0:T(8,128)(2,1)}, u32[]{:S(2)}, u32[]{:S(2)}) async-start(bf16[32,40,128]{2,1,0:T(8,128)(2,1)} %send.1), calls=%async_computation | async-start | bytes 655360 | tf_op jit(solution)/shard_map/all_to_all | solution.py:442
  34.9 4.6 %collective-permute-start = (f32[16,1024]{1,0:T(8,128)}, f32[16,1024]{1,0:T(8,128)}, u32[]{:S(2)}, u32[]{:S(2)}) collective-permute-start(f32[16,1024]{1,0:T(8,128)} %get-tuple-element.17), channel_id=1, source_target_pairs={{0,16},{16,0},{1,17},{17,1},{2,18},{18,2},{3,19},{19,3},{4,20},{20... | collective-permute-start | bytes 196616 | tf_op jit(solution)/shard_map/ppermute | solution.py:507

commit v6 on v5

--- a/solution.py
+++ b/solution.py
@@ -11,6 +11,7 @@
 
 NT = 5120
 NF = 16
+NTAB = 16
 LANES = 128
 DEGREES = 32
 REACH = 1.5
@@ -167,32 +168,53 @@
     return dot(even, cosine) + dot(odd, sine)
 
 
-def station_order(table_row):
+def station_plan(table_row, width):
     count = table_row.shape[1]
     shape = (count, count)
     here = lax.broadcasted_iota(jnp.int32, shape, 0)
     there = lax.broadcasted_iota(jnp.int32, shape, 1)
-    key_row = table_row * count + there[:1]
-    spread = jnp.broadcast_to(key_row, shape)
-    key_column = jnp.sum(jnp.where(here == there, spread, 0), axis=1, keepdims=True)
-    rank = jnp.sum(jnp.where(key_column < key_row, 1, 0), axis=0, keepdims=True)
-    table_column = key_column // count
-    bound = lax.broadcasted_iota(jnp.int32, (count, LANES), 1)
-    starts = jnp.sum(jnp.where(table_column < bound, 1, 0), axis=0, keepdims=True)
-    first = lax.broadcasted_iota(jnp.int32, (count, LANES), 1) * 8
-    place_column = jnp.sum(jnp.where(here == there, jnp.broadcast_to(rank, shape), 0), axis=1, keepdims=True)
-    low = jnp.sum(jnp.where(place_column == first, table_column, 0), axis=0, keepdims=True)
-    high = jnp.sum(jnp.where(place_column == first + 7, table_column, 0), axis=0, keepdims=True)
-    plan = jnp.concatenate([starts, low, high, jnp.zeros((5, LANES), jnp.int32)], axis=0)
-    return rank, plan
-
-
-def prepare_kernel(
-    bins_hbm, table_hbm, ids_hbm, tables_hbm, cos_hbm, sin_hbm, coef_hbm, sorter_hbm, plan_hbm, *rest
-):
-    bins_ref, table_ref, ids_ref, tables_ref, cos_ref, sin_ref, coef_ref, sorter_ref, plan_ref = rest[:9]
-    left_ref, right_ref, sems, table_sems = rest[9:]
-    ntab, _, nodes = cos_ref.shape
+    column_of = lambda row: jnp.sum(jnp.where(here == there, jnp.broadcast_to(row, shape), 0), axis=1, keepdims=True)
+    table_column = column_of(table_row)
+    same = (table_column == table_row) & (here < there)
+    within = jnp.sum(jnp.where(same, 1, 0), axis=0, keepdims=True)
+    place_row = within
+    spot = jnp.zeros((1, 1), jnp.int32)
+    held = jnp.zeros((1, 1), jnp.int32)
+    for table in range(NTAB):
+        size = jnp.sum(jnp.where(table_row == table, 1, 0), axis=1, keepdims=True)
+        some = size > 0
+        edge = (spot & 7) == 0
+        skip = some & (held >= 2) & ~edge
+        spot = jnp.where(skip, (spot + 7) >> 3 << 3, spot)
+        held = jnp.where(skip | edge, 0, held)
+        after = spot + size
+        place_row = place_row + jnp.where(table_row == table, spot, 0)
+        held = jnp.where(some, jnp.where(after >> 3 == spot >> 3, held + 1, 1), held)
+        spot = after
+    groups = (spot + 7) >> 3
+    place_column = column_of(place_row)
+    group = lax.broadcasted_iota(jnp.int32, (count, width), 1)
+    inside = place_column >> 3 == group
+    first = jnp.sum(jnp.where(place_column == group * 8, table_column, 0), axis=0, keepdims=True)
+    last = jnp.max(jnp.where(inside, table_column, 0), axis=0, keepdims=True)
+    length = jnp.sum(jnp.where(inside & (table_column == first), 1, 0), axis=0, keepdims=True)
+    rows = [first, last, length, jnp.broadcast_to(groups, (1, width))]
+    if width > count:
+        place_row = jnp.concatenate([place_row, jnp.zeros((1, width - count), jnp.int32)], axis=1)
+    rows += [place_row, jnp.zeros((3, width), jnp.int32)]
+    return jnp.concatenate(rows, axis=0).astype(jnp.float32)
+
+
+def packed_rows(ntab):
+    ends = [ntab * NF, 2 * ntab * NF, 2 * ntab * NF + DEGREES, 2 * ntab * NF + DEGREES + 8]
+    return [slice(start, end) for start, end in zip([0] + ends, ends)]
+
+
+def prepare_kernel(bins_hbm, table_hbm, ids_hbm, tables_hbm, out_hbm, *rest):
+    bins_ref, table_ref, ids_ref, tables_ref, cos_ref, sin_ref, coef_ref, plan_ref = rest[:8]
+    left_ref, right_ref, sems, table_sems = rest[8:]
+    ntab = tables_ref.shape[0]
+    nodes = cos_ref.shape[1]
     near = ids_ref.shape[0]
     first = pl.multiple_of(own_place() * (nodes // LANES) // near * near, 8)
     ins = start_all(
@@ -210,67 +232,58 @@
     start_all(table_copies)
     for copy in ins:
         copy.wait()
+    cos_at, sin_at, coef_at, plan_at = packed_rows(ntab)
     coef_ref[...] = chebyshev_coefs(bins_ref)
-    rank, plan = station_order(table_ref[...])
-    plan_ref[...] = plan
-    count = table_ref.shape[1]
-    place = lax.broadcasted_iota(jnp.int32, (count, count), 0)
-    sorter_ref[...] = jnp.where(place == rank, 1.0, 0.0).astype(jnp.bfloat16)
+    plan_ref[...] = station_plan(table_ref[...], plan_ref.shape[1])
     outs = start_all(
         [
-            pltpu.make_async_copy(coef_ref, coef_hbm, sems.at[0]),
-            pltpu.make_async_copy(plan_ref, plan_hbm, sems.at[1]),
-            pltpu.make_async_copy(sorter_ref, sorter_hbm, sems.at[2]),
+            pltpu.make_async_copy(coef_ref, out_hbm.at[coef_at, pl.ds(0, LANES)], sems.at[0]),
+            pltpu.make_async_copy(plan_ref, out_hbm.at[plan_at, pl.ds(0, plan_ref.shape[1])], sems.at[1]),
         ]
     )
     turns = pick_columns(ids_ref, tables_ref, table_copies, nodes, left_ref, right_ref) * (1.0 / 256.0)
     bins = bins_column(bins_ref)
     for table in range(ntab):
         cosine, sine = cos_sin(bins * turns[table : table + 1])
-        cos_ref[table] = cosine
-        sin_ref[table] = sine
+        at = pl.ds(table * NF, NF)
+        cos_ref[at, :] = cosine
+        sin_ref[at, :] = sine
         outs += start_all(
             [
-                pltpu.make_async_copy(cos_ref.at[table], cos_hbm.at[table], sems.at[3 + 2 * table]),
-                pltpu.make_async_copy(sin_ref.at[table], sin_hbm.at[table], sems.at[4 + 2 * table]),
+                pltpu.make_async_copy(
+                    cos_ref.at[at, :], out_hbm.at[pl.ds(cos_at.start + table * NF, NF), pl.ds(0, nodes)],
+                    sems.at[3 + 2 * table],
+                ),
+                pltpu.make_async_copy(
+                    sin_ref.at[at, :], out_hbm.at[pl.ds(sin_at.start + table * NF, NF), pl.ds(0, nodes)],
+                    sems.at[4 + 2 * table],
+                ),
             ]
         )
     for copy in outs:
         copy.wait()
 
 
-def image_kernel(merged, stations_dev, plan_hbm, sorter_hbm, coef_hbm, cos_hbm, sin_hbm, block_hbm, *rest):
-    corr_hbm, rest = (None, rest) if merged else (rest[0], rest[1:])
-    keep_ref, send_ref, plan_ref, sorter_ref, coef_ref, block_ref, corr_ref, cos_ref, sin_ref, sems = rest[:10]
-    place_ref, weight_ref, left_ref, sums_ref, basis_a, basis_b = rest[10:]
-    pairs = [
-        (sorter_hbm, sorter_ref), (block_hbm, block_ref), (plan_hbm, plan_ref), (coef_hbm, coef_ref),
-        (cos_hbm, cos_ref), (sin_hbm, sin_ref),
-    ]
-    if not merged:
-        pairs.append((corr_hbm, corr_ref))
-    copies = [pltpu.make_async_copy(src, dst, sems.at[at]) for at, (src, dst) in enumerate(pairs)]
-    start_all(copies)
-    stations, nodes = place_ref.shape
+def image_kernel(merged, stations_dev, packed_hbm, block_ref, *rest):
+    corr_ref, rest = (None, rest) if merged else (rest[0], rest[1:])
+    keep_ref, send_ref, plan_ref, place_of_ref, coef_ref, cos_ref, sin_ref, sems = rest[:8]
+    place_ref, weight_ref, left_ref, sums_ref, basis_a, basis_b = rest[8:]
+    places, nodes = place_ref.shape
     windows, groups, cores = (lax.axis_size(a) for a in ("win", "sta", "freq"))
-    ntab = cos_ref.shape[0]
-    for copy in copies[:4] + copies[6:]:
-        copy.wait()
-    sorter = sorter_ref[...]
+    stations = stations_dev * groups
+    cos_at, sin_at, coef_at, plan_at = packed_rows(cos_ref.shape[0] // NF)
+    width = plan_ref.shape[1]
+    copies = start_all(
+        [
+            pltpu.make_async_copy(packed_hbm.at[plan_at, pl.ds(0, width)], place_of_ref, sems.at[0]),
+            pltpu.make_async_copy(packed_hbm.at[plan_at, pl.ds(0, width)], plan_ref, sems.at[1]),
+            pltpu.make_async_copy(packed_hbm.at[coef_at, pl.ds(0, LANES)], coef_ref, sems.at[2]),
+            pltpu.make_async_copy(packed_hbm.at[cos_at, pl.ds(0, nodes)], cos_ref, sems.at[3]),
+            pltpu.make_async_copy(packed_hbm.at[sin_at, pl.ds(0, nodes)], sin_ref, sems.at[4]),
+        ]
+    )
     height = block_ref.shape[1]
     rows_of = lambda win, core: [(win * groups + group) * cores + core for group in range(groups)]
-
-    if merged:
-        parts = []
-        for win in range(windows):
-            for core in range(cores):
-                for first in range(0, height - 8, stations_dev):
-                    rows = [block_ref[at, first : first + stations_dev, :] for at in rows_of(win, core)]
-                    parts.append(jnp.concatenate(rows, axis=0))
-        corr = jnp.concatenate(parts, axis=1)
-    else:
-        corr = corr_ref[...]
-    place_ref[...] = jnp.dot(sorter, corr, preferred_element_type=jnp.float32) * (1.0 / REACH)
 
     even, odd = [], []
     for win in range(windows):
@@ -285,18 +298,36 @@
         value = jnp.concatenate(value, axis=0)
         even.append(value)
         odd.append(jnp.concatenate([-value[:, NF:], value[:, :NF]], axis=1))
+    spectra = jnp.concatenate(even + odd, axis=1)
+    if merged:
+        parts = []
+        for win in range(windows):
+            for core in range(cores):
+                for first in range(0, height - 8, stations_dev):
+                    rows = [block_ref[at, first : first + stations_dev, :] for at in rows_of(win, core)]
+                    parts.append(jnp.concatenate(rows, axis=0))
+        corr = jnp.concatenate(parts, axis=1)
+    else:
+        corr = corr_ref[...]
+
+    copies[0].wait()
+    place_row = place_of_ref[4:5, :stations].astype(jnp.int32)
+    sorter = lax.broadcasted_iota(jnp.int32, (places, stations), 0) == place_row
+    sorter = jnp.where(sorter, 1.0, 0.0).astype(jnp.bfloat16)
     found = None
-    for piece in split_bf16(jnp.concatenate(even + odd, axis=1), 3):
+    for piece in split_bf16(spectra, 3):
         part = jnp.dot(sorter, piece, preferred_element_type=jnp.float32)
         found = part if found is None else found + part
     weight_ref[...] = found
+    place_ref[...] = jnp.dot(sorter, corr, preferred_element_type=jnp.float32) * (1.0 / REACH)
     sums_ref[...] = jnp.zeros_like(sums_ref)
     chunk = min(256, nodes)
     depth = DEGREES * 8
     lanes = windows * 2 * NF
-    total_groups = stations // 8
-
-    def make_left(pair, carry):
+    for copy in copies[1:3]:
+        copy.wait()
+
+    def make_left(pair):
         top = weight_ref[pl.ds(pl.multiple_of(pair * 16, 16), 8), :]
         bottom = weight_ref[pl.ds(pl.multiple_of(pair * 16 + 8, 8), 8), :]
         sides = [
@@ -312,16 +343,26 @@
             for term, value in enumerate(split_bf16(tall.T, 2)):
                 left_ref[2 * pair, term * lanes : (term + 1) * lanes, at] = value[:lanes]
                 left_ref[2 * pair + 1, term * lanes : (term + 1) * lanes, at] = value[lanes:]
-        return carry
-
-    lax.fori_loop(0, total_groups // 2, make_left, 0)
-    spot = lax.broadcasted_iota(jnp.int32, (16, depth), 1) % 8
-
-    def left_of(group, table):
-        here = spot + group * 8
-        mask = (here >= plan_ref[0, table]) & (here < plan_ref[0, table + 1])
-        mask = jnp.where(mask, 1.0, 0.0).astype(jnp.bfloat16)
-        return left_ref[group] * jnp.concatenate([mask] * (2 * lanes // 16), axis=0)
+
+    used = plan_ref[3, 0].astype(jnp.int32)
+    sure = stations // 16
+    if sure <= 8:
+        for pair in range(sure):
+            make_left(pair)
+    else:
+        lax.fori_loop(0, sure, lambda pair, carry: (make_left(pair), carry)[1], 0)
+    lax.fori_loop(sure, (used + 1) // 2, lambda pair, carry: (make_left(pair), carry)[1], 0)
+    spot = (lax.broadcasted_iota(jnp.int32, (16, depth), 1) & 7).astype(jnp.float32)
+
+    def left_of(group):
+        mask = spot < plan_ref[2, group]
+        results = []
+        for keep, drop in ((1.0, 0.0), (0.0, 1.0)):
+            side = jnp.where(mask, keep, drop).astype(jnp.bfloat16)
+            results.append(left_ref[group] * jnp.concatenate([side] * (2 * lanes // 16), axis=0))
+        high = jnp.concatenate([result[:lanes] for result in results], axis=0)
+        low = jnp.concatenate([result[lanes:] for result in results], axis=0)
+        return jnp.concatenate([high, high, low], axis=1)
 
     def basis_steps(group, basis_ref):
         arg = place_ref[pl.ds(pl.multiple_of(group * 8, 8), 8), :]
@@ -341,53 +382,38 @@
         for _ in steps:
             pass
 
-    def add_tables(group, table, basis_ref, steps):
-        other = jnp.minimum(table + 1, ntab - 1)
-        left_a, left_b = left_of(group, table), left_of(group, table + 1)
-        both = jnp.concatenate([left_a, left_b], axis=0)
-        high = jnp.concatenate([left_a[:lanes], left_b[:lanes]], axis=0)
+    def add_group(group, basis_ref, steps):
+        left = left_of(group)
+        tables = [plan_ref[slot, group].astype(jnp.int32) for slot in range(2)]
+        phasor_rows = [pl.ds(pl.multiple_of(table * NF, NF), NF) for table in tables]
         for first in range(0, nodes, chunk):
             at = slice(first, first + chunk)
-            got = jnp.dot(both, basis_ref[:depth, at], preferred_element_type=jnp.float32)
-            more = jnp.dot(high, basis_ref[depth:, at], preferred_element_type=jnp.float32)
+            right = jnp.concatenate([basis_ref[:, at], basis_ref[:depth, at]], axis=0)
+            got = jnp.dot(left, right, preferred_element_type=jnp.float32)
             next(steps, None)
-            for slot, place in enumerate((table, other)):
-                row = slot * 2 * lanes
-                value = got[row : row + lanes] + got[row + lanes : row + 2 * lanes]
-                value = value + more[slot * lanes : (slot + 1) * lanes]
-                cosine, sine = cos_ref[place, :, at], sin_ref[place, :, at]
-                for win in range(windows):
-                    row = win * 2 * NF
-                    real, imag = value[row : row + NF], value[row + NF : row + 2 * NF]
-                    sums_ref[row : row + NF, at] += real * cosine - imag * sine
-                    sums_ref[row + NF : row + 2 * NF, at] += real * sine + imag * cosine
+            for win in range(windows):
+                row = win * 2 * NF
+                real_sum, imag_sum = sums_ref[row : row + NF, at], sums_ref[row + NF : row + 2 * NF, at]
+                for slot, rows in enumerate(phasor_rows):
+                    cosine, sine = cos_ref[rows, at], sin_ref[rows, at]
+                    real = got[slot * lanes + row : slot * lanes + row + NF]
+                    imag = got[slot * lanes + row + NF : slot * lanes + row + 2 * NF]
+                    real_sum += real * cosine - imag * sine
+                    imag_sum += real * sine + imag * cosine
+                sums_ref[row : row + NF, at], sums_ref[row + NF : row + 2 * NF, at] = real_sum, imag_sum
         run(steps)
 
-    def more_tables(group, basis_ref):
-        first, last = plan_ref[1, group], plan_ref[2, group]
-
-        def step(turn, carry):
-            add_tables(group, first + 2 * turn, basis_ref, iter(()))
-            return carry
-
-        lax.fori_loop(1, (last - first) // 2 + 1, step, 0)
-
     run(basis_steps(0, basis_a))
-    for copy in copies[4:6]:
+    for copy in copies[3:]:
         copy.wait()
-
-    def stage(group, after, basis_ref, next_basis):
-        add_tables(group, plan_ref[1, group], basis_ref, basis_steps(after, next_basis))
-        more_tables(group, basis_ref)
 
     def body(pair, carry):
         group = pair * 2
-        after = jnp.minimum(group + 2, total_groups - 1)
-        stage(group, group + 1, basis_a, basis_b)
-        stage(group + 1, after, basis_b, basis_a)
+        add_group(group, basis_a, basis_steps(group + 1, basis_b))
+        add_group(group + 1, basis_b, basis_steps(jnp.minimum(group + 2, places // 8 - 1), basis_a))
         return carry
 
-    lax.fori_loop(0, total_groups // 2, body, 0)
+    lax.fori_loop(0, (used + 1) // 2, body, 0)
     powers = []
     for win in range(windows):
         row = win * 2 * NF
@@ -416,7 +442,7 @@
     devices = windows * groups * cores
     nodes = grid // devices
     ntab = tables.shape[0]
-    params = pltpu.CompilerParams(vmem_limit_bytes=VMEM_LIMIT)
+    params = lambda free: pltpu.CompilerParams(vmem_limit_bytes=VMEM_LIMIT - free)
     vmem = pl.BlockSpec(memory_space=pltpu.VMEM)
     hbm = pl.BlockSpec(memory_space=pltpu.HBM)
     bins = freq_bins.reshape(1, NF)
@@ -436,7 +462,7 @@
             pltpu.VMEM(traces.shape, traces.dtype),
             pltpu.SemaphoreType.DMA((2 + devices * max(pieces, 1),)),
         ],
-        compiler_params=params,
+        compiler_params=params(0),
         name="send",
     )(bins, traces, corrections)
     received = [lax.all_to_all(blocks, ("win", "sta", "freq"), split_axis=0, concat_axis=0, tiled=True)]
@@ -448,62 +474,60 @@
         received.append(corr.reshape(stations, nodes))
 
     wide = 512
-    products = [
-        ((ntab, NF, nodes), jnp.float32),
-        ((ntab, NF, nodes), jnp.float32),
-        ((DEGREES, LANES), jnp.float32),
-        ((stations, stations), jnp.bfloat16),
-        ((8, LANES), jnp.int32),
-    ]
-    cosine, sine, coefs, sorter, plan = pl.pallas_call(
+    plan_width = max(LANES, stations)
+    phasors = pltpu.VMEM((ntab * NF, nodes), jnp.float32)
+    coefs = pltpu.VMEM((DEGREES, LANES), jnp.float32)
+    plan = pltpu.VMEM((8, plan_width), jnp.float32)
+    packed_shape = (packed_rows(ntab)[-1].stop, max(nodes, plan_width))
+    packed = pl.pallas_call(
         prepare_kernel,
-        out_shape=[jax.ShapeDtypeStruct(*product) for product in products],
+        out_shape=jax.ShapeDtypeStruct(packed_shape, jnp.float32),
         in_specs=[hbm] * 4,
-        out_specs=[hbm] * 5,
+        out_specs=hbm,
         scratch_shapes=[
             bins_scratch,
             pltpu.VMEM((1, stations), jnp.int32),
             pltpu.VMEM((max(nodes // LANES, 8), LANES), jnp.int32),
             pltpu.VMEM(tables.shape, tables.dtype),
-        ]
-        + [pltpu.VMEM(*product) for product in products]
-        + [
+            phasors,
+            phasors,
+            coefs,
+            plan,
             pltpu.VMEM((grid // wide * ntab, 3 * wide), jnp.bfloat16),
             pltpu.VMEM((3 * wide, nodes), jnp.bfloat16),
             pltpu.SemaphoreType.DMA((3 + 2 * ntab,)),
             pltpu.SemaphoreType.DMA((TABLE_PIECES,)),
         ],
-        compiler_params=params,
+        compiler_params=params(blocks.size * 2 + 16 * 1024),
         name="prepare",
     )(bins, station_table.reshape(1, stations), node_ids.reshape(grid // LANES, LANES), tables)
 
+    places = (stations // 8 + ntab // 2 + 2) // 2 * 16
     half = jax.ShapeDtypeStruct((NF, nodes), jnp.float32)
     rows = 2 * windows * 2 * NF
     basis = pltpu.VMEM((2 * DEGREES * 8, nodes), jnp.bfloat16)
     keep, send = pl.pallas_call(
         functools.partial(image_kernel, merged, stations_dev),
         out_shape=[half, half],
-        in_specs=[hbm] * (5 + len(received)),
+        in_specs=[hbm] + [vmem] * len(received),
         out_specs=[vmem, vmem],
         scratch_shapes=[
-            pltpu.SMEM(*products[4]),
-            pltpu.VMEM(*products[3]),
-            pltpu.VMEM(*products[2]),
-            pltpu.VMEM((devices, height, LANES), jnp.bfloat16),
-            pltpu.VMEM((16, LANES) if merged else (stations, nodes), jnp.bfloat16),
-            pltpu.VMEM(*products[0]),
-            pltpu.VMEM(*products[1]),
-            pltpu.SemaphoreType.DMA((7,)),
-            pltpu.VMEM((stations, nodes), jnp.float32),
-            pltpu.VMEM((stations, rows), jnp.float32),
-            pltpu.VMEM((stations // 8, rows, DEGREES * 8), jnp.bfloat16),
+            pltpu.SMEM((8, plan_width), jnp.float32),
+            plan,
+            coefs,
+            phasors,
+            phasors,
+            pltpu.SemaphoreType.DMA((5,)),
+            pltpu.VMEM((places, nodes), jnp.float32),
+            pltpu.VMEM((places, rows), jnp.float32),
+            pltpu.VMEM((places // 8, rows, DEGREES * 8), jnp.bfloat16),
             pltpu.VMEM((rows // 2, nodes), jnp.float32),
             basis,
             basis,
         ],
-        compiler_params=params,
+        compiler_params=params(blocks.size * 2 + half.size * 8 + 16 * 1024),
         name="image",
-    )(plan, sorter, coefs, cosine, sine, *received)
+    )(packed, *received)
     got = lax.ppermute(send, "win", [(0, 1), (1, 0)])
     spectrum, beam_power = pl.pallas_call(
         functools.partial(finish_kernel, stations),
@@ -513,7 +537,7 @@
         ],
         in_specs=[vmem, vmem],
         out_specs=[vmem, vmem],
-        compiler_params=params,
+        compiler_params=params(32 * 1024 * 1024),
         name="finish",
     )(keep, got)
     return spectrum, beam_power.reshape(windows * nodes)

time: 41.8 us -> 40.8 us (0.976)
  Pallas kernels: 24.5 us -> 22.7 us
  local copies, waits for them, and re-layouts: 0 us -> 1.55 us
    unnamed x0 -> x4, local copies, waits for them, and re-layouts: none -> 1.55 us
    pallas_call x1, Pallas kernels: 12.4 us -> 11.3 us  [on_device(): pl.pallas_call(functools.partial(image_kernel, merged, stations_dev), out...]
    pallas_call x1, Pallas kernels: 1.57 us -> 0.69 us  [on_device(): pl.pallas_call(functools.partial(finish_kernel, stations), out_shape=[jax...]
  transfers between devices with their start and end apart: 2 -> 2, of which waited for: 2 -> 2; matrix products, arithmetic and copies ran while one was open for 0% -> 0% of each run, Pallas kernels for 19% -> 20%
where the time goes in v6:
time: 40.8 us; the launch traced here: 40.5 us
  Pallas kernels  22.7 us (56%)
  starting transfers between devices  8.38 us (21%)
  waiting for transfers between devices  7.24 us (18%)
  local copies, waits for them, and re-layouts  1.55 us (4%)
  between operations  0.66 us (2%)
    pallas_call x1, Pallas kernels, on_device(): pl.pallas_call(functools.partial(image_kernel, merged, stations_dev), out...  11.3 us
    pallas_call x1, Pallas kernels, on_device(): pl.pallas_call(prepare_kernel, out_shape=jax.ShapeDtypeStruct(packed_shap...  7.92 us
    all_to_all x1, starting transfers between devices, on_device(): lax.all_to_all(blocks, ('win', 'sta', 'freq'), split_axis=0, concat_axis=...  7.3 us
    all_to_all x1, waiting for transfers between devices, on_device(): lax.all_to_all(blocks, ('win', 'sta', 'freq'), split_axis=0, concat_axis=...  3.78 us
    ppermute x1, waiting for transfers between devices, on_device(): got = lax.ppermute(send, 'win', [(0, 1), (1, 0)])  3.47 us
    pallas_call x1, Pallas kernels, on_device(): pl.pallas_call(functools.partial(send_kernel, nodes), out_shape=jax.Shape...  2.73 us
    unnamed x4, local copies, waits for them, and re-layouts  1.55 us
    ppermute x1, starting transfers between devices, on_device(): got = lax.ppermute(send, 'win', [(0, 1), (1, 0)])  1.08 us
  transfers between devices with their start and end apart: 2, of which 2 were waited for; matrix products, arithmetic and copies ran while one was open for 0% of the time, Pallas kernels for 20%

profile of v6, /device:TPU:0, one launch (start us, length us, event | category | flops | bytes accessed | tf_op | source)
XLA Modules:
  0.0 40.5 jit_solution(8321580013939278085)
XLA Ops:
  0.6 2.7 %send.1 = bf16[32,40,128]{2,1,0:T(8,128)(2,1)} custom-call(s32[1,16]{1,0:T(1,128)} %bitcast.5, bf16[16,2560]{1,0:T(8,128)(2,1)} %traces_hbm.1, bf16[16,32768]{1,0:T(8,128)(2,1)} %corr_hbm.1), custom_call_target="tpu_custom_call" | custom-call | tf_op jit(solution)/shard_map/send/pallas_call | solution.py:455
  3.4 7.3 %all-to-all-start = ((bf16[32,40,128]{2,1,0:T(8,128)(2,1)}), bf16[32,40,128]{2,1,0:T(8,128)(2,1)S(1)}, u32[]{:S(2)}, u32[]{:S(2)}) async-start(bf16[32,40,128]{2,1,0:T(8,128)(2,1)} %send.1), calls=%async_computation | async-start | bytes 655360 | tf_op jit(solution)/shard_map/all_to_all | solution.py:468
  10.7 7.9 %prepare.1.packed_hbm = f32[552,1024]{1,0:T(8,128)} custom-call(s32[1,16]{1,0:T(1,128)} %bitcast.6, s32[1,128]{1,0:T(1,128)} %bitcast.7, s32[256,128]{1,0:T(8,128)} %bitcast.4, f32[16,32768]{1,0:T(8,128)} %tables_hbm.1), custom_call_target="tpu_custom_call" | custom-call | tf_op jit(solution)/shard_map/prepare/pallas_call | solution.py:482
  18.6 3.8 %all-to-all-done.block_ref = bf16[32,40,128]{2,1,0:T(8,128)(2,1)S(1)} async-done(((bf16[32,40,128]{2,1,0:T(8,128)(2,1)}), bf16[32,40,128]{2,1,0:T(8,128)(2,1)S(1)}, u32[]{:S(2)}, u32[]{:S(2)}) %all-to-all-start) | async-done | bytes 327712 | tf_op jit(solution)/shard_map/all_to_all | solution.py:468
  22.4 0.0 copy-start.1
  22.4 0.7 %copy-done.1 = bf16[32,40,128]{2,1,0:T(8,128)(2,1)} copy-done((bf16[32,40,128]{2,1,0:T(8,128)(2,1)}, bf16[32,40,128]{2,1,0:T(8,128)(2,1)S(1)}, u32[]{:S(2)}) %copy-start.1) | copy-done | bytes 327704
  23.1 11.3 %image.1 = (f32[16,1024]{1,0:T(8,128)}, f32[16,1024]{1,0:T(8,128)}) custom-call(f32[552,1024]{1,0:T(8,128)} %prepare.1.packed_hbm, bf16[32,40,128]{2,1,0:T(8,128)(2,1)} %copy-done.1), custom_call_target="tpu_custom_call" | custom-call | tf_op jit(solution)/shard_map/image/pallas_call | solution.py:509
  34.4 1.1 %collective-permute-start = (f32[16,1024]{1,0:T(8,128)}, f32[16,1024]{1,0:T(8,128)S(1)}, u32[]{:S(2)}, u32[]{:S(2)}) collective-permute-start(f32[16,1024]{1,0:T(8,128)} %get-tuple-element.7), channel_id=1, source_target_pairs={{0,16},{16,0},{1,17},{17,1},{2,18},{18,2},{3,19},{19,3},{4,20},{20... | collective-permute-start | bytes 196616 | tf_op jit(solution)/shard_map/ppermute | solution.py:531
  35.5 3.5 %collective-permute-done.got_ref = f32[16,1024]{1,0:T(8,128)S(1)} collective-permute-done((f32[16,1024]{1,0:T(8,128)}, f32[16,1024]{1,0:T(8,128)S(1)}, u32[]{:S(2)}, u32[]{:S(2)}) %collective-permute-start) | collective-permute-done | bytes 65568 | tf_op jit(solution)/shard_map/ppermute | solution.py:531
  39.0 0.0 copy-start
  39.0 0.8 %copy-done = f32[16,1024]{1,0:T(8,128)S(1)} copy-done((f32[16,1024]{1,0:T(8,128)S(1)}, f32[16,1024]{1,0:T(8,128)}, u32[]{:S(2)}) %copy-start) | copy-done | bytes 65560
  39.8 0.7 %finish.1 = (f32[16,2048]{1,0:T(8,128)}, f32[1,2048]{1,0:T(1,128)}) custom-call(f32[16,1024]{1,0:T(8,128)S(1)} %copy-done, f32[16,1024]{1,0:T(8,128)S(1)} %collective-permute-done.got_ref), custom_call_target="tpu_custom_call" | custom-call | tf_op jit(solution)/shard_map/finish/pallas_call | solution.py:532
Async XLA Ops:
  3.4 19.0 %all-to-all-start = ((bf16[32,40,128]{2,1,0:T(8,128)(2,1)}), bf16[32,40,128]{2,1,0:T(8,128)(2,1)S(1)}, u32[]{:S(2)}, u32[]{:S(2)}) async-start(bf16[32,40,128]{2,1,0:T(8,128)(2,1)} %send.1), calls=%async_computation | async-start | bytes 655360 | tf_op jit(solution)/shard_map/all_to_all | solution.py:468
  22.4 0.7 %copy-start.1 = (bf16[32,40,128]{2,1,0:T(8,128)(2,1)}, bf16[32,40,128]{2,1,0:T(8,128)(2,1)S(1)}, u32[]{:S(2)}) copy-start(bf16[32,40,128]{2,1,0:T(8,128)(2,1)S(1)} %all-to-all-done.block_ref) | copy-start | bytes 983044
  34.4 4.5 %collective-permute-start = (f32[16,1024]{1,0:T(8,128)}, f32[16,1024]{1,0:T(8,128)S(1)}, u32[]{:S(2)}, u32[]{:S(2)}) collective-permute-start(f32[16,1024]{1,0:T(8,128)} %get-tuple-element.7), channel_id=1, source_target_pairs={{0,16},{16,0},{1,17},{17,1},{2,18},{18,2},{3,19},{19,3},{4,20},{20... | collective-permute-start | bytes 196616 | tf_op jit(solution)/shard_map/ppermute | solution.py:531
  39.0 0.8 %copy-start = (f32[16,1024]{1,0:T(8,128)S(1)}, f32[16,1024]{1,0:T(8,128)}, u32[]{:S(2)}) copy-start(f32[16,1024]{1,0:T(8,128)} %get-tuple-element.6.keep_ref) | copy-start | bytes 196612

commit v7 on v6

--- a/solution.py
+++ b/solution.py
@@ -498,7 +498,7 @@
             pltpu.SemaphoreType.DMA((3 + 2 * ntab,)),
             pltpu.SemaphoreType.DMA((TABLE_PIECES,)),
         ],
-        compiler_params=params(blocks.size * 2 + 16 * 1024),
+        compiler_params=params(512 * 1024),
         name="prepare",
     )(bins, station_table.reshape(1, stations), node_ids.reshape(grid // LANES, LANES), tables)
 
@@ -525,7 +525,7 @@
             basis,
             basis,
         ],
-        compiler_params=params(blocks.size * 2 + half.size * 8 + 16 * 1024),
+        compiler_params=params(1024 * 1024),
         name="image",
     )(packed, *received)
     got = lax.ppermute(send, "win", [(0, 1), (1, 0)])

time: 40.8 us -> 40.8 us (level)
  no operation moved by 1% of the time
where the time goes in v7:
time: 40.8 us; the launch traced here: 40.5 us
  Pallas kernels  22.7 us (56%)
  starting transfers between devices  8.38 us (21%)
  waiting for transfers between devices  7.24 us (18%)
  local copies, waits for them, and re-layouts  1.55 us (4%)
  between operations  0.66 us (2%)
    pallas_call x1, Pallas kernels, on_device(): pl.pallas_call(functools.partial(image_kernel, merged, stations_dev), out...  11.3 us
    pallas_call x1, Pallas kernels, on_device(): pl.pallas_call(prepare_kernel, out_shape=jax.ShapeDtypeStruct(packed_shap...  7.92 us
    all_to_all x1, starting transfers between devices, on_device(): lax.all_to_all(blocks, ('win', 'sta', 'freq'), split_axis=0, concat_axis=...  7.3 us
    all_to_all x1, waiting for transfers between devices, on_device(): lax.all_to_all(blocks, ('win', 'sta', 'freq'), split_axis=0, concat_axis=...  3.78 us
    ppermute x1, waiting for transfers between devices, on_device(): got = lax.ppermute(send, 'win', [(0, 1), (1, 0)])  3.47 us
    pallas_call x1, Pallas kernels, on_device(): pl.pallas_call(functools.partial(send_kernel, nodes), out_shape=jax.Shape...  2.73 us
    unnamed x4, local copies, waits for them, and re-layouts  1.55 us
    ppermute x1, starting transfers between devices, on_device(): got = lax.ppermute(send, 'win', [(0, 1), (1, 0)])  1.08 us
  transfers between devices with their start and end apart: 2, of which 2 were waited for; matrix products, arithmetic and copies ran while one was open for 0% of the time, Pallas kernels for 20%

profile of v7, /device:TPU:0, one launch (start us, length us, event | category | flops | bytes accessed | tf_op | source)
XLA Modules:
  0.0 40.5 jit_solution(11411374850107191407)
XLA Ops:
  0.6 2.7 %send.1 = bf16[32,40,128]{2,1,0:T(8,128)(2,1)} custom-call(s32[1,16]{1,0:T(1,128)} %bitcast.5, bf16[16,2560]{1,0:T(8,128)(2,1)} %traces_hbm.1, bf16[16,32768]{1,0:T(8,128)(2,1)} %corr_hbm.1), custom_call_target="tpu_custom_call" | custom-call | tf_op jit(solution)/shard_map/send/pallas_call | solution.py:455
  3.4 7.3 %all-to-all-start = ((bf16[32,40,128]{2,1,0:T(8,128)(2,1)}), bf16[32,40,128]{2,1,0:T(8,128)(2,1)S(1)}, u32[]{:S(2)}, u32[]{:S(2)}) async-start(bf16[32,40,128]{2,1,0:T(8,128)(2,1)} %send.1), calls=%async_computation | async-start | bytes 655360 | tf_op jit(solution)/shard_map/all_to_all | solution.py:468
  10.7 7.9 %prepare.1.packed_hbm = f32[552,1024]{1,0:T(8,128)} custom-call(s32[1,16]{1,0:T(1,128)} %bitcast.6, s32[1,128]{1,0:T(1,128)} %bitcast.7, s32[256,128]{1,0:T(8,128)} %bitcast.4, f32[16,32768]{1,0:T(8,128)} %tables_hbm.1), custom_call_target="tpu_custom_call" | custom-call | tf_op jit(solution)/shard_map/prepare/pallas_call | solution.py:482
  18.6 3.8 %all-to-all-done.block_ref = bf16[32,40,128]{2,1,0:T(8,128)(2,1)S(1)} async-done(((bf16[32,40,128]{2,1,0:T(8,128)(2,1)}), bf16[32,40,128]{2,1,0:T(8,128)(2,1)S(1)}, u32[]{:S(2)}, u32[]{:S(2)}) %all-to-all-start) | async-done | bytes 327712 | tf_op jit(solution)/shard_map/all_to_all | solution.py:468
  22.4 0.0 copy-start.1
  22.4 0.7 %copy-done.1 = bf16[32,40,128]{2,1,0:T(8,128)(2,1)} copy-done((bf16[32,40,128]{2,1,0:T(8,128)(2,1)}, bf16[32,40,128]{2,1,0:T(8,128)(2,1)S(1)}, u32[]{:S(2)}) %copy-start.1) | copy-done | bytes 327704
  23.1 11.3 %image.1 = (f32[16,1024]{1,0:T(8,128)}, f32[16,1024]{1,0:T(8,128)}) custom-call(f32[552,1024]{1,0:T(8,128)} %prepare.1.packed_hbm, bf16[32,40,128]{2,1,0:T(8,128)(2,1)} %copy-done.1), custom_call_target="tpu_custom_call" | custom-call | tf_op jit(solution)/shard_map/image/pallas_call | solution.py:509
  34.4 1.1 %collective-permute-start = (f32[16,1024]{1,0:T(8,128)}, f32[16,1024]{1,0:T(8,128)S(1)}, u32[]{:S(2)}, u32[]{:S(2)}) collective-permute-start(f32[16,1024]{1,0:T(8,128)} %get-tuple-element.7), channel_id=1, source_target_pairs={{0,16},{16,0},{1,17},{17,1},{2,18},{18,2},{3,19},{19,3},{4,20},{20... | collective-permute-start | bytes 196616 | tf_op jit(solution)/shard_map/ppermute | solution.py:531
  35.5 3.5 %collective-permute-done.got_ref = f32[16,1024]{1,0:T(8,128)S(1)} collective-permute-done((f32[16,1024]{1,0:T(8,128)}, f32[16,1024]{1,0:T(8,128)S(1)}, u32[]{:S(2)}, u32[]{:S(2)}) %collective-permute-start) | collective-permute-done | bytes 65568 | tf_op jit(solution)/shard_map/ppermute | solution.py:531
  39.0 0.0 copy-start
  39.0 0.8 %copy-done = f32[16,1024]{1,0:T(8,128)S(1)} copy-done((f32[16,1024]{1,0:T(8,128)S(1)}, f32[16,1024]{1,0:T(8,128)}, u32[]{:S(2)}) %copy-start) | copy-done | bytes 65560
  39.8 0.7 %finish.1 = (f32[16,2048]{1,0:T(8,128)}, f32[1,2048]{1,0:T(1,128)}) custom-call(f32[16,1024]{1,0:T(8,128)S(1)} %copy-done, f32[16,1024]{1,0:T(8,128)S(1)} %collective-permute-done.got_ref), custom_call_target="tpu_custom_call" | custom-call | tf_op jit(solution)/shard_map/finish/pallas_call | solution.py:532
Async XLA Ops:
  3.4 19.0 %all-to-all-start = ((bf16[32,40,128]{2,1,0:T(8,128)(2,1)}), bf16[32,40,128]{2,1,0:T(8,128)(2,1)S(1)}, u32[]{:S(2)}, u32[]{:S(2)}) async-start(bf16[32,40,128]{2,1,0:T(8,128)(2,1)} %send.1), calls=%async_computation | async-start | bytes 655360 | tf_op jit(solution)/shard_map/all_to_all | solution.py:468
  22.4 0.7 %copy-start.1 = (bf16[32,40,128]{2,1,0:T(8,128)(2,1)}, bf16[32,40,128]{2,1,0:T(8,128)(2,1)S(1)}, u32[]{:S(2)}) copy-start(bf16[32,40,128]{2,1,0:T(8,128)(2,1)S(1)} %all-to-all-done.block_ref) | copy-start | bytes 983044
  34.4 4.5 %collective-permute-start = (f32[16,1024]{1,0:T(8,128)}, f32[16,1024]{1,0:T(8,128)S(1)}, u32[]{:S(2)}, u32[]{:S(2)}) collective-permute-start(f32[16,1024]{1,0:T(8,128)} %get-tuple-element.7), channel_id=1, source_target_pairs={{0,16},{16,0},{1,17},{17,1},{2,18},{18,2},{3,19},{19,3},{4,20},{20... | collective-permute-start | bytes 196616 | tf_op jit(solution)/shard_map/ppermute | solution.py:531
  39.0 0.8 %copy-start = (f32[16,1024]{1,0:T(8,128)S(1)}, f32[16,1024]{1,0:T(8,128)}, u32[]{:S(2)}) copy-start(f32[16,1024]{1,0:T(8,128)} %get-tuple-element.6.keep_ref) | copy-start | bytes 196612

commit v8 on v7

--- a/solution.py
+++ b/solution.py
@@ -361,8 +361,7 @@
             side = jnp.where(mask, keep, drop).astype(jnp.bfloat16)
             results.append(left_ref[group] * jnp.concatenate([side] * (2 * lanes // 16), axis=0))
         high = jnp.concatenate([result[:lanes] for result in results], axis=0)
-        low = jnp.concatenate([result[lanes:] for result in results], axis=0)
-        return jnp.concatenate([high, high, low], axis=1)
+        return jnp.concatenate(results, axis=0), high
 
     def basis_steps(group, basis_ref):
         arg = place_ref[pl.ds(pl.multiple_of(group * 8, 8), 8), :]
@@ -383,21 +382,26 @@
             pass
 
     def add_group(group, basis_ref, steps):
-        left = left_of(group)
+        both, high = left_of(group)
         tables = [plan_ref[slot, group].astype(jnp.int32) for slot in range(2)]
         phasor_rows = [pl.ds(pl.multiple_of(table * NF, NF), NF) for table in tables]
         for first in range(0, nodes, chunk):
             at = slice(first, first + chunk)
-            right = jnp.concatenate([basis_ref[:, at], basis_ref[:depth, at]], axis=0)
-            got = jnp.dot(left, right, preferred_element_type=jnp.float32)
+            got = jnp.dot(both, basis_ref[:depth, at], preferred_element_type=jnp.float32)
+            more = jnp.dot(high, basis_ref[depth:, at], preferred_element_type=jnp.float32)
             next(steps, None)
+            got = [
+                got[2 * slot * lanes : (2 * slot + 1) * lanes]
+                + got[(2 * slot + 1) * lanes : (2 * slot + 2) * lanes]
+                + more[slot * lanes : (slot + 1) * lanes]
+                for slot in range(2)
+            ]
             for win in range(windows):
                 row = win * 2 * NF
                 real_sum, imag_sum = sums_ref[row : row + NF, at], sums_ref[row + NF : row + 2 * NF, at]
                 for slot, rows in enumerate(phasor_rows):
                     cosine, sine = cos_ref[rows, at], sin_ref[rows, at]
-                    real = got[slot * lanes + row : slot * lanes + row + NF]
-                    imag = got[slot * lanes + row + NF : slot * lanes + row + 2 * NF]
+                    real, imag = got[slot][row : row + NF], got[slot][row + NF : row + 2 * NF]
                     real_sum += real * cosine - imag * sine
                     imag_sum += real * sine + imag * cosine
                 sums_ref[row : row + NF, at], sums_ref[row + NF : row + 2 * NF, at] = real_sum, imag_sum
@@ -525,7 +529,7 @@
             basis,
             basis,
         ],
-        compiler_params=params(1024 * 1024),
+        compiler_params=params(23 * 512 * 1024),
         name="image",
     )(packed, *received)
     got = lax.ppermute(send, "win", [(0, 1), (1, 0)])

time: 40.8 us -> 37.1 us (0.909)
  Pallas kernels: 22.7 us -> 20.7 us
  local copies, waits for them, and re-layouts: 1.55 us -> 0 us
    pallas_call x1, Pallas kernels: 11.3 us -> 9.38 us  [on_device(): pl.pallas_call(functools.partial(image_kernel, merged, stations_dev), out...]
    unnamed x4 -> x0, local copies, waits for them, and re-layouts: 1.55 us -> none
  transfers between devices with their start and end apart: 2 -> 2, of which waited for: 2 -> 2; matrix products, arithmetic and copies ran while one was open for 0% -> 0% of each run, Pallas kernels for 20% -> 21%
where the time goes in v8:
time: 37.1 us; the launch traced here: 36.8 us
  Pallas kernels  20.7 us (56%)
  starting transfers between devices  8.37 us (23%)
  waiting for transfers between devices  7.07 us (19%)
  between operations  0.66 us (2%)
    pallas_call x1, Pallas kernels, on_device(): pl.pallas_call(functools.partial(image_kernel, merged, stations_dev), out...  9.38 us
    pallas_call x1, Pallas kernels, on_device(): pl.pallas_call(prepare_kernel, out_shape=jax.ShapeDtypeStruct(packed_shap...  7.88 us
    all_to_all x1, starting transfers between devices, on_device(): lax.all_to_all(blocks, ('win', 'sta', 'freq'), split_axis=0, concat_axis=...  7.3 us
    all_to_all x1, waiting for transfers between devices, on_device(): lax.all_to_all(blocks, ('win', 'sta', 'freq'), split_axis=0, concat_axis=...  3.81 us
    ppermute x1, waiting for transfers between devices, on_device(): got = lax.ppermute(send, 'win', [(0, 1), (1, 0)])  3.26 us
    pallas_call x1, Pallas kernels, on_device(): pl.pallas_call(functools.partial(send_kernel, nodes), out_shape=jax.Shape...  2.74 us
    ppermute x1, starting transfers between devices, on_device(): got = lax.ppermute(send, 'win', [(0, 1), (1, 0)])  1.07 us
  transfers between devices with their start and end apart: 2, of which 2 were waited for; matrix products, arithmetic and copies ran while one was open for 0% of the time, Pallas kernels for 21%

profile of v8, /device:TPU:0, one launch (start us, length us, event | category | flops | bytes accessed | tf_op | source)
XLA Modules:
  0.0 36.8 jit_solution(12687960976990661762)
XLA Ops:
  0.6 2.7 %send.1 = bf16[32,40,128]{2,1,0:T(8,128)(2,1)} custom-call(s32[1,16]{1,0:T(1,128)} %bitcast.5, bf16[16,2560]{1,0:T(8,128)(2,1)} %traces_hbm.1, bf16[16,32768]{1,0:T(8,128)(2,1)} %corr_hbm.1), custom_call_target="tpu_custom_call" | custom-call | tf_op jit(solution)/shard_map/send/pallas_call | solution.py:459
  3.4 7.3 %all-to-all-start = ((bf16[32,40,128]{2,1,0:T(8,128)(2,1)}), bf16[32,40,128]{2,1,0:T(8,128)(2,1)S(1)}, u32[]{:S(2)}, u32[]{:S(2)}) async-start(bf16[32,40,128]{2,1,0:T(8,128)(2,1)} %send.1), calls=%async_computation | async-start | bytes 655360 | tf_op jit(solution)/shard_map/all_to_all | solution.py:472
  10.7 7.9 %prepare.1.packed_hbm = f32[552,1024]{1,0:T(8,128)} custom-call(s32[1,16]{1,0:T(1,128)} %bitcast.6, s32[1,128]{1,0:T(1,128)} %bitcast.7, s32[256,128]{1,0:T(8,128)} %bitcast.4, f32[16,32768]{1,0:T(8,128)} %tables_hbm.1), custom_call_target="tpu_custom_call" | custom-call | tf_op jit(solution)/shard_map/prepare/pallas_call | solution.py:486
  18.6 3.8 %all-to-all-done.block_ref = bf16[32,40,128]{2,1,0:T(8,128)(2,1)S(1)} async-done(((bf16[32,40,128]{2,1,0:T(8,128)(2,1)}), bf16[32,40,128]{2,1,0:T(8,128)(2,1)S(1)}, u32[]{:S(2)}, u32[]{:S(2)}) %all-to-all-start) | async-done | bytes 327712 | tf_op jit(solution)/shard_map/all_to_all | solution.py:472
  22.4 9.4 %image.1 = (f32[16,1024]{1,0:T(8,128)S(1)}, f32[16,1024]{1,0:T(8,128)S(1)}) custom-call(f32[552,1024]{1,0:T(8,128)} %prepare.1.packed_hbm, bf16[32,40,128]{2,1,0:T(8,128)(2,1)S(1)} %all-to-all-done.block_ref), custom_call_target="tpu_custom_call" | custom-call | tf_op jit(solution)/shard_map/image/pallas_call | solution.py:513
  31.8 1.1 %collective-permute-start = (f32[16,1024]{1,0:T(8,128)S(1)}, f32[16,1024]{1,0:T(8,128)S(1)}, u32[]{:S(2)}, u32[]{:S(2)}) collective-permute-start(f32[16,1024]{1,0:T(8,128)S(1)} %get-tuple-element.7), channel_id=1, source_target_pairs={{0,16},{16,0},{1,17},{17,1},{2,18},{18,2},{3,19},{19,3},{4,20},{20... | collective-permute-start | bytes 196616 | tf_op jit(solution)/shard_map/ppermute | solution.py:535
  32.9 3.3 %collective-permute-done.got_ref = f32[16,1024]{1,0:T(8,128)S(1)} collective-permute-done((f32[16,1024]{1,0:T(8,128)S(1)}, f32[16,1024]{1,0:T(8,128)S(1)}, u32[]{:S(2)}, u32[]{:S(2)}) %collective-permute-start) | collective-permute-done | bytes 65568 | tf_op jit(solution)/shard_map/ppermute | solution.py:535
  36.1 0.7 %finish.1 = (f32[16,2048]{1,0:T(8,128)}, f32[1,2048]{1,0:T(1,128)}) custom-call(f32[16,1024]{1,0:T(8,128)S(1)} %get-tuple-element.6.keep_ref, f32[16,1024]{1,0:T(8,128)S(1)} %collective-permute-done.got_ref), custom_call_target="tpu_custom_call" | custom-call | tf_op jit(solution)/shard_map/finish/pallas_call | solution.py:536
Async XLA Ops:
  3.4 19.0 %all-to-all-start = ((bf16[32,40,128]{2,1,0:T(8,128)(2,1)}), bf16[32,40,128]{2,1,0:T(8,128)(2,1)S(1)}, u32[]{:S(2)}, u32[]{:S(2)}) async-start(bf16[32,40,128]{2,1,0:T(8,128)(2,1)} %send.1), calls=%async_computation | async-start | bytes 655360 | tf_op jit(solution)/shard_map/all_to_all | solution.py:472
  31.8 4.3 %collective-permute-start = (f32[16,1024]{1,0:T(8,128)S(1)}, f32[16,1024]{1,0:T(8,128)S(1)}, u32[]{:S(2)}, u32[]{:S(2)}) collective-permute-start(f32[16,1024]{1,0:T(8,128)S(1)} %get-tuple-element.7), channel_id=1, source_target_pairs={{0,16},{16,0},{1,17},{17,1},{2,18},{18,2},{3,19},{19,3},{4,20},{20... | collective-permute-start | bytes 196616 | tf_op jit(solution)/shard_map/ppermute | solution.py:535

commit v9 on v7

--- a/solution.py
+++ b/solution.py
@@ -321,7 +321,7 @@
     weight_ref[...] = found
     place_ref[...] = jnp.dot(sorter, corr, preferred_element_type=jnp.float32) * (1.0 / REACH)
     sums_ref[...] = jnp.zeros_like(sums_ref)
-    chunk = min(256, nodes)
+    chunk = nodes
     depth = DEGREES * 8
     lanes = windows * 2 * NF
     for copy in copies[1:3]:
@@ -390,7 +390,7 @@
             at = slice(first, first + chunk)
             right = jnp.concatenate([basis_ref[:, at], basis_ref[:depth, at]], axis=0)
             got = jnp.dot(left, right, preferred_element_type=jnp.float32)
-            next(steps, None)
+            run(steps)
             for win in range(windows):
                 row = win * 2 * NF
                 real_sum, imag_sum = sums_ref[row : row + NF, at], sums_ref[row + NF : row + 2 * NF, at]
@@ -525,7 +525,7 @@
             basis,
             basis,
         ],
-        compiler_params=params(1024 * 1024),
+        compiler_params=params(23 * 512 * 1024),
         name="image",
     )(packed, *received)
     got = lax.ppermute(send, "win", [(0, 1), (1, 0)])

time: 40.8 us -> 37.8 us (0.926)
  local copies, waits for them, and re-layouts: 1.55 us -> 0 us
  Pallas kernels: 22.7 us -> 21.5 us
    unnamed x4 -> x0, local copies, waits for them, and re-layouts: 1.55 us -> none
    pallas_call x1, Pallas kernels: 11.3 us -> 10.1 us  [on_device(): pl.pallas_call(functools.partial(image_kernel, merged, stations_dev), out...]
  transfers between devices with their start and end apart: 2 -> 2, of which waited for: 2 -> 2; matrix products, arithmetic and copies ran while one was open for 0% -> 0% of each run, Pallas kernels for 20% -> 21%
where the time goes in v9:
time: 37.8 us; the launch traced here: 37.6 us
  Pallas kernels  21.5 us (57%)
  starting transfers between devices  8.37 us (22%)
  waiting for transfers between devices  7.07 us (19%)
  between operations  0.66 us (2%)
    pallas_call x1, Pallas kernels, on_device(): pl.pallas_call(functools.partial(image_kernel, merged, stations_dev), out...  10.1 us
    pallas_call x1, Pallas kernels, on_device(): pl.pallas_call(prepare_kernel, out_shape=jax.ShapeDtypeStruct(packed_shap...  7.88 us
    all_to_all x1, starting transfers between devices, on_device(): lax.all_to_all(blocks, ('win', 'sta', 'freq'), split_axis=0, concat_axis=...  7.3 us
    all_to_all x1, waiting for transfers between devices, on_device(): lax.all_to_all(blocks, ('win', 'sta', 'freq'), split_axis=0, concat_axis=...  3.81 us
    ppermute x1, waiting for transfers between devices, on_device(): got = lax.ppermute(send, 'win', [(0, 1), (1, 0)])  3.26 us
    pallas_call x1, Pallas kernels, on_device(): pl.pallas_call(functools.partial(send_kernel, nodes), out_shape=jax.Shape...  2.74 us
    ppermute x1, starting transfers between devices, on_device(): got = lax.ppermute(send, 'win', [(0, 1), (1, 0)])  1.07 us
  transfers between devices with their start and end apart: 2, of which 2 were waited for; matrix products, arithmetic and copies ran while one was open for 0% of the time, Pallas kernels for 21%

profile of v9, /device:TPU:0, one launch (start us, length us, event | category | flops | bytes accessed | tf_op | source)
XLA Modules:
  0.0 37.6 jit_solution(3727448470235998121)
XLA Ops:
  0.6 2.7 %send.1 = bf16[32,40,128]{2,1,0:T(8,128)(2,1)} custom-call(s32[1,16]{1,0:T(1,128)} %bitcast.5, bf16[16,2560]{1,0:T(8,128)(2,1)} %traces_hbm.1, bf16[16,32768]{1,0:T(8,128)(2,1)} %corr_hbm.1), custom_call_target="tpu_custom_call" | custom-call | tf_op jit(solution)/shard_map/send/pallas_call | solution.py:455
  3.4 7.3 %all-to-all-start = ((bf16[32,40,128]{2,1,0:T(8,128)(2,1)}), bf16[32,40,128]{2,1,0:T(8,128)(2,1)S(1)}, u32[]{:S(2)}, u32[]{:S(2)}) async-start(bf16[32,40,128]{2,1,0:T(8,128)(2,1)} %send.1), calls=%async_computation | async-start | bytes 655360 | tf_op jit(solution)/shard_map/all_to_all | solution.py:468
  10.7 7.9 %prepare.1.packed_hbm = f32[552,1024]{1,0:T(8,128)} custom-call(s32[1,16]{1,0:T(1,128)} %bitcast.6, s32[1,128]{1,0:T(1,128)} %bitcast.7, s32[256,128]{1,0:T(8,128)} %bitcast.4, f32[16,32768]{1,0:T(8,128)} %tables_hbm.1), custom_call_target="tpu_custom_call" | custom-call | tf_op jit(solution)/shard_map/prepare/pallas_call | solution.py:482
  18.6 3.8 %all-to-all-done.block_ref = bf16[32,40,128]{2,1,0:T(8,128)(2,1)S(1)} async-done(((bf16[32,40,128]{2,1,0:T(8,128)(2,1)}), bf16[32,40,128]{2,1,0:T(8,128)(2,1)S(1)}, u32[]{:S(2)}, u32[]{:S(2)}) %all-to-all-start) | async-done | bytes 327712 | tf_op jit(solution)/shard_map/all_to_all | solution.py:468
  22.4 10.1 %image.1 = (f32[16,1024]{1,0:T(8,128)S(1)}, f32[16,1024]{1,0:T(8,128)S(1)}) custom-call(f32[552,1024]{1,0:T(8,128)} %prepare.1.packed_hbm, bf16[32,40,128]{2,1,0:T(8,128)(2,1)S(1)} %all-to-all-done.block_ref), custom_call_target="tpu_custom_call" | custom-call | tf_op jit(solution)/shard_map/image/pallas_call | solution.py:509
  32.5 1.1 %collective-permute-start = (f32[16,1024]{1,0:T(8,128)S(1)}, f32[16,1024]{1,0:T(8,128)S(1)}, u32[]{:S(2)}, u32[]{:S(2)}) collective-permute-start(f32[16,1024]{1,0:T(8,128)S(1)} %get-tuple-element.7), channel_id=1, source_target_pairs={{0,16},{16,0},{1,17},{17,1},{2,18},{18,2},{3,19},{19,3},{4,20},{20... | collective-permute-start | bytes 196616 | tf_op jit(solution)/shard_map/ppermute | solution.py:531
  33.6 3.3 %collective-permute-done.got_ref = f32[16,1024]{1,0:T(8,128)S(1)} collective-permute-done((f32[16,1024]{1,0:T(8,128)S(1)}, f32[16,1024]{1,0:T(8,128)S(1)}, u32[]{:S(2)}, u32[]{:S(2)}) %collective-permute-start) | collective-permute-done | bytes 65568 | tf_op jit(solution)/shard_map/ppermute | solution.py:531
  36.9 0.7 %finish.1 = (f32[16,2048]{1,0:T(8,128)}, f32[1,2048]{1,0:T(1,128)}) custom-call(f32[16,1024]{1,0:T(8,128)S(1)} %get-tuple-element.6.keep_ref, f32[16,1024]{1,0:T(8,128)S(1)} %collective-permute-done.got_ref), custom_call_target="tpu_custom_call" | custom-call | tf_op jit(solution)/shard_map/finish/pallas_call | solution.py:532
Async XLA Ops:
  3.4 19.0 %all-to-all-start = ((bf16[32,40,128]{2,1,0:T(8,128)(2,1)}), bf16[32,40,128]{2,1,0:T(8,128)(2,1)S(1)}, u32[]{:S(2)}, u32[]{:S(2)}) async-start(bf16[32,40,128]{2,1,0:T(8,128)(2,1)} %send.1), calls=%async_computation | async-start | bytes 655360 | tf_op jit(solution)/shard_map/all_to_all | solution.py:468
  32.5 4.3 %collective-permute-start = (f32[16,1024]{1,0:T(8,128)S(1)}, f32[16,1024]{1,0:T(8,128)S(1)}, u32[]{:S(2)}, u32[]{:S(2)}) collective-permute-start(f32[16,1024]{1,0:T(8,128)S(1)} %get-tuple-element.7), channel_id=1, source_target_pairs={{0,16},{16,0},{1,17},{17,1},{2,18},{18,2},{3,19},{19,3},{4,20},{20... | collective-permute-start | bytes 196616 | tf_op jit(solution)/shard_map/ppermute | solution.py:531

commit v10 on v8

--- a/solution.py
+++ b/solution.py
@@ -48,10 +48,10 @@
     return 1.0 - versine, sine
 
 
-def bins_column(bins_ref):
+def bins_column(row):
     rows = lax.broadcasted_iota(jnp.int32, (NF, NF), 0)
     lanes = lax.broadcasted_iota(jnp.int32, (NF, NF), 1)
-    square = jnp.broadcast_to(bins_ref[...].astype(jnp.float32), (NF, NF))
+    square = jnp.broadcast_to(row, (NF, NF))
     return jnp.sum(jnp.where(rows == lanes, square, 0.0), axis=1, keepdims=True)
 
 
@@ -72,11 +72,10 @@
 
 
 def send_kernel(nodes, bins_hbm, traces_hbm, corr_hbm, out_ref, bins_ref, traces_ref, sems):
-    devices, height, _ = out_ref.shape
+    peers, height, _ = out_ref.shape
     stations_dev, half_length = traces_ref.shape
     pieces = (height - 8) // stations_dev
     windows, groups, cores = (lax.axis_size(a) for a in ("win", "sta", "freq"))
-    place = lax.axis_index("win") * cores + lax.axis_index("freq")
     small = start_all(
         [
             pltpu.make_async_copy(bins_hbm, bins_ref, sems.at[0]),
@@ -84,18 +83,17 @@
         ]
     )
     copies = []
-    for dev in range(devices):
-        win, sta, core = dev // (groups * cores), dev // cores % groups, dev % cores
-        first = ((sta * cores + core) * windows + win) * nodes
+    for peer in range(peers):
+        first = ((peer % groups * cores + lax.axis_index("freq")) * windows + peer // groups) * nodes
         for piece in range(pieces):
-            at = pl.multiple_of(first + (place * pieces + piece) * LANES, LANES)
-            to = out_ref.at[dev, pl.ds(piece * stations_dev, stations_dev), :]
-            sem = sems.at[2 + dev * pieces + piece]
+            at = pl.multiple_of(first + (lax.axis_index("win") * pieces + piece) * LANES, LANES)
+            to = out_ref.at[peer, pl.ds(piece * stations_dev, stations_dev), :]
+            sem = sems.at[2 + peer * pieces + piece]
             copies.append(pltpu.make_async_copy(corr_hbm.at[:, pl.ds(at, LANES)], to, sem))
     start_all(copies)
     start = lax.axis_index("freq") * half_length
     small[0].wait()
-    bins = bins_column(bins_ref)
+    bins = bins_column(bins_ref[...].astype(jnp.float32))
     pos = (start + lax.broadcasted_iota(jnp.int32, (NF, half_length), 1)).astype(jnp.float32)
     product = bins * pos
     turns = jnp.round(product * (1.0 / NT))
@@ -112,8 +110,8 @@
     terms = [term.astype(jnp.float32) for term in split_bf16(sums, 2)]
     tile = jnp.concatenate([term[at : at + 8] for term in terms for at in range(0, stations_dev, 8)], axis=1)
     tile = tile.astype(jnp.bfloat16)
-    for dev in range(devices):
-        out_ref[dev, height - 8 :, :] = tile
+    for peer in range(peers):
+        out_ref[peer, height - 8 :, :] = tile
     for copy in copies:
         copy.wait()
 
@@ -123,7 +121,7 @@
     return (lax.axis_index("sta") * cores + lax.axis_index("freq")) * windows + lax.axis_index("win")
 
 
-def pick_columns(ids_ref, tables_ref, table_copies, nodes, left_ref, right_ref):
+def pick_columns(ids_ref, tables_ref, table_copies, nodes, left_ref, right_ref, beside):
     ntab, grid = tables_ref.shape
     count = nodes // LANES
     wide = right_ref.shape[0] // 3
@@ -142,6 +140,8 @@
         for block in range(at * step, (at + 1) * step):
             pieces = split_bf16(tables_ref[:, block * wide : (block + 1) * wide], 3)
             left_ref[block * ntab : (block + 1) * ntab, :] = jnp.concatenate(pieces, axis=1)
+        if at < len(beside):
+            beside[at]()
         rows = left_ref[at * step * ntab : (at + 1) * step * ntab, :]
         picked = jnp.dot(rows, right_ref[...], preferred_element_type=jnp.float32)
         for block in range(step):
@@ -168,7 +168,7 @@
     return dot(even, cosine) + dot(odd, sine)
 
 
-def station_plan(table_row, width):
+def station_plan(table_row, bins_row, width):
     count = table_row.shape[1]
     shape = (count, count)
     here = lax.broadcasted_iota(jnp.int32, shape, 0)
@@ -201,20 +201,18 @@
     rows = [first, last, length, jnp.broadcast_to(groups, (1, width))]
     if width > count:
         place_row = jnp.concatenate([place_row, jnp.zeros((1, width - count), jnp.int32)], axis=1)
-    rows += [place_row, jnp.zeros((3, width), jnp.int32)]
+    bins_row = jnp.concatenate([bins_row, jnp.zeros((1, width - NF), jnp.int32)], axis=1)
+    rows += [place_row, bins_row, jnp.zeros((2, width), jnp.int32)]
     return jnp.concatenate(rows, axis=0).astype(jnp.float32)
 
 
-def packed_rows(ntab):
-    ends = [ntab * NF, 2 * ntab * NF, 2 * ntab * NF + DEGREES, 2 * ntab * NF + DEGREES + 8]
-    return [slice(start, end) for start, end in zip([0] + ends, ends)]
+TURNS_AT, COEF_AT, PLAN_AT, PACKED_ROWS = slice(0, NTAB), slice(16, 48), slice(48, 56), 640
 
 
 def prepare_kernel(bins_hbm, table_hbm, ids_hbm, tables_hbm, out_hbm, *rest):
-    bins_ref, table_ref, ids_ref, tables_ref, cos_ref, sin_ref, coef_ref, plan_ref = rest[:8]
-    left_ref, right_ref, sems, table_sems = rest[8:]
-    ntab = tables_ref.shape[0]
-    nodes = cos_ref.shape[1]
+    bins_ref, table_ref, ids_ref, tables_ref, turns_ref, coef_ref, plan_ref = rest[:7]
+    left_ref, right_ref, sems, table_sems = rest[7:]
+    nodes = turns_ref.shape[1]
     near = ids_ref.shape[0]
     first = pl.multiple_of(own_place() * (nodes // LANES) // near * near, 8)
     ins = start_all(
@@ -232,67 +230,50 @@
     start_all(table_copies)
     for copy in ins:
         copy.wait()
-    cos_at, sin_at, coef_at, plan_at = packed_rows(ntab)
-    coef_ref[...] = chebyshev_coefs(bins_ref)
-    plan_ref[...] = station_plan(table_ref[...], plan_ref.shape[1])
+
+    def make_coefs():
+        coef_ref[...] = chebyshev_coefs(bins_ref)
+
+    def make_plan():
+        plan_ref[...] = station_plan(table_ref[...], bins_ref[...], plan_ref.shape[1])
+
+    beside = [make_coefs, make_plan]
+    turns_ref[...] = pick_columns(ids_ref, tables_ref, table_copies, nodes, left_ref, right_ref, beside) * (1.0 / 256.0)
     outs = start_all(
         [
-            pltpu.make_async_copy(coef_ref, out_hbm.at[coef_at, pl.ds(0, LANES)], sems.at[0]),
-            pltpu.make_async_copy(plan_ref, out_hbm.at[plan_at, pl.ds(0, plan_ref.shape[1])], sems.at[1]),
+            pltpu.make_async_copy(coef_ref, out_hbm.at[COEF_AT, pl.ds(0, LANES)], sems.at[0]),
+            pltpu.make_async_copy(plan_ref, out_hbm.at[PLAN_AT, pl.ds(0, plan_ref.shape[1])], sems.at[1]),
+            pltpu.make_async_copy(turns_ref, out_hbm.at[TURNS_AT, pl.ds(0, nodes)], sems.at[2]),
         ]
     )
-    turns = pick_columns(ids_ref, tables_ref, table_copies, nodes, left_ref, right_ref) * (1.0 / 256.0)
-    bins = bins_column(bins_ref)
-    for table in range(ntab):
-        cosine, sine = cos_sin(bins * turns[table : table + 1])
-        at = pl.ds(table * NF, NF)
-        cos_ref[at, :] = cosine
-        sin_ref[at, :] = sine
-        outs += start_all(
-            [
-                pltpu.make_async_copy(
-                    cos_ref.at[at, :], out_hbm.at[pl.ds(cos_at.start + table * NF, NF), pl.ds(0, nodes)],
-                    sems.at[3 + 2 * table],
-                ),
-                pltpu.make_async_copy(
-                    sin_ref.at[at, :], out_hbm.at[pl.ds(sin_at.start + table * NF, NF), pl.ds(0, nodes)],
-                    sems.at[4 + 2 * table],
-                ),
-            ]
-        )
     for copy in outs:
         copy.wait()
 
 
-def image_kernel(merged, stations_dev, packed_hbm, block_ref, *rest):
+def image_kernel(merged, stations_dev, packed_hbm, other_ref, block_ref, *rest):
     corr_ref, rest = (None, rest) if merged else (rest[0], rest[1:])
-    keep_ref, send_ref, plan_ref, place_of_ref, coef_ref, cos_ref, sin_ref, sems = rest[:8]
-    place_ref, weight_ref, left_ref, sums_ref, basis_a, basis_b = rest[8:]
+    keep_ref, send_ref, plan_ref, place_of_ref, coef_ref, turns_ref, cos_ref, sin_ref, sems = rest[:9]
+    place_ref, weight_ref, left_ref, sums_ref, basis_a, basis_b = rest[9:]
     places, nodes = place_ref.shape
-    windows, groups, cores = (lax.axis_size(a) for a in ("win", "sta", "freq"))
+    windows, groups = lax.axis_size("win"), lax.axis_size("sta")
     stations = stations_dev * groups
-    cos_at, sin_at, coef_at, plan_at = packed_rows(cos_ref.shape[0] // NF)
     width = plan_ref.shape[1]
     copies = start_all(
         [
-            pltpu.make_async_copy(packed_hbm.at[plan_at, pl.ds(0, width)], place_of_ref, sems.at[0]),
-            pltpu.make_async_copy(packed_hbm.at[plan_at, pl.ds(0, width)], plan_ref, sems.at[1]),
-            pltpu.make_async_copy(packed_hbm.at[coef_at, pl.ds(0, LANES)], coef_ref, sems.at[2]),
-            pltpu.make_async_copy(packed_hbm.at[cos_at, pl.ds(0, nodes)], cos_ref, sems.at[3]),
-            pltpu.make_async_copy(packed_hbm.at[sin_at, pl.ds(0, nodes)], sin_ref, sems.at[4]),
+            pltpu.make_async_copy(packed_hbm.at[PLAN_AT, pl.ds(0, width)], place_of_ref, sems.at[0]),
+            pltpu.make_async_copy(packed_hbm.at[TURNS_AT, pl.ds(0, nodes)], turns_ref, sems.at[1]),
+            pltpu.make_async_copy(packed_hbm.at[COEF_AT, pl.ds(0, LANES)], coef_ref, sems.at[2]),
+            pltpu.make_async_copy(packed_hbm.at[PLAN_AT, pl.ds(0, width)], plan_ref, sems.at[3]),
         ]
     )
     height = block_ref.shape[1]
-    rows_of = lambda win, core: [(win * groups + group) * cores + core for group in range(groups)]
 
     even, odd = [], []
     for win in range(windows):
         value = []
         for group in range(groups):
-            tile = None
-            for core in range(cores):
-                part = block_ref[(win * groups + group) * cores + core, height - 8 :, :].astype(jnp.float32)
-                tile = part if tile is None else tile + part
+            at = win * groups + group
+            tile = block_ref[at, height - 8 :, :].astype(jnp.float32) + other_ref[at].astype(jnp.float32)
             tile = tile[:, : LANES // 2] + tile[:, LANES // 2 :]
             value += [tile[:, 2 * NF * piece : 2 * NF * (piece + 1)] for piece in range(stations_dev // 8)]
         value = jnp.concatenate(value, axis=0)
@@ -302,10 +283,9 @@
     if merged:
         parts = []
         for win in range(windows):
-            for core in range(cores):
-                for first in range(0, height - 8, stations_dev):
-                    rows = [block_ref[at, first : first + stations_dev, :] for at in rows_of(win, core)]
-                    parts.append(jnp.concatenate(rows, axis=0))
+            for first in range(0, height - 8, stations_dev):
+                rows = slice(first, first + stations_dev)
+                parts.append(jnp.concatenate([block_ref[win * groups + at, rows, :] for at in range(groups)], axis=0))
         corr = jnp.concatenate(parts, axis=1)
     else:
         corr = corr_ref[...]
@@ -324,8 +304,14 @@
     chunk = min(256, nodes)
     depth = DEGREES * 8
     lanes = windows * 2 * NF
-    for copy in copies[1:3]:
+    for copy in copies[1:]:
         copy.wait()
+
+    bins = bins_column(place_of_ref[5:6, :NF])
+    for table in range(NTAB):
+        cosine, sine = cos_sin(bins * turns_ref[table : table + 1, :])
+        cos_ref[table * NF : (table + 1) * NF, :] = cosine
+        sin_ref[table * NF : (table + 1) * NF, :] = sine
 
     def make_left(pair):
         top = weight_ref[pl.ds(pl.multiple_of(pair * 16, 16), 8), :]
@@ -408,8 +394,6 @@
         run(steps)
 
     run(basis_steps(0, basis_a))
-    for copy in copies[3:]:
-        copy.wait()
 
     def body(pair, carry):
         group = pair * 2
@@ -452,26 +436,27 @@
     bins = freq_bins.reshape(1, NF)
     bins_scratch = pltpu.VMEM((1, NF), jnp.int32)
 
-    holders = windows * cores
-    merged = nodes % (holders * LANES) == 0
-    pieces = nodes // (holders * LANES) if merged else 0
+    peers = windows * groups
+    merged = nodes % (windows * LANES) == 0
+    pieces = nodes // (windows * LANES) if merged else 0
     height = pieces * stations_dev + 8
     blocks = pl.pallas_call(
         functools.partial(send_kernel, nodes),
-        out_shape=jax.ShapeDtypeStruct((devices, height, LANES), jnp.bfloat16),
+        out_shape=jax.ShapeDtypeStruct((peers, height, LANES), jnp.bfloat16),
         in_specs=[hbm] * 3,
         out_specs=vmem,
         scratch_shapes=[
             bins_scratch,
             pltpu.VMEM(traces.shape, traces.dtype),
-            pltpu.SemaphoreType.DMA((2 + devices * max(pieces, 1),)),
+            pltpu.SemaphoreType.DMA((2 + peers * max(pieces, 1),)),
         ],
         compiler_params=params(0),
         name="send",
     )(bins, traces, corrections)
-    received = [lax.all_to_all(blocks, ("win", "sta", "freq"), split_axis=0, concat_axis=0, tiled=True)]
+    received = [lax.all_to_all(blocks, ("win", "sta"), split_axis=0, concat_axis=0, tiled=True)]
+    other = lax.ppermute(received[0][:, height - 8 :, :], "freq", [(0, 1), (1, 0)])
     if not merged:
-        parts = corrections.reshape(stations_dev, groups, holders, nodes)
+        parts = corrections.reshape(stations_dev, groups, cores * windows, nodes)
         place = lax.axis_index("freq") * windows + lax.axis_index("win")
         mine = lax.dynamic_index_in_dim(parts, place, axis=2, keepdims=False)
         corr = lax.all_to_all(mine.transpose(1, 0, 2), "sta", split_axis=0, concat_axis=0, tiled=True)
@@ -479,10 +464,11 @@
 
     wide = 512
     plan_width = max(LANES, stations)
+    turns = pltpu.VMEM((ntab, nodes), jnp.float32)
     phasors = pltpu.VMEM((ntab * NF, nodes), jnp.float32)
     coefs = pltpu.VMEM((DEGREES, LANES), jnp.float32)
     plan = pltpu.VMEM((8, plan_width), jnp.float32)
-    packed_shape = (packed_rows(ntab)[-1].stop, max(nodes, plan_width))
+    packed_shape = (PACKED_ROWS, max(nodes, plan_width))
     packed = pl.pallas_call(
         prepare_kernel,
         out_shape=jax.ShapeDtypeStruct(packed_shape, jnp.float32),
@@ -493,13 +479,12 @@
             pltpu.VMEM((1, stations), jnp.int32),
             pltpu.VMEM((max(nodes // LANES, 8), LANES), jnp.int32),
             pltpu.VMEM(tables.shape, tables.dtype),
-            phasors,
-            phasors,
+            turns,
             coefs,
             plan,
             pltpu.VMEM((grid // wide * ntab, 3 * wide), jnp.bfloat16),
             pltpu.VMEM((3 * wide, nodes), jnp.bfloat16),
-            pltpu.SemaphoreType.DMA((3 + 2 * ntab,)),
+            pltpu.SemaphoreType.DMA((3,)),
             pltpu.SemaphoreType.DMA((TABLE_PIECES,)),
         ],
         compiler_params=params(512 * 1024),
@@ -513,15 +498,16 @@
     keep, send = pl.pallas_call(
         functools.partial(image_kernel, merged, stations_dev),
         out_shape=[half, half],
-        in_specs=[hbm] + [vmem] * len(received),
+        in_specs=[hbm] + [vmem] * (1 + len(received)),
         out_specs=[vmem, vmem],
         scratch_shapes=[
             pltpu.SMEM((8, plan_width), jnp.float32),
             plan,
             coefs,
+            turns,
             phasors,
             phasors,
-            pltpu.SemaphoreType.DMA((5,)),
+            pltpu.SemaphoreType.DMA((4,)),
             pltpu.VMEM((places, nodes), jnp.float32),
             pltpu.VMEM((places, rows), jnp.float32),
             pltpu.VMEM((places // 8, rows, DEGREES * 8), jnp.bfloat16),
@@ -531,7 +517,7 @@
         ],
         compiler_params=params(23 * 512 * 1024),
         name="image",
-    )(packed, *received)
+    )(packed, other, *received)
     got = lax.ppermute(send, "win", [(0, 1), (1, 0)])
     spectrum, beam_power = pl.pallas_call(
         functools.partial(finish_kernel, stations),

time: 37.1 us -> 44.1 us (1.19); the launches traced: 36.8 us -> 44.3 us
  blocking collectives: 0 us -> 19 us
  starting transfers between devices: 8.37 us -> 1.05 us
  waiting for transfers between devices: 7.07 us -> 3.58 us
  Pallas kernels: 20.7 us -> 20 us
    all_to_all x0 -> x1, blocking collectives: none -> 19 us  [on_device(): lax.all_to_all(blocks, ('win', 'sta'), split_axis=0, concat_axis=0, tiled...]
    all_to_all x1 -> x0, starting transfers between devices: 7.3 us -> none  [on_device(): lax.all_to_all(blocks, ('win', 'sta', 'freq'), split_axis=0, concat_axis=...]
    all_to_all x1 -> x0, waiting for transfers between devices: 3.81 us -> none  [on_device(): lax.all_to_all(blocks, ('win', 'sta', 'freq'), split_axis=0, concat_axis=...]
    pallas_call x1, Pallas kernels: 7.88 us -> 6.4 us  [on_device(): pl.pallas_call(prepare_kernel, out_shape=jax.ShapeDtypeStruct(packed_shap...]
    pallas_call x1, Pallas kernels: 9.38 us -> 10.2 us  [on_device(): pl.pallas_call(functools.partial(image_kernel, merged, stations_dev), out...]
  transfers between devices with their start and end apart: 2 -> 2, of which waited for: 2 -> 1; matrix products, arithmetic and copies ran while one was open for 0% -> 0% of each run, Pallas kernels for 21% -> 14%
where the time goes in v10:
time: 44.1 us; the launch traced here: 44.3 us
  Pallas kernels  20 us (45%)
  blocking collectives  19 us (43%)
  waiting for transfers between devices  3.58 us (8%)
  starting transfers between devices  1.05 us (2%)
  between operations  0.66 us (1%)
    all_to_all x1, blocking collectives, on_device(): lax.all_to_all(blocks, ('win', 'sta'), split_axis=0, concat_axis=0, tiled...  19 us
    pallas_call x1, Pallas kernels, on_device(): pl.pallas_call(functools.partial(image_kernel, merged, stations_dev), out...  10.2 us
    pallas_call x1, Pallas kernels, on_device(): pl.pallas_call(prepare_kernel, out_shape=jax.ShapeDtypeStruct(packed_shap...  6.4 us
    ppermute x1, waiting for transfers between devices, on_device(): got = lax.ppermute(send, 'win', [(0, 1), (1, 0)])  3.58 us
    pallas_call x1, Pallas kernels, on_device(): pl.pallas_call(functools.partial(send_kernel, nodes), out_shape=jax.Shape...  2.72 us
    ppermute x1, starting transfers between devices, on_device(): got = lax.ppermute(send, 'win', [(0, 1), (1, 0)])  1.05 us
  transfers between devices with their start and end apart: 2, of which 1 were waited for; matrix products, arithmetic and copies ran while one was open for 0% of the time, Pallas kernels for 14%

profile of v10, /device:TPU:0, one launch (start us, length us, event | category | flops | bytes accessed | tf_op | source)
XLA Modules:
  0.0 44.3 jit_solution(17230031564344106452)
XLA Ops:
  0.6 2.7 %send.1 = bf16[16,72,128]{2,1,0:T(8,128)(2,1)} custom-call(s32[1,16]{1,0:T(1,128)} %bitcast.5, bf16[16,2560]{1,0:T(8,128)(2,1)} %traces_hbm.1, bf16[16,32768]{1,0:T(8,128)(2,1)} %corr_hbm.1), custom_call_target="tpu_custom_call" | custom-call | tf_op jit(solution)/shard_map/send/pallas_call | solution.py:443
  3.4 19.0 %all_to_all.5.block_ref = bf16[16,72,128]{2,1,0:T(8,128)(2,1)S(1)} all-to-all(bf16[16,72,128]{2,1,0:T(8,128)(2,1)} %send.1), channel_id=1, replica_groups=mesh['win'=2,'sta'=8,'freq'=2] {'win','sta'}, dimensions={0} | all-to-all | bytes 589824 | tf_op jit(solution)/shard_map/all_to_all | solution.py:456
  22.4 0.0 collective-permute-start
  22.4 6.4 %prepare.1.packed_hbm = f32[640,1024]{1,0:T(8,128)} custom-call(s32[1,16]{1,0:T(1,128)} %bitcast.6, s32[1,128]{1,0:T(1,128)} %bitcast.7, s32[256,128]{1,0:T(8,128)} %bitcast.4, f32[16,32768]{1,0:T(8,128)} %tables_hbm.1), custom_call_target="tpu_custom_call" | custom-call | tf_op jit(solution)/shard_map/prepare/pallas_call | solution.py:472
  28.8 0.0 collective-permute-done.other_ref
  28.8 10.2 %image.1 = (f32[16,1024]{1,0:T(8,128)S(1)}, f32[16,1024]{1,0:T(8,128)S(1)}) custom-call(f32[640,1024]{1,0:T(8,128)} %prepare.1.packed_hbm, bf16[16,8,128]{2,1,0:T(8,128)(2,1)S(1)} %collective-permute-done.other_ref, bf16[16,72,128]{2,1,0:T(8,128)(2,1)S(1)} %all_to_all.5.block_ref), custom_call_target="tpu_custom_call" | custom-call | tf_op jit(solution)/shard_map/image/pallas_call | solution.py:498
  39.0 1.0 %collective-permute-start.1 = (f32[16,1024]{1,0:T(8,128)S(1)}, f32[16,1024]{1,0:T(8,128)S(1)}, u32[]{:S(2)}, u32[]{:S(2)}) collective-permute-start(f32[16,1024]{1,0:T(8,128)S(1)} %get-tuple-element.7), channel_id=1, source_target_pairs={{0,16},{16,0},{1,17},{17,1},{2,18},{18,2},{3,19},{19,3},{4,20},{20... | collective-permute-start | bytes 196616 | tf_op jit(solution)/shard_map/ppermute | solution.py:521
  40.0 3.6 %collective-permute-done.1.got_ref = f32[16,1024]{1,0:T(8,128)S(1)} collective-permute-done((f32[16,1024]{1,0:T(8,128)S(1)}, f32[16,1024]{1,0:T(8,128)S(1)}, u32[]{:S(2)}, u32[]{:S(2)}) %collective-permute-start.1) | collective-permute-done | bytes 65568 | tf_op jit(solution)/shard_map/ppermute | solution.py:521
  43.6 0.7 %finish.1 = (f32[16,2048]{1,0:T(8,128)}, f32[1,2048]{1,0:T(1,128)}) custom-call(f32[16,1024]{1,0:T(8,128)S(1)} %get-tuple-element.6.keep_ref, f32[16,1024]{1,0:T(8,128)S(1)} %collective-permute-done.1.got_ref), custom_call_target="tpu_custom_call" | custom-call | tf_op jit(solution)/shard_map/finish/pallas_call | solution.py:522
  (1 shorter events, 0.0 us)
Async XLA Ops:
  22.4 6.4 %collective-permute-start = (bf16[16,8,128]{2,1,0:T(8,128)(2,1)S(1)}, bf16[16,8,128]{2,1,0:T(8,128)(2,1)S(1)}, u32[]{:S(2)}, u32[]{:S(2)}) collective-permute-start(bf16[16,8,128]{2,1,0:T(8,128)(2,1)S(1)} %slice.4), channel_id=1, source_target_pairs={{0,1},{1,0},{2,3},{3,2},{4,5},{5,4},{6,7},{7,6},{8,9},{9,8},{10,11... | collective-permute-start | bytes 98312 | tf_op jit(solution)/shard_map/ppermute | solution.py:457
  39.0 4.6 %collective-permute-start.1 = (f32[16,1024]{1,0:T(8,128)S(1)}, f32[16,1024]{1,0:T(8,128)S(1)}, u32[]{:S(2)}, u32[]{:S(2)}) collective-permute-start(f32[16,1024]{1,0:T(8,128)S(1)} %get-tuple-element.7), channel_id=1, source_target_pairs={{0,16},{16,0},{1,17},{17,1},{2,18},{18,2},{3,19},{19,3},{4,20},{20... | collective-permute-start | bytes 196616 | tf_op jit(solution)/shard_map/ppermute | solution.py:521

commit v11 on v9

--- a/solution.py
+++ b/solution.py
@@ -267,7 +267,7 @@
 def image_kernel(merged, stations_dev, packed_hbm, block_ref, *rest):
     corr_ref, rest = (None, rest) if merged else (rest[0], rest[1:])
     keep_ref, send_ref, plan_ref, place_of_ref, coef_ref, cos_ref, sin_ref, sems = rest[:8]
-    place_ref, weight_ref, left_ref, sums_ref, basis_a, basis_b = rest[8:]
+    place_ref, weight_ref, left_ref, sums_ref, basis_a, basis_b, got_a, got_b = rest[8:]
     places, nodes = place_ref.shape
     windows, groups, cores = (lax.axis_size(a) for a in ("win", "sta", "freq"))
     stations = stations_dev * groups
@@ -321,7 +321,7 @@
     weight_ref[...] = found
     place_ref[...] = jnp.dot(sorter, corr, preferred_element_type=jnp.float32) * (1.0 / REACH)
     sums_ref[...] = jnp.zeros_like(sums_ref)
-    chunk = nodes
+    chunk = min(256, nodes)
     depth = DEGREES * 8
     lanes = windows * 2 * NF
     for copy in copies[1:3]:
@@ -364,56 +364,59 @@
         low = jnp.concatenate([result[lanes:] for result in results], axis=0)
         return jnp.concatenate([high, high, low], axis=1)
 
-    def basis_steps(group, basis_ref):
-        arg = place_ref[pl.ds(pl.multiple_of(group * 8, 8), 8), :]
+    def make_basis(group, basis_ref, at):
+        arg = place_ref[pl.ds(pl.multiple_of(group * 8, 8), 8), at]
         twice = arg + arg
         before, now = jnp.ones_like(arg), arg
         for degree in range(0, DEGREES, 2):
-            pair = jnp.concatenate([before, now], axis=0)
-            high, low = split_bf16(pair, 2)
-            basis_ref[degree * 8 : degree * 8 + 16, :] = high
-            basis_ref[depth + degree * 8 : depth + degree * 8 + 16, :] = low
+            high, low = split_bf16(jnp.concatenate([before, now], axis=0), 2)
+            basis_ref[degree * 8 : degree * 8 + 16, at] = high
+            basis_ref[depth + degree * 8 : depth + degree * 8 + 16, at] = low
             before = twice * now - before
             now = twice * before - now
-            if degree % 8 == 6:
-                yield
-
-    def run(steps):
-        for _ in steps:
-            pass
-
-    def add_group(group, basis_ref, steps):
+
+    def phasor_rows(group):
+        tables = [plan_ref[slot, group].astype(jnp.int32) for slot in range(2)]
+        return [pl.ds(pl.multiple_of(table * NF, NF), NF) for table in tables]
+
+    def add_product(rows_of_slot, got_ref, at):
+        for win in range(windows):
+            row = win * 2 * NF
+            real_sum, imag_sum = sums_ref[row : row + NF, at], sums_ref[row + NF : row + 2 * NF, at]
+            for slot, rows in enumerate(rows_of_slot):
+                cosine, sine = cos_ref[rows, at], sin_ref[rows, at]
+                real = got_ref[slot * lanes + row : slot * lanes + row + NF, at]
+                imag = got_ref[slot * lanes + row + NF : slot * lanes + row + 2 * NF, at]
+                real_sum += real * cosine - imag * sine
+                imag_sum += real * sine + imag * cosine
+            sums_ref[row : row + NF, at], sums_ref[row + NF : row + 2 * NF, at] = real_sum, imag_sum
+
+    chunks = [slice(first, first + chunk) for first in range(0, nodes, chunk)]
+
+    def stage(group, basis_ref, next_basis, got_ref, last_got):
         left = left_of(group)
-        tables = [plan_ref[slot, group].astype(jnp.int32) for slot in range(2)]
-        phasor_rows = [pl.ds(pl.multiple_of(table * NF, NF), NF) for table in tables]
-        for first in range(0, nodes, chunk):
-            at = slice(first, first + chunk)
+        rows_of_slot = phasor_rows(jnp.maximum(group - 1, 0))
+        for at in chunks:
             right = jnp.concatenate([basis_ref[:, at], basis_ref[:depth, at]], axis=0)
-            got = jnp.dot(left, right, preferred_element_type=jnp.float32)
-            run(steps)
-            for win in range(windows):
-                row = win * 2 * NF
-                real_sum, imag_sum = sums_ref[row : row + NF, at], sums_ref[row + NF : row + 2 * NF, at]
-                for slot, rows in enumerate(phasor_rows):
-                    cosine, sine = cos_ref[rows, at], sin_ref[rows, at]
-                    real = got[slot * lanes + row : slot * lanes + row + NF]
-                    imag = got[slot * lanes + row + NF : slot * lanes + row + 2 * NF]
-                    real_sum += real * cosine - imag * sine
-                    imag_sum += real * sine + imag * cosine
-                sums_ref[row : row + NF, at], sums_ref[row + NF : row + 2 * NF, at] = real_sum, imag_sum
-        run(steps)
-
-    run(basis_steps(0, basis_a))
+            got_ref[:, at] = jnp.dot(left, right, preferred_element_type=jnp.float32)
+            make_basis(group + 1, next_basis, at)
+            add_product(rows_of_slot, last_got, at)
+
+    got_b[...] = jnp.zeros_like(got_b)
+    for at in chunks:
+        make_basis(0, basis_a, at)
     for copy in copies[3:]:
         copy.wait()
 
     def body(pair, carry):
-        group = pair * 2
-        add_group(group, basis_a, basis_steps(group + 1, basis_b))
-        add_group(group + 1, basis_b, basis_steps(jnp.minimum(group + 2, places // 8 - 1), basis_a))
+        stage(pair * 2, basis_a, basis_b, got_a, got_b)
+        stage(pair * 2 + 1, basis_b, basis_a, got_b, got_a)
         return carry
 
-    lax.fori_loop(0, (used + 1) // 2, body, 0)
+    turns = (used + 1) // 2
+    lax.fori_loop(0, turns, body, 0)
+    for at in chunks:
+        add_product(phasor_rows(turns * 2 - 1), got_b, at)
     powers = []
     for win in range(windows):
         row = win * 2 * NF
@@ -502,7 +505,7 @@
         name="prepare",
     )(bins, station_table.reshape(1, stations), node_ids.reshape(grid // LANES, LANES), tables)
 
-    places = (stations // 8 + ntab // 2 + 2) // 2 * 16
+    places = (stations // 8 + ntab // 2 + 3) // 2 * 16
     half = jax.ShapeDtypeStruct((NF, nodes), jnp.float32)
     rows = 2 * windows * 2 * NF
     basis = pltpu.VMEM((2 * DEGREES * 8, nodes), jnp.bfloat16)
@@ -524,6 +527,8 @@
             pltpu.VMEM((rows // 2, nodes), jnp.float32),
             basis,
             basis,
+            pltpu.VMEM((rows, nodes), jnp.float32),
+            pltpu.VMEM((rows, nodes), jnp.float32),
         ],
         compiler_params=params(23 * 512 * 1024),
         name="image",

time: 37.8 us -> 37.3 us (0.987)
  Pallas kernels: 21.5 us -> 20.9 us
    pallas_call x1, Pallas kernels: 10.1 us -> 9.59 us  [on_device(): pl.pallas_call(functools.partial(image_kernel, merged, stations_dev), out...]
where the time goes in v11:
time: 37.3 us; the launch traced here: 37 us
  Pallas kernels  20.9 us (56%)
  starting transfers between devices  8.37 us (22%)
  waiting for transfers between devices  7.08 us (19%)
  between operations  0.66 us (2%)
    pallas_call x1, Pallas kernels, on_device(): pl.pallas_call(functools.partial(image_kernel, merged, stations_dev), out...  9.59 us
    pallas_call x1, Pallas kernels, on_device(): pl.pallas_call(prepare_kernel, out_shape=jax.ShapeDtypeStruct(packed_shap...  7.88 us
    all_to_all x1, starting transfers between devices, on_device(): lax.all_to_all(blocks, ('win', 'sta', 'freq'), split_axis=0, concat_axis=...  7.3 us
    all_to_all x1, waiting for transfers between devices, on_device(): lax.all_to_all(blocks, ('win', 'sta', 'freq'), split_axis=0, concat_axis=...  3.81 us
    ppermute x1, waiting for transfers between devices, on_device(): got = lax.ppermute(send, 'win', [(0, 1), (1, 0)])  3.27 us
    pallas_call x1, Pallas kernels, on_device(): pl.pallas_call(functools.partial(send_kernel, nodes), out_shape=jax.Shape...  2.74 us
    ppermute x1, starting transfers between devices, on_device(): got = lax.ppermute(send, 'win', [(0, 1), (1, 0)])  1.06 us
  transfers between devices with their start and end apart: 2, of which 2 were waited for; matrix products, arithmetic and copies ran while one was open for 0% of the time, Pallas kernels for 21%

profile of v11, /device:TPU:0, one launch (start us, length us, event | category | flops | bytes accessed | tf_op | source)
XLA Modules:
  0.0 37.0 jit_solution(10454471361378963602)
XLA Ops:
  0.6 2.7 %send.1 = bf16[32,40,128]{2,1,0:T(8,128)(2,1)} custom-call(s32[1,16]{1,0:T(1,128)} %bitcast.5, bf16[16,2560]{1,0:T(8,128)(2,1)} %traces_hbm.1, bf16[16,32768]{1,0:T(8,128)(2,1)} %corr_hbm.1), custom_call_target="tpu_custom_call" | custom-call | tf_op jit(solution)/shard_map/send/pallas_call | solution.py:458
  3.4 7.3 %all-to-all-start = ((bf16[32,40,128]{2,1,0:T(8,128)(2,1)}), bf16[32,40,128]{2,1,0:T(8,128)(2,1)S(1)}, u32[]{:S(2)}, u32[]{:S(2)}) async-start(bf16[32,40,128]{2,1,0:T(8,128)(2,1)} %send.1), calls=%async_computation | async-start | bytes 655360 | tf_op jit(solution)/shard_map/all_to_all | solution.py:471
  10.7 7.9 %prepare.1.packed_hbm = f32[552,1024]{1,0:T(8,128)} custom-call(s32[1,16]{1,0:T(1,128)} %bitcast.6, s32[1,128]{1,0:T(1,128)} %bitcast.7, s32[256,128]{1,0:T(8,128)} %bitcast.4, f32[16,32768]{1,0:T(8,128)} %tables_hbm.1), custom_call_target="tpu_custom_call" | custom-call | tf_op jit(solution)/shard_map/prepare/pallas_call | solution.py:485
  18.6 3.8 %all-to-all-done.block_ref = bf16[32,40,128]{2,1,0:T(8,128)(2,1)S(1)} async-done(((bf16[32,40,128]{2,1,0:T(8,128)(2,1)}), bf16[32,40,128]{2,1,0:T(8,128)(2,1)S(1)}, u32[]{:S(2)}, u32[]{:S(2)}) %all-to-all-start) | async-done | bytes 327712 | tf_op jit(solution)/shard_map/all_to_all | solution.py:471
  22.4 9.6 %image.1 = (f32[16,1024]{1,0:T(8,128)S(1)}, f32[16,1024]{1,0:T(8,128)S(1)}) custom-call(f32[552,1024]{1,0:T(8,128)} %prepare.1.packed_hbm, bf16[32,40,128]{2,1,0:T(8,128)(2,1)S(1)} %all-to-all-done.block_ref), custom_call_target="tpu_custom_call" | custom-call | tf_op jit(solution)/shard_map/image/pallas_call | solution.py:512
  32.0 1.1 %collective-permute-start = (f32[16,1024]{1,0:T(8,128)S(1)}, f32[16,1024]{1,0:T(8,128)S(1)}, u32[]{:S(2)}, u32[]{:S(2)}) collective-permute-start(f32[16,1024]{1,0:T(8,128)S(1)} %get-tuple-element.7), channel_id=1, source_target_pairs={{0,16},{16,0},{1,17},{17,1},{2,18},{18,2},{3,19},{19,3},{4,20},{20... | collective-permute-start | bytes 196616 | tf_op jit(solution)/shard_map/ppermute | solution.py:536
  33.0 3.3 %collective-permute-done.got_ref = f32[16,1024]{1,0:T(8,128)S(1)} collective-permute-done((f32[16,1024]{1,0:T(8,128)S(1)}, f32[16,1024]{1,0:T(8,128)S(1)}, u32[]{:S(2)}, u32[]{:S(2)}) %collective-permute-start) | collective-permute-done | bytes 65568 | tf_op jit(solution)/shard_map/ppermute | solution.py:536
  36.3 0.7 %finish.1 = (f32[16,2048]{1,0:T(8,128)}, f32[1,2048]{1,0:T(1,128)}) custom-call(f32[16,1024]{1,0:T(8,128)S(1)} %get-tuple-element.6.keep_ref, f32[16,1024]{1,0:T(8,128)S(1)} %collective-permute-done.got_ref), custom_call_target="tpu_custom_call" | custom-call | tf_op jit(solution)/shard_map/finish/pallas_call | solution.py:537
Async XLA Ops:
  3.4 19.0 %all-to-all-start = ((bf16[32,40,128]{2,1,0:T(8,128)(2,1)}), bf16[32,40,128]{2,1,0:T(8,128)(2,1)S(1)}, u32[]{:S(2)}, u32[]{:S(2)}) async-start(bf16[32,40,128]{2,1,0:T(8,128)(2,1)} %send.1), calls=%async_computation | async-start | bytes 655360 | tf_op jit(solution)/shard_map/all_to_all | solution.py:471
  32.0 4.3 %collective-permute-start = (f32[16,1024]{1,0:T(8,128)S(1)}, f32[16,1024]{1,0:T(8,128)S(1)}, u32[]{:S(2)}, u32[]{:S(2)}) collective-permute-start(f32[16,1024]{1,0:T(8,128)S(1)} %get-tuple-element.7), channel_id=1, source_target_pairs={{0,16},{16,0},{1,17},{17,1},{2,18},{18,2},{3,19},{19,3},{4,20},{20... | collective-permute-start | bytes 196616 | tf_op jit(solution)/shard_map/ppermute | solution.py:536

commit v12 on v7

--- a/solution.py
+++ b/solution.py
@@ -14,6 +14,7 @@
 NTAB = 16
 LANES = 128
 DEGREES = 32
+FINE = 24
 REACH = 1.5
 TABLE_PIECES = 4
 VMEM_LIMIT = 64 * 1024 * 1024 - 64 * 1024
@@ -106,9 +107,9 @@
     both = jnp.concatenate(split_bf16(table, 2), axis=0)
     small[1].wait()
     sums = lax.dot_general(
-        traces_ref[...], both, (((1,), (1,)), ((), ())), preferred_element_type=jnp.float32
+        both, traces_ref[...], (((1,), (1,)), ((), ())), preferred_element_type=jnp.float32
     )
-    sums = sums[:, : 2 * NF] + sums[:, 2 * NF :]
+    sums = (sums[: 2 * NF] + sums[2 * NF :]).T
     terms = [term.astype(jnp.float32) for term in split_bf16(sums, 2)]
     tile = jnp.concatenate([term[at : at + 8] for term in terms for at in range(0, stations_dev, 8)], axis=1)
     tile = tile.astype(jnp.bfloat16)
@@ -278,8 +279,15 @@
             pltpu.make_async_copy(packed_hbm.at[plan_at, pl.ds(0, width)], place_of_ref, sems.at[0]),
             pltpu.make_async_copy(packed_hbm.at[plan_at, pl.ds(0, width)], plan_ref, sems.at[1]),
             pltpu.make_async_copy(packed_hbm.at[coef_at, pl.ds(0, LANES)], coef_ref, sems.at[2]),
-            pltpu.make_async_copy(packed_hbm.at[cos_at, pl.ds(0, nodes)], cos_ref, sems.at[3]),
-            pltpu.make_async_copy(packed_hbm.at[sin_at, pl.ds(0, nodes)], sin_ref, sems.at[4]),
+        ]
+        + [
+            pltpu.make_async_copy(
+                packed_hbm.at[pl.ds(at.start + first, 4 * NF), pl.ds(0, nodes)],
+                ref.at[pl.ds(first, 4 * NF), :],
+                sems.at[3 + 2 * (first // (4 * NF)) + which],
+            )
+            for first in range(0, NTAB * NF, 4 * NF)
+            for which, (at, ref) in enumerate(((cos_at, cos_ref), (sin_at, sin_ref)))
         ]
     )
     height = block_ref.shape[1]
@@ -339,10 +347,17 @@
             tall = jnp.concatenate(
                 [sides[k % 2] * coef_ref[k : k + 1, :] for k in range(half * per, (half + 1) * per)], axis=0
             )
-            at = slice(half * LANES, (half + 1) * LANES)
-            for term, value in enumerate(split_bf16(tall.T, 2)):
-                left_ref[2 * pair, term * lanes : (term + 1) * lanes, at] = value[:lanes]
-                left_ref[2 * pair + 1, term * lanes : (term + 1) * lanes, at] = value[lanes:]
+            high, low = split_bf16(tall.T, 2)
+            first = half * LANES
+            fine = min(FINE * 8 - first, LANES)
+            if fine == LANES:
+                parts = [(first, high), (depth + first, high), (2 * FINE * 8 + first + LANES, low)]
+            else:
+                mixed = [high[:, :fine].astype(jnp.float32), low[:, :fine].astype(jnp.float32)]
+                parts = [(first, high), (depth + first, jnp.concatenate(mixed, axis=1).astype(jnp.bfloat16))]
+            for at, value in parts:
+                left_ref[2 * pair, :, at : at + LANES] = value[:lanes]
+                left_ref[2 * pair + 1, :, at : at + LANES] = value[lanes:]
 
     used = plan_ref[3, 0].astype(jnp.int32)
     sure = stations // 16
@@ -352,17 +367,15 @@
     else:
         lax.fori_loop(0, sure, lambda pair, carry: (make_left(pair), carry)[1], 0)
     lax.fori_loop(sure, (used + 1) // 2, lambda pair, carry: (make_left(pair), carry)[1], 0)
-    spot = (lax.broadcasted_iota(jnp.int32, (16, depth), 1) & 7).astype(jnp.float32)
+    spot = (lax.broadcasted_iota(jnp.int32, (16, left_ref.shape[2]), 1) & 7).astype(jnp.float32)
 
     def left_of(group):
         mask = spot < plan_ref[2, group]
         results = []
         for keep, drop in ((1.0, 0.0), (0.0, 1.0)):
             side = jnp.where(mask, keep, drop).astype(jnp.bfloat16)
-            results.append(left_ref[group] * jnp.concatenate([side] * (2 * lanes // 16), axis=0))
-        high = jnp.concatenate([result[:lanes] for result in results], axis=0)
-        low = jnp.concatenate([result[lanes:] for result in results], axis=0)
-        return jnp.concatenate([high, high, low], axis=1)
+            results.append(left_ref[group] * jnp.concatenate([side] * (lanes // 16), axis=0))
+        return jnp.concatenate(results, axis=0)
 
     def basis_steps(group, basis_ref):
         arg = place_ref[pl.ds(pl.multiple_of(group * 8, 8), 8), :]
@@ -370,9 +383,9 @@
         before, now = jnp.ones_like(arg), arg
         for degree in range(0, DEGREES, 2):
             pair = jnp.concatenate([before, now], axis=0)
-            high, low = split_bf16(pair, 2)
-            basis_ref[degree * 8 : degree * 8 + 16, :] = high
-            basis_ref[depth + degree * 8 : depth + degree * 8 + 16, :] = low
+            terms = split_bf16(pair, 2 if degree < FINE else 1)
+            for term, value in enumerate(terms):
+                basis_ref[term * depth + degree * 8 : term * depth + degree * 8 + 16, :] = value
             before = twice * now - before
             now = twice * before - now
             if degree % 8 == 6:
@@ -386,10 +399,15 @@
         left = left_of(group)
         tables = [plan_ref[slot, group].astype(jnp.int32) for slot in range(2)]
         phasor_rows = [pl.ds(pl.multiple_of(table * NF, NF), NF) for table in tables]
+        fine = FINE * 8
         for first in range(0, nodes, chunk):
             at = slice(first, first + chunk)
-            right = jnp.concatenate([basis_ref[:, at], basis_ref[:depth, at]], axis=0)
-            got = jnp.dot(left, right, preferred_element_type=jnp.float32)
+            right = [
+                basis_ref[: depth + fine, at],
+                basis_ref[LANES:fine, at],
+                basis_ref[:LANES, at],
+            ]
+            got = jnp.dot(left, jnp.concatenate(right, axis=0), preferred_element_type=jnp.float32)
             next(steps, None)
             for win in range(windows):
                 row = win * 2 * NF
@@ -413,7 +431,12 @@
         add_group(group + 1, basis_b, basis_steps(jnp.minimum(group + 2, places // 8 - 1), basis_a))
         return carry
 
-    lax.fori_loop(0, (used + 1) // 2, body, 0)
+    lax.fori_loop(0, used // 2, body, 0)
+
+    @pl.when(used % 2 == 1)
+    def _():
+        add_group(used - 1, basis_a, iter(()))
+
     powers = []
     for win in range(windows):
         row = win * 2 * NF
@@ -505,7 +528,7 @@
     places = (stations // 8 + ntab // 2 + 2) // 2 * 16
     half = jax.ShapeDtypeStruct((NF, nodes), jnp.float32)
     rows = 2 * windows * 2 * NF
-    basis = pltpu.VMEM((2 * DEGREES * 8, nodes), jnp.bfloat16)
+    basis = pltpu.VMEM(((DEGREES + FINE) * 8, nodes), jnp.bfloat16)
     keep, send = pl.pallas_call(
         functools.partial(image_kernel, merged, stations_dev),
         out_shape=[half, half],
@@ -517,15 +540,15 @@
             coefs,
             phasors,
             phasors,
-            pltpu.SemaphoreType.DMA((5,)),
+            pltpu.SemaphoreType.DMA((3 + ntab // 2,)),
             pltpu.VMEM((places, nodes), jnp.float32),
             pltpu.VMEM((places, rows), jnp.float32),
-            pltpu.VMEM((places // 8, rows, DEGREES * 8), jnp.bfloat16),
+            pltpu.VMEM((places // 8, rows // 2, (DEGREES + 2 * FINE) * 8), jnp.bfloat16),
             pltpu.VMEM((rows // 2, nodes), jnp.float32),
             basis,
             basis,
         ],
-        compiler_params=params(1024 * 1024),
+        compiler_params=params(23 * 512 * 1024),
         name="image",
     )(packed, *received)
     got = lax.ppermute(send, "win", [(0, 1), (1, 0)])

time: 40.8 us -> 37.3 us (0.914)
  Pallas kernels: 22.7 us -> 20.9 us
  local copies, waits for them, and re-layouts: 1.55 us -> 0 us
    pallas_call x1, Pallas kernels: 11.3 us -> 9.62 us  [on_device(): pl.pallas_call(functools.partial(image_kernel, merged, stations_dev), out...]
    unnamed x4 -> x0, local copies, waits for them, and re-layouts: 1.55 us -> none
  transfers between devices with their start and end apart: 2 -> 2, of which waited for: 2 -> 2; matrix products, arithmetic and copies ran while one was open for 0% -> 0% of each run, Pallas kernels for 20% -> 21%
where the time goes in v12:
time: 37.3 us; the launch traced here: 37.1 us
  Pallas kernels  20.9 us (56%)
  starting transfers between devices  8.38 us (22%)
  waiting for transfers between devices  7.08 us (19%)
  between operations  0.66 us (2%)
    pallas_call x1, Pallas kernels, on_device(): pl.pallas_call(functools.partial(image_kernel, merged, stations_dev), out...  9.62 us
    pallas_call x1, Pallas kernels, on_device(): pl.pallas_call(prepare_kernel, out_shape=jax.ShapeDtypeStruct(packed_shap...  7.88 us
    all_to_all x1, starting transfers between devices, on_device(): lax.all_to_all(blocks, ('win', 'sta', 'freq'), split_axis=0, concat_axis=...  7.31 us
    all_to_all x1, waiting for transfers between devices, on_device(): lax.all_to_all(blocks, ('win', 'sta', 'freq'), split_axis=0, concat_axis=...  3.81 us
    ppermute x1, waiting for transfers between devices, on_device(): got = lax.ppermute(send, 'win', [(0, 1), (1, 0)])  3.27 us
    pallas_call x1, Pallas kernels, on_device(): pl.pallas_call(functools.partial(send_kernel, nodes), out_shape=jax.Shape...  2.75 us
    ppermute x1, starting transfers between devices, on_device(): got = lax.ppermute(send, 'win', [(0, 1), (1, 0)])  1.06 us
  transfers between devices with their start and end apart: 2, of which 2 were waited for; matrix products, arithmetic and copies ran while one was open for 0% of the time, Pallas kernels for 21%

profile of v12, /device:TPU:0, one launch (start us, length us, event | category | flops | bytes accessed | tf_op | source)
XLA Modules:
  0.0 37.1 jit_solution(5909416950663261411)
XLA Ops:
  0.6 2.8 %send.1 = bf16[32,40,128]{2,1,0:T(8,128)(2,1)} custom-call(s32[1,16]{1,0:T(1,128)} %bitcast.5, bf16[16,2560]{1,0:T(8,128)(2,1)} %traces_hbm.1, bf16[16,32768]{1,0:T(8,128)(2,1)} %corr_hbm.1), custom_call_target="tpu_custom_call" | custom-call | tf_op jit(solution)/shard_map/send/pallas_call | solution.py:478
  3.4 7.3 %all-to-all-start = ((bf16[32,40,128]{2,1,0:T(8,128)(2,1)}), bf16[32,40,128]{2,1,0:T(8,128)(2,1)S(1)}, u32[]{:S(2)}, u32[]{:S(2)}) async-start(bf16[32,40,128]{2,1,0:T(8,128)(2,1)} %send.1), calls=%async_computation | async-start | bytes 655360 | tf_op jit(solution)/shard_map/all_to_all | solution.py:491
  10.7 7.9 %prepare.1.packed_hbm = f32[552,1024]{1,0:T(8,128)} custom-call(s32[1,16]{1,0:T(1,128)} %bitcast.6, s32[1,128]{1,0:T(1,128)} %bitcast.7, s32[256,128]{1,0:T(8,128)} %bitcast.4, f32[16,32768]{1,0:T(8,128)} %tables_hbm.1), custom_call_target="tpu_custom_call" | custom-call | tf_op jit(solution)/shard_map/prepare/pallas_call | solution.py:505
  18.6 3.8 %all-to-all-done.block_ref = bf16[32,40,128]{2,1,0:T(8,128)(2,1)S(1)} async-done(((bf16[32,40,128]{2,1,0:T(8,128)(2,1)}), bf16[32,40,128]{2,1,0:T(8,128)(2,1)S(1)}, u32[]{:S(2)}, u32[]{:S(2)}) %all-to-all-start) | async-done | bytes 327712 | tf_op jit(solution)/shard_map/all_to_all | solution.py:491
  22.4 9.6 %image.1 = (f32[16,1024]{1,0:T(8,128)S(1)}, f32[16,1024]{1,0:T(8,128)S(1)}) custom-call(f32[552,1024]{1,0:T(8,128)} %prepare.1.packed_hbm, bf16[32,40,128]{2,1,0:T(8,128)(2,1)S(1)} %all-to-all-done.block_ref), custom_call_target="tpu_custom_call" | custom-call | tf_op jit(solution)/shard_map/image/pallas_call | solution.py:532
  32.0 1.1 %collective-permute-start = (f32[16,1024]{1,0:T(8,128)S(1)}, f32[16,1024]{1,0:T(8,128)S(1)}, u32[]{:S(2)}, u32[]{:S(2)}) collective-permute-start(f32[16,1024]{1,0:T(8,128)S(1)} %get-tuple-element.7), channel_id=1, source_target_pairs={{0,16},{16,0},{1,17},{17,1},{2,18},{18,2},{3,19},{19,3},{4,20},{20... | collective-permute-start | bytes 196616 | tf_op jit(solution)/shard_map/ppermute | solution.py:554
  33.1 3.3 %collective-permute-done.got_ref = f32[16,1024]{1,0:T(8,128)S(1)} collective-permute-done((f32[16,1024]{1,0:T(8,128)S(1)}, f32[16,1024]{1,0:T(8,128)S(1)}, u32[]{:S(2)}, u32[]{:S(2)}) %collective-permute-start) | collective-permute-done | bytes 65568 | tf_op jit(solution)/shard_map/ppermute | solution.py:554
  36.4 0.7 %finish.1 = (f32[16,2048]{1,0:T(8,128)}, f32[1,2048]{1,0:T(1,128)}) custom-call(f32[16,1024]{1,0:T(8,128)S(1)} %get-tuple-element.6.keep_ref, f32[16,1024]{1,0:T(8,128)S(1)} %collective-permute-done.got_ref), custom_call_target="tpu_custom_call" | custom-call | tf_op jit(solution)/shard_map/finish/pallas_call | solution.py:555
Async XLA Ops:
  3.4 19.0 %all-to-all-start = ((bf16[32,40,128]{2,1,0:T(8,128)(2,1)}), bf16[32,40,128]{2,1,0:T(8,128)(2,1)S(1)}, u32[]{:S(2)}, u32[]{:S(2)}) async-start(bf16[32,40,128]{2,1,0:T(8,128)(2,1)} %send.1), calls=%async_computation | async-start | bytes 655360 | tf_op jit(solution)/shard_map/all_to_all | solution.py:491
  32.0 4.3 %collective-permute-start = (f32[16,1024]{1,0:T(8,128)S(1)}, f32[16,1024]{1,0:T(8,128)S(1)}, u32[]{:S(2)}, u32[]{:S(2)}) collective-permute-start(f32[16,1024]{1,0:T(8,128)S(1)} %get-tuple-element.7), channel_id=1, source_target_pairs={{0,16},{16,0},{1,17},{17,1},{2,18},{18,2},{3,19},{19,3},{4,20},{20... | collective-permute-start | bytes 196616 | tf_op jit(solution)/shard_map/ppermute | solution.py:554

commit v13 on v12

--- a/solution.py
+++ b/solution.py
@@ -335,6 +335,8 @@
     for copy in copies[1:3]:
         copy.wait()
 
+    spot = (lax.broadcasted_iota(jnp.int32, (lanes, LANES), 1) & 7).astype(jnp.float32)
+
     def make_left(pair):
         top = weight_ref[pl.ds(pl.multiple_of(pair * 16, 16), 8), :]
         bottom = weight_ref[pl.ds(pl.multiple_of(pair * 16 + 8, 8), 8), :]
@@ -347,17 +349,22 @@
             tall = jnp.concatenate(
                 [sides[k % 2] * coef_ref[k : k + 1, :] for k in range(half * per, (half + 1) * per)], axis=0
             )
-            high, low = split_bf16(tall.T, 2)
+            turned = tall.T
             first = half * LANES
             fine = min(FINE * 8 - first, LANES)
-            if fine == LANES:
-                parts = [(first, high), (depth + first, high), (2 * FINE * 8 + first + LANES, low)]
-            else:
-                mixed = [high[:, :fine].astype(jnp.float32), low[:, :fine].astype(jnp.float32)]
-                parts = [(first, high), (depth + first, jnp.concatenate(mixed, axis=1).astype(jnp.bfloat16))]
-            for at, value in parts:
-                left_ref[2 * pair, :, at : at + LANES] = value[:lanes]
-                left_ref[2 * pair + 1, :, at : at + LANES] = value[lanes:]
+            for which in range(2):
+                group = 2 * pair + which
+                mask = spot < plan_ref[2, group]
+                value = turned[which * lanes : (which + 1) * lanes]
+                value = jnp.concatenate([jnp.where(mask, value, 0.0), jnp.where(mask, 0.0, value)], axis=0)
+                high, low = split_bf16(value, 2)
+                if fine == LANES:
+                    parts = [(first, high), (depth + first, high), (2 * FINE * 8 + first + LANES, low)]
+                else:
+                    mixed = [high[:, :fine].astype(jnp.float32), low[:, :fine].astype(jnp.float32)]
+                    parts = [(first, high), (depth + first, jnp.concatenate(mixed, axis=1).astype(jnp.bfloat16))]
+                for at, part in parts:
+                    left_ref[group, :, at : at + LANES] = part
 
     used = plan_ref[3, 0].astype(jnp.int32)
     sure = stations // 16
@@ -367,16 +374,6 @@
     else:
         lax.fori_loop(0, sure, lambda pair, carry: (make_left(pair), carry)[1], 0)
     lax.fori_loop(sure, (used + 1) // 2, lambda pair, carry: (make_left(pair), carry)[1], 0)
-    spot = (lax.broadcasted_iota(jnp.int32, (16, left_ref.shape[2]), 1) & 7).astype(jnp.float32)
-
-    def left_of(group):
-        mask = spot < plan_ref[2, group]
-        results = []
-        for keep, drop in ((1.0, 0.0), (0.0, 1.0)):
-            side = jnp.where(mask, keep, drop).astype(jnp.bfloat16)
-            results.append(left_ref[group] * jnp.concatenate([side] * (lanes // 16), axis=0))
-        return jnp.concatenate(results, axis=0)
-
     def basis_steps(group, basis_ref):
         arg = place_ref[pl.ds(pl.multiple_of(group * 8, 8), 8), :]
         twice = arg + arg
@@ -396,7 +393,7 @@
             pass
 
     def add_group(group, basis_ref, steps):
-        left = left_of(group)
+        left = left_ref[group]
         tables = [plan_ref[slot, group].astype(jnp.int32) for slot in range(2)]
         phasor_rows = [pl.ds(pl.multiple_of(table * NF, NF), NF) for table in tables]
         fine = FINE * 8
@@ -543,7 +540,7 @@
             pltpu.SemaphoreType.DMA((3 + ntab // 2,)),
             pltpu.VMEM((places, nodes), jnp.float32),
             pltpu.VMEM((places, rows), jnp.float32),
-            pltpu.VMEM((places // 8, rows // 2, (DEGREES + 2 * FINE) * 8), jnp.bfloat16),
+            pltpu.VMEM((places // 8, rows, (DEGREES + 2 * FINE) * 8), jnp.bfloat16),
             pltpu.VMEM((rows // 2, nodes), jnp.float32),
             basis,
             basis,

time: 37.3 us -> 37.4 us (level)
  no operation moved by 1% of the time
where the time goes in v13:
time: 37.4 us; the launch traced here: 37.1 us
  Pallas kernels  21 us (56%)
  starting transfers between devices  8.38 us (22%)
  waiting for transfers between devices  7.07 us (19%)
  between operations  0.66 us (2%)
    pallas_call x1, Pallas kernels, on_device(): pl.pallas_call(functools.partial(image_kernel, merged, stations_dev), out...  9.64 us
    pallas_call x1, Pallas kernels, on_device(): pl.pallas_call(prepare_kernel, out_shape=jax.ShapeDtypeStruct(packed_shap...  7.88 us
    all_to_all x1, starting transfers between devices, on_device(): lax.all_to_all(blocks, ('win', 'sta', 'freq'), split_axis=0, concat_axis=...  7.31 us
    all_to_all x1, waiting for transfers between devices, on_device(): lax.all_to_all(blocks, ('win', 'sta', 'freq'), split_axis=0, concat_axis=...  3.81 us
    ppermute x1, waiting for transfers between devices, on_device(): got = lax.ppermute(send, 'win', [(0, 1), (1, 0)])  3.26 us
    pallas_call x1, Pallas kernels, on_device(): pl.pallas_call(functools.partial(send_kernel, nodes), out_shape=jax.Shape...  2.75 us
    ppermute x1, starting transfers between devices, on_device(): got = lax.ppermute(send, 'win', [(0, 1), (1, 0)])  1.07 us
  transfers between devices with their start and end apart: 2, of which 2 were waited for; matrix products, arithmetic and copies ran while one was open for 0% of the time, Pallas kernels for 21%

profile of v13, /device:TPU:0, one launch (start us, length us, event | category | flops | bytes accessed | tf_op | source)
XLA Modules:
  0.0 37.1 jit_solution(16388427340929299809)
XLA Ops:
  0.6 2.8 %send.1 = bf16[32,40,128]{2,1,0:T(8,128)(2,1)} custom-call(s32[1,16]{1,0:T(1,128)} %bitcast.5, bf16[16,2560]{1,0:T(8,128)(2,1)} %traces_hbm.1, bf16[16,32768]{1,0:T(8,128)(2,1)} %corr_hbm.1), custom_call_target="tpu_custom_call" | custom-call | tf_op jit(solution)/shard_map/send/pallas_call | solution.py:475
  3.4 7.3 %all-to-all-start = ((bf16[32,40,128]{2,1,0:T(8,128)(2,1)}), bf16[32,40,128]{2,1,0:T(8,128)(2,1)S(1)}, u32[]{:S(2)}, u32[]{:S(2)}) async-start(bf16[32,40,128]{2,1,0:T(8,128)(2,1)} %send.1), calls=%async_computation | async-start | bytes 655360 | tf_op jit(solution)/shard_map/all_to_all | solution.py:488
  10.7 7.9 %prepare.1.packed_hbm = f32[552,1024]{1,0:T(8,128)} custom-call(s32[1,16]{1,0:T(1,128)} %bitcast.6, s32[1,128]{1,0:T(1,128)} %bitcast.7, s32[256,128]{1,0:T(8,128)} %bitcast.4, f32[16,32768]{1,0:T(8,128)} %tables_hbm.1), custom_call_target="tpu_custom_call" | custom-call | tf_op jit(solution)/shard_map/prepare/pallas_call | solution.py:502
  18.6 3.8 %all-to-all-done.block_ref = bf16[32,40,128]{2,1,0:T(8,128)(2,1)S(1)} async-done(((bf16[32,40,128]{2,1,0:T(8,128)(2,1)}), bf16[32,40,128]{2,1,0:T(8,128)(2,1)S(1)}, u32[]{:S(2)}, u32[]{:S(2)}) %all-to-all-start) | async-done | bytes 327712 | tf_op jit(solution)/shard_map/all_to_all | solution.py:488
  22.4 9.6 %image.1 = (f32[16,1024]{1,0:T(8,128)S(1)}, f32[16,1024]{1,0:T(8,128)S(1)}) custom-call(f32[552,1024]{1,0:T(8,128)} %prepare.1.packed_hbm, bf16[32,40,128]{2,1,0:T(8,128)(2,1)S(1)} %all-to-all-done.block_ref), custom_call_target="tpu_custom_call" | custom-call | tf_op jit(solution)/shard_map/image/pallas_call | solution.py:529
  32.1 1.1 %collective-permute-start = (f32[16,1024]{1,0:T(8,128)S(1)}, f32[16,1024]{1,0:T(8,128)S(1)}, u32[]{:S(2)}, u32[]{:S(2)}) collective-permute-start(f32[16,1024]{1,0:T(8,128)S(1)} %get-tuple-element.7), channel_id=1, source_target_pairs={{0,16},{16,0},{1,17},{17,1},{2,18},{18,2},{3,19},{19,3},{4,20},{20... | collective-permute-start | bytes 196616 | tf_op jit(solution)/shard_map/ppermute | solution.py:551
  33.1 3.3 %collective-permute-done.got_ref = f32[16,1024]{1,0:T(8,128)S(1)} collective-permute-done((f32[16,1024]{1,0:T(8,128)S(1)}, f32[16,1024]{1,0:T(8,128)S(1)}, u32[]{:S(2)}, u32[]{:S(2)}) %collective-permute-start) | collective-permute-done | bytes 65568 | tf_op jit(solution)/shard_map/ppermute | solution.py:551
  36.4 0.7 %finish.1 = (f32[16,2048]{1,0:T(8,128)}, f32[1,2048]{1,0:T(1,128)}) custom-call(f32[16,1024]{1,0:T(8,128)S(1)} %get-tuple-element.6.keep_ref, f32[16,1024]{1,0:T(8,128)S(1)} %collective-permute-done.got_ref), custom_call_target="tpu_custom_call" | custom-call | tf_op jit(solution)/shard_map/finish/pallas_call | solution.py:552
Async XLA Ops:
  3.4 19.0 %all-to-all-start = ((bf16[32,40,128]{2,1,0:T(8,128)(2,1)}), bf16[32,40,128]{2,1,0:T(8,128)(2,1)S(1)}, u32[]{:S(2)}, u32[]{:S(2)}) async-start(bf16[32,40,128]{2,1,0:T(8,128)(2,1)} %send.1), calls=%async_computation | async-start | bytes 655360 | tf_op jit(solution)/shard_map/all_to_all | solution.py:488
  32.1 4.3 %collective-permute-start = (f32[16,1024]{1,0:T(8,128)S(1)}, f32[16,1024]{1,0:T(8,128)S(1)}, u32[]{:S(2)}, u32[]{:S(2)}) collective-permute-start(f32[16,1024]{1,0:T(8,128)S(1)} %get-tuple-element.7), channel_id=1, source_target_pairs={{0,16},{16,0},{1,17},{17,1},{2,18},{18,2},{3,19},{19,3},{4,20},{20... | collective-permute-start | bytes 196616 | tf_op jit(solution)/shard_map/ppermute | solution.py:551

commit v14 on v13

--- a/solution.py
+++ b/solution.py
@@ -17,6 +17,7 @@
 FINE = 24
 REACH = 1.5
 TABLE_PIECES = 4
+PARTS = 2
 VMEM_LIMIT = 64 * 1024 * 1024 - 64 * 1024
 
 
@@ -91,8 +92,7 @@
         for piece in range(pieces):
             at = pl.multiple_of(first + (place * pieces + piece) * LANES, LANES)
             to = out_ref.at[dev, pl.ds(piece * stations_dev, stations_dev), :]
-            sem = sems.at[2 + dev * pieces + piece]
-            copies.append(pltpu.make_async_copy(corr_hbm.at[:, pl.ds(at, LANES)], to, sem))
+            copies.append(pltpu.make_async_copy(corr_hbm.at[:, pl.ds(at, LANES)], to, sems.at[2]))
     start_all(copies)
     start = lax.axis_index("freq") * half_length
     small[0].wait()
@@ -115,8 +115,9 @@
     tile = tile.astype(jnp.bfloat16)
     for dev in range(devices):
         out_ref[dev, height - 8 :, :] = tile
-    for copy in copies:
-        copy.wait()
+    if copies:
+        filled = out_ref.at[:, pl.ds(0, height - 8), :]
+        pltpu.make_async_copy(filled, filled, sems.at[2]).wait()
 
 
 def own_place():
@@ -267,8 +268,9 @@
 
 def image_kernel(merged, stations_dev, packed_hbm, block_ref, *rest):
     corr_ref, rest = (None, rest) if merged else (rest[0], rest[1:])
-    keep_ref, send_ref, plan_ref, place_of_ref, coef_ref, cos_ref, sin_ref, sems = rest[:8]
-    place_ref, weight_ref, left_ref, sums_ref, basis_a, basis_b = rest[8:]
+    keep_ref, *send_refs = rest[: 1 + PARTS]
+    plan_ref, place_of_ref, coef_ref, cos_ref, sin_ref, sems = rest[1 + PARTS : 7 + PARTS]
+    place_ref, weight_ref, left_ref, sums_ref, basis_a, basis_b = rest[7 + PARTS :]
     places, nodes = place_ref.shape
     windows, groups, cores = (lax.axis_size(a) for a in ("win", "sta", "freq"))
     stations = stations_dev * groups
@@ -441,14 +443,17 @@
         powers.append(real * real + imag * imag)
     mine = lax.axis_index("win") == 0
     keep_ref[...] = jnp.where(mine, powers[0], powers[1])
-    send_ref[...] = jnp.where(mine, powers[1], powers[0])
-
-
-def finish_kernel(stations, keep_ref, got_ref, spectrum_ref, beam_ref):
+    other = jnp.where(mine, powers[1], powers[0])
+    for at, ref in enumerate(send_refs):
+        ref[...] = other[at * ref.shape[0] : (at + 1) * ref.shape[0]]
+
+
+def finish_kernel(stations, keep_ref, *rest):
+    *got_refs, spectrum_ref, beam_ref = rest
     nodes = keep_ref.shape[1]
     win = lax.axis_index("win")
-    for place, ref in ((win, keep_ref), (1 - win, got_ref)):
-        power = ref[...]
+    for place, refs in ((win, [keep_ref]), (1 - win, got_refs)):
+        power = jnp.concatenate([ref[...] for ref in refs], axis=0)
         total = jnp.sum(power, axis=0, keepdims=True)
         at = pl.ds(pl.multiple_of(place * nodes, LANES), nodes)
         spectrum_ref[:, at] = power * (NF / total)
@@ -480,7 +485,7 @@
         scratch_shapes=[
             bins_scratch,
             pltpu.VMEM(traces.shape, traces.dtype),
-            pltpu.SemaphoreType.DMA((2 + devices * max(pieces, 1),)),
+            pltpu.SemaphoreType.DMA((3,)),
         ],
         compiler_params=params(0),
         name="send",
@@ -526,11 +531,12 @@
     half = jax.ShapeDtypeStruct((NF, nodes), jnp.float32)
     rows = 2 * windows * 2 * NF
     basis = pltpu.VMEM(((DEGREES + FINE) * 8, nodes), jnp.bfloat16)
-    keep, send = pl.pallas_call(
+    part = jax.ShapeDtypeStruct((NF // PARTS, nodes), jnp.float32)
+    keep, *sends = pl.pallas_call(
         functools.partial(image_kernel, merged, stations_dev),
-        out_shape=[half, half],
+        out_shape=[half] + [part] * PARTS,
         in_specs=[hbm] + [vmem] * len(received),
-        out_specs=[vmem, vmem],
+        out_specs=[vmem] * (1 + PARTS),
         scratch_shapes=[
             pltpu.SMEM((8, plan_width), jnp.float32),
             plan,
@@ -548,18 +554,18 @@
         compiler_params=params(23 * 512 * 1024),
         name="image",
     )(packed, *received)
-    got = lax.ppermute(send, "win", [(0, 1), (1, 0)])
+    got = [lax.ppermute(send, "win", [(0, 1), (1, 0)]) for send in sends]
     spectrum, beam_power = pl.pallas_call(
         functools.partial(finish_kernel, stations),
         out_shape=[
             jax.ShapeDtypeStruct((NF, windows * nodes), jnp.float32),
             jax.ShapeDtypeStruct((1, windows * nodes), jnp.float32),
         ],
-        in_specs=[vmem, vmem],
+        in_specs=[vmem] * (1 + PARTS),
         out_specs=[vmem, vmem],
         compiler_params=params(32 * 1024 * 1024),
         name="finish",
-    )(keep, got)
+    )(keep, *got)
     return spectrum, beam_power.reshape(windows * nodes)
 
 

time: 37.4 us -> 37 us (0.989); the launches traced: 37.1 us -> 37.1 us
  starting transfers between devices: 8.38 us -> 9.41 us
  Pallas kernels: 21 us -> 20.3 us
  waiting for transfers between devices: 7.07 us -> 6.68 us
    ppermute x1 -> x2, starting transfers between devices: 1.07 us -> 2.09 us  [on_device(): got = [lax.ppermute(send, 'win', [(0, 1), (1, 0)]) for send in sends]]
    pallas_call x1, Pallas kernels: 2.75 us -> 2.09 us  [on_device(): pl.pallas_call(functools.partial(send_kernel, nodes), out_shape=jax.Shape...]
    ppermute x1 -> x2, waiting for transfers between devices: 3.26 us -> 2.89 us  [on_device(): got = [lax.ppermute(send, 'win', [(0, 1), (1, 0)]) for send in sends]]
  transfers between devices with their start and end apart: 2 -> 3, of which waited for: 2 -> 3; matrix products, arithmetic and copies ran while one was open for 0% -> 0% of each run, Pallas kernels for 21% -> 21%
where the time goes in v14:
time: 37 us; the launch traced here: 37.1 us
  Pallas kernels  20.3 us (55%)
  starting transfers between devices  9.41 us (25%)
  waiting for transfers between devices  6.68 us (18%)
  between operations  0.66 us (2%)
    pallas_call x1, Pallas kernels, on_device(): pl.pallas_call(functools.partial(image_kernel, merged, stations_dev), out...  9.64 us
    pallas_call x1, Pallas kernels, on_device(): pl.pallas_call(prepare_kernel, out_shape=jax.ShapeDtypeStruct(packed_shap...  7.9 us
    all_to_all x1, starting transfers between devices, on_device(): lax.all_to_all(blocks, ('win', 'sta', 'freq'), split_axis=0, concat_axis=...  7.31 us
    all_to_all x1, waiting for transfers between devices, on_device(): lax.all_to_all(blocks, ('win', 'sta', 'freq'), split_axis=0, concat_axis=...  3.79 us
    ppermute x2, waiting for transfers between devices, on_device(): got = [lax.ppermute(send, 'win', [(0, 1), (1, 0)]) for send in sends]  2.89 us
    ppermute x2, starting transfers between devices, on_device(): got = [lax.ppermute(send, 'win', [(0, 1), (1, 0)]) for send in sends]  2.09 us
    pallas_call x1, Pallas kernels, on_device(): pl.pallas_call(functools.partial(send_kernel, nodes), out_shape=jax.Shape...  2.09 us
  transfers between devices with their start and end apart: 3, of which 3 were waited for; matrix products, arithmetic and copies ran while one was open for 0% of the time, Pallas kernels for 21%

profile of v14, /device:TPU:0, one launch (start us, length us, event | category | flops | bytes accessed | tf_op | source)
XLA Modules:
  0.0 37.1 jit_solution(1041713732597631514)
XLA Ops:
  0.6 2.1 %send.1 = bf16[32,40,128]{2,1,0:T(8,128)(2,1)} custom-call(s32[1,16]{1,0:T(1,128)} %bitcast.5, bf16[16,2560]{1,0:T(8,128)(2,1)} %traces_hbm.1, bf16[16,32768]{1,0:T(8,128)(2,1)} %corr_hbm.1), custom_call_target="tpu_custom_call" | custom-call | tf_op jit(solution)/shard_map/send/pallas_call | solution.py:480
  2.7 7.3 %all-to-all-start = ((bf16[32,40,128]{2,1,0:T(8,128)(2,1)}), bf16[32,40,128]{2,1,0:T(8,128)(2,1)S(1)}, u32[]{:S(2)}, u32[]{:S(2)}) async-start(bf16[32,40,128]{2,1,0:T(8,128)(2,1)} %send.1), calls=%async_computation | async-start | bytes 655360 | tf_op jit(solution)/shard_map/all_to_all | solution.py:493
  10.0 7.9 %prepare.1.packed_hbm = f32[552,1024]{1,0:T(8,128)} custom-call(s32[1,16]{1,0:T(1,128)} %bitcast.6, s32[1,128]{1,0:T(1,128)} %bitcast.7, s32[256,128]{1,0:T(8,128)} %bitcast.4, f32[16,32768]{1,0:T(8,128)} %tables_hbm.1), custom_call_target="tpu_custom_call" | custom-call | tf_op jit(solution)/shard_map/prepare/pallas_call | solution.py:507
  18.0 3.8 %all-to-all-done.block_ref = bf16[32,40,128]{2,1,0:T(8,128)(2,1)S(1)} async-done(((bf16[32,40,128]{2,1,0:T(8,128)(2,1)}), bf16[32,40,128]{2,1,0:T(8,128)(2,1)S(1)}, u32[]{:S(2)}, u32[]{:S(2)}) %all-to-all-start) | async-done | bytes 327712 | tf_op jit(solution)/shard_map/all_to_all | solution.py:493
  21.7 9.6 %image.1 = (f32[16,1024]{1,0:T(8,128)S(1)}, f32[8,1024]{1,0:T(8,128)S(1)}, f32[8,1024]{1,0:T(8,128)S(1)}) custom-call(f32[552,1024]{1,0:T(8,128)} %prepare.1.packed_hbm, bf16[32,40,128]{2,1,0:T(8,128)(2,1)S(1)} %all-to-all-done.block_ref), custom_call_target="tpu_custom_call" | custom-call | tf_op jit(solution)/shard_map/image/pallas_call | solution.py:535
  31.4 1.1 %collective-permute-start = (f32[8,1024]{1,0:T(8,128)S(1)}, f32[8,1024]{1,0:T(8,128)S(1)}, u32[]{:S(2)}, u32[]{:S(2)}) collective-permute-start(f32[8,1024]{1,0:T(8,128)S(1)} %get-tuple-element.8), channel_id=1, source_target_pairs={{0,16},{16,0},{1,17},{17,1},{2,18},{18,2},{3,19},{19,3},{4,20},{20... | collective-permute-start | bytes 98312 | tf_op jit(solution)/shard_map/ppermute | solution.py:557
  32.5 1.0 %collective-permute-start.1 = (f32[8,1024]{1,0:T(8,128)S(1)}, f32[8,1024]{1,0:T(8,128)S(1)}, u32[]{:S(2)}, u32[]{:S(2)}) collective-permute-start(f32[8,1024]{1,0:T(8,128)S(1)} %get-tuple-element.9), channel_id=1, source_target_pairs={{0,16},{16,0},{1,17},{17,1},{2,18},{18,2},{3,19},{19,3},{4,20},{20... | collective-permute-start | bytes 98312 | tf_op jit(solution)/shard_map/ppermute | solution.py:557
  33.5 2.1 %collective-permute-done.rest_0_ = f32[8,1024]{1,0:T(8,128)S(1)} collective-permute-done((f32[8,1024]{1,0:T(8,128)S(1)}, f32[8,1024]{1,0:T(8,128)S(1)}, u32[]{:S(2)}, u32[]{:S(2)}) %collective-permute-start) | collective-permute-done | bytes 32800 | tf_op jit(solution)/shard_map/ppermute | solution.py:557
  35.6 0.8 %collective-permute-done.1.rest_1_ = f32[8,1024]{1,0:T(8,128)S(1)} collective-permute-done((f32[8,1024]{1,0:T(8,128)S(1)}, f32[8,1024]{1,0:T(8,128)S(1)}, u32[]{:S(2)}, u32[]{:S(2)}) %collective-permute-start.1) | collective-permute-done | bytes 32800 | tf_op jit(solution)/shard_map/ppermute | solution.py:557
  36.4 0.7 %finish.1 = (f32[16,2048]{1,0:T(8,128)}, f32[1,2048]{1,0:T(1,128)}) custom-call(f32[16,1024]{1,0:T(8,128)S(1)} %get-tuple-element.7.keep_ref, f32[8,1024]{1,0:T(8,128)S(1)} %collective-permute-done.rest_0_, f32[8,1024]{1,0:T(8,128)S(1)} %collective-permute-done.1.rest_1_), custom_call_target="tpu_custom_call" | custom-call | tf_op jit(solution)/shard_map/finish/pallas_call | solution.py:558
Async XLA Ops:
  2.7 19.0 %all-to-all-start = ((bf16[32,40,128]{2,1,0:T(8,128)(2,1)}), bf16[32,40,128]{2,1,0:T(8,128)(2,1)S(1)}, u32[]{:S(2)}, u32[]{:S(2)}) async-start(bf16[32,40,128]{2,1,0:T(8,128)(2,1)} %send.1), calls=%async_computation | async-start | bytes 655360 | tf_op jit(solution)/shard_map/all_to_all | solution.py:493
  31.4 4.2 %collective-permute-start = (f32[8,1024]{1,0:T(8,128)S(1)}, f32[8,1024]{1,0:T(8,128)S(1)}, u32[]{:S(2)}, u32[]{:S(2)}) collective-permute-start(f32[8,1024]{1,0:T(8,128)S(1)} %get-tuple-element.8), channel_id=1, source_target_pairs={{0,16},{16,0},{1,17},{17,1},{2,18},{18,2},{3,19},{19,3},{4,20},{20... | collective-permute-start | bytes 98312 | tf_op jit(solution)/shard_map/ppermute | solution.py:557
  32.5 3.9 %collective-permute-start.1 = (f32[8,1024]{1,0:T(8,128)S(1)}, f32[8,1024]{1,0:T(8,128)S(1)}, u32[]{:S(2)}, u32[]{:S(2)}) collective-permute-start(f32[8,1024]{1,0:T(8,128)S(1)} %get-tuple-element.9), channel_id=1, source_target_pairs={{0,16},{16,0},{1,17},{17,1},{2,18},{18,2},{3,19},{19,3},{4,20},{20... | collective-permute-start | bytes 98312 | tf_op jit(solution)/shard_map/ppermute | solution.py:557

commit v15 on v14

--- a/solution.py
+++ b/solution.py
@@ -17,7 +17,7 @@
 FINE = 24
 REACH = 1.5
 TABLE_PIECES = 4
-PARTS = 2
+PARTS = 1
 VMEM_LIMIT = 64 * 1024 * 1024 - 64 * 1024
 
 
@@ -337,6 +337,7 @@
     for copy in copies[1:3]:
         copy.wait()
 
+    rows = 2 * lanes
     spot = (lax.broadcasted_iota(jnp.int32, (lanes, LANES), 1) & 7).astype(jnp.float32)
 
     def make_left(pair):
@@ -360,13 +361,13 @@
                 value = turned[which * lanes : (which + 1) * lanes]
                 value = jnp.concatenate([jnp.where(mask, value, 0.0), jnp.where(mask, 0.0, value)], axis=0)
                 high, low = split_bf16(value, 2)
-                if fine == LANES:
-                    parts = [(first, high), (depth + first, high), (2 * FINE * 8 + first + LANES, low)]
-                else:
-                    mixed = [high[:, :fine].astype(jnp.float32), low[:, :fine].astype(jnp.float32)]
-                    parts = [(first, high), (depth + first, jnp.concatenate(mixed, axis=1).astype(jnp.bfloat16))]
-                for at, part in parts:
-                    left_ref[group, :, at : at + LANES] = part
+                left_ref[group, :rows, first : first + LANES] = high
+                left_ref[group, rows:, first : first + LANES] = low
+                if fine < LANES:
+                    lane = lax.broadcasted_iota(jnp.int32, high.shape, 1)
+                    high = jnp.where(lane < fine, high.astype(jnp.float32), 0.0).astype(jnp.bfloat16)
+                left_ref[group, :rows, depth + first : depth + first + LANES] = high
+                left_ref[group, rows:, depth + first : depth + first + LANES] = jnp.zeros_like(low)
 
     used = plan_ref[3, 0].astype(jnp.int32)
     sure = stations // 16
@@ -398,15 +399,10 @@
         left = left_ref[group]
         tables = [plan_ref[slot, group].astype(jnp.int32) for slot in range(2)]
         phasor_rows = [pl.ds(pl.multiple_of(table * NF, NF), NF) for table in tables]
-        fine = FINE * 8
         for first in range(0, nodes, chunk):
             at = slice(first, first + chunk)
-            right = [
-                basis_ref[: depth + fine, at],
-                basis_ref[LANES:fine, at],
-                basis_ref[:LANES, at],
-            ]
-            got = jnp.dot(left, jnp.concatenate(right, axis=0), preferred_element_type=jnp.float32)
+            got = jnp.dot(left, basis_ref[:, at], preferred_element_type=jnp.float32)
+            got = got[: 2 * lanes] + got[2 * lanes :]
             next(steps, None)
             for win in range(windows):
                 row = win * 2 * NF
@@ -420,6 +416,8 @@
                 sums_ref[row : row + NF, at], sums_ref[row + NF : row + 2 * NF, at] = real_sum, imag_sum
         run(steps)
 
+    for ref in (basis_a, basis_b):
+        ref[depth + FINE * 8 :, :] = jnp.zeros((depth - FINE * 8, nodes), jnp.bfloat16)
     run(basis_steps(0, basis_a))
     for copy in copies[3:]:
         copy.wait()
@@ -530,7 +528,7 @@
     places = (stations // 8 + ntab // 2 + 2) // 2 * 16
     half = jax.ShapeDtypeStruct((NF, nodes), jnp.float32)
     rows = 2 * windows * 2 * NF
-    basis = pltpu.VMEM(((DEGREES + FINE) * 8, nodes), jnp.bfloat16)
+    basis = pltpu.VMEM((2 * DEGREES * 8, nodes), jnp.bfloat16)
     part = jax.ShapeDtypeStruct((NF // PARTS, nodes), jnp.float32)
     keep, *sends = pl.pallas_call(
         functools.partial(image_kernel, merged, stations_dev),
@@ -546,7 +544,7 @@
             pltpu.SemaphoreType.DMA((3 + ntab // 2,)),
             pltpu.VMEM((places, nodes), jnp.float32),
             pltpu.VMEM((places, rows), jnp.float32),
-            pltpu.VMEM((places // 8, rows, (DEGREES + 2 * FINE) * 8), jnp.bfloat16),
+            pltpu.VMEM((places // 8, 2 * rows, 2 * DEGREES * 8), jnp.bfloat16),
             pltpu.VMEM((rows // 2, nodes), jnp.float32),
             basis,
             basis,

time: 37 us -> 36.2 us (0.978)
  starting transfers between devices: 9.41 us -> 8.39 us
  Pallas kernels: 20.3 us -> 19.8 us
  waiting for transfers between devices: 6.68 us -> 7.07 us
    ppermute x2 -> x1, starting transfers between devices: 2.09 us -> 1.08 us  [on_device(): got = [lax.ppermute(send, 'win', [(0, 1), (1, 0)]) for send in sends]]
    pallas_call x1, Pallas kernels: 9.64 us -> 9.17 us  [on_device(): pl.pallas_call(functools.partial(image_kernel, merged, stations_dev), out...]
    ppermute x2 -> x1, waiting for transfers between devices: 2.89 us -> 3.25 us  [on_device(): got = [lax.ppermute(send, 'win', [(0, 1), (1, 0)]) for send in sends]]
  transfers between devices with their start and end apart: 3 -> 2, of which waited for: 3 -> 2; matrix products, arithmetic and copies ran while one was open for 0% -> 0% of each run, Pallas kernels for 21% -> 22%
where the time goes in v15:
time: 36.2 us; the launch traced here: 36 us
  Pallas kernels  19.8 us (55%)
  starting transfers between devices  8.39 us (23%)
  waiting for transfers between devices  7.07 us (20%)
  between operations  0.66 us (2%)
    pallas_call x1, Pallas kernels, on_device(): pl.pallas_call(functools.partial(image_kernel, merged, stations_dev), out...  9.17 us
    pallas_call x1, Pallas kernels, on_device(): pl.pallas_call(prepare_kernel, out_shape=jax.ShapeDtypeStruct(packed_shap...  7.88 us
    all_to_all x1, starting transfers between devices, on_device(): lax.all_to_all(blocks, ('win', 'sta', 'freq'), split_axis=0, concat_axis=...  7.31 us
    all_to_all x1, waiting for transfers between devices, on_device(): lax.all_to_all(blocks, ('win', 'sta', 'freq'), split_axis=0, concat_axis=...  3.81 us
    ppermute x1, waiting for transfers between devices, on_device(): got = [lax.ppermute(send, 'win', [(0, 1), (1, 0)]) for send in sends]  3.25 us
    pallas_call x1, Pallas kernels, on_device(): pl.pallas_call(functools.partial(send_kernel, nodes), out_shape=jax.Shape...  2.09 us
    ppermute x1, starting transfers between devices, on_device(): got = [lax.ppermute(send, 'win', [(0, 1), (1, 0)]) for send in sends]  1.08 us
  transfers between devices with their start and end apart: 2, of which 2 were waited for; matrix products, arithmetic and copies ran while one was open for 0% of the time, Pallas kernels for 22%

profile of v15, /device:TPU:0, one launch (start us, length us, event | category | flops | bytes accessed | tf_op | source)
XLA Modules:
  0.0 36.0 jit_solution(2784362417471775735)
XLA Ops:
  0.6 2.1 %send.1 = bf16[32,40,128]{2,1,0:T(8,128)(2,1)} custom-call(s32[1,16]{1,0:T(1,128)} %bitcast.5, bf16[16,2560]{1,0:T(8,128)(2,1)} %traces_hbm.1, bf16[16,32768]{1,0:T(8,128)(2,1)} %corr_hbm.1), custom_call_target="tpu_custom_call" | custom-call | tf_op jit(solution)/shard_map/send/pallas_call | solution.py:478
  2.7 7.3 %all-to-all-start = ((bf16[32,40,128]{2,1,0:T(8,128)(2,1)}), bf16[32,40,128]{2,1,0:T(8,128)(2,1)S(1)}, u32[]{:S(2)}, u32[]{:S(2)}) async-start(bf16[32,40,128]{2,1,0:T(8,128)(2,1)} %send.1), calls=%async_computation | async-start | bytes 655360 | tf_op jit(solution)/shard_map/all_to_all | solution.py:491
  10.0 7.9 %prepare.1.packed_hbm = f32[552,1024]{1,0:T(8,128)} custom-call(s32[1,16]{1,0:T(1,128)} %bitcast.6, s32[1,128]{1,0:T(1,128)} %bitcast.7, s32[256,128]{1,0:T(8,128)} %bitcast.4, f32[16,32768]{1,0:T(8,128)} %tables_hbm.1), custom_call_target="tpu_custom_call" | custom-call | tf_op jit(solution)/shard_map/prepare/pallas_call | solution.py:505
  17.9 3.8 %all-to-all-done.block_ref = bf16[32,40,128]{2,1,0:T(8,128)(2,1)S(1)} async-done(((bf16[32,40,128]{2,1,0:T(8,128)(2,1)}), bf16[32,40,128]{2,1,0:T(8,128)(2,1)S(1)}, u32[]{:S(2)}, u32[]{:S(2)}) %all-to-all-start) | async-done | bytes 327712 | tf_op jit(solution)/shard_map/all_to_all | solution.py:491
  21.8 9.2 %image.1 = (f32[16,1024]{1,0:T(8,128)S(1)}, f32[16,1024]{1,0:T(8,128)S(1)}) custom-call(f32[552,1024]{1,0:T(8,128)} %prepare.1.packed_hbm, bf16[32,40,128]{2,1,0:T(8,128)(2,1)S(1)} %all-to-all-done.block_ref), custom_call_target="tpu_custom_call" | custom-call | tf_op jit(solution)/shard_map/image/pallas_call | solution.py:533
  30.9 1.1 %collective-permute-start = (f32[16,1024]{1,0:T(8,128)S(1)}, f32[16,1024]{1,0:T(8,128)S(1)}, u32[]{:S(2)}, u32[]{:S(2)}) collective-permute-start(f32[16,1024]{1,0:T(8,128)S(1)} %get-tuple-element.7), channel_id=1, source_target_pairs={{0,16},{16,0},{1,17},{17,1},{2,18},{18,2},{3,19},{19,3},{4,20},{20... | collective-permute-start | bytes 196616 | tf_op jit(solution)/shard_map/ppermute | solution.py:555
  32.0 3.3 %collective-permute-done.rest_0_ = f32[16,1024]{1,0:T(8,128)S(1)} collective-permute-done((f32[16,1024]{1,0:T(8,128)S(1)}, f32[16,1024]{1,0:T(8,128)S(1)}, u32[]{:S(2)}, u32[]{:S(2)}) %collective-permute-start) | collective-permute-done | bytes 65568 | tf_op jit(solution)/shard_map/ppermute | solution.py:555
  35.3 0.7 %finish.1 = (f32[16,2048]{1,0:T(8,128)}, f32[1,2048]{1,0:T(1,128)}) custom-call(f32[16,1024]{1,0:T(8,128)S(1)} %get-tuple-element.6.keep_ref, f32[16,1024]{1,0:T(8,128)S(1)} %collective-permute-done.rest_0_), custom_call_target="tpu_custom_call" | custom-call | tf_op jit(solution)/shard_map/finish/pallas_call | solution.py:556
Async XLA Ops:
  2.7 19.0 %all-to-all-start = ((bf16[32,40,128]{2,1,0:T(8,128)(2,1)}), bf16[32,40,128]{2,1,0:T(8,128)(2,1)S(1)}, u32[]{:S(2)}, u32[]{:S(2)}) async-start(bf16[32,40,128]{2,1,0:T(8,128)(2,1)} %send.1), calls=%async_computation | async-start | bytes 655360 | tf_op jit(solution)/shard_map/all_to_all | solution.py:491
  30.9 4.3 %collective-permute-start = (f32[16,1024]{1,0:T(8,128)S(1)}, f32[16,1024]{1,0:T(8,128)S(1)}, u32[]{:S(2)}, u32[]{:S(2)}) collective-permute-start(f32[16,1024]{1,0:T(8,128)S(1)} %get-tuple-element.7), channel_id=1, source_target_pairs={{0,16},{16,0},{1,17},{17,1},{2,18},{18,2},{3,19},{19,3},{4,20},{20... | collective-permute-start | bytes 196616 | tf_op jit(solution)/shard_map/ppermute | solution.py:555

commit v16 on v13

--- a/solution.py
+++ b/solution.py
@@ -17,6 +17,7 @@
 FINE = 24
 REACH = 1.5
 TABLE_PIECES = 4
+ROUNDER = 1.5 * 2.0**15
 VMEM_LIMIT = 64 * 1024 * 1024 - 64 * 1024
 
 
@@ -91,8 +92,7 @@
         for piece in range(pieces):
             at = pl.multiple_of(first + (place * pieces + piece) * LANES, LANES)
             to = out_ref.at[dev, pl.ds(piece * stations_dev, stations_dev), :]
-            sem = sems.at[2 + dev * pieces + piece]
-            copies.append(pltpu.make_async_copy(corr_hbm.at[:, pl.ds(at, LANES)], to, sem))
+            copies.append(pltpu.make_async_copy(corr_hbm.at[:, pl.ds(at, LANES)], to, sems.at[2]))
     start_all(copies)
     start = lax.axis_index("freq") * half_length
     small[0].wait()
@@ -115,8 +115,9 @@
     tile = tile.astype(jnp.bfloat16)
     for dev in range(devices):
         out_ref[dev, height - 8 :, :] = tile
-    for copy in copies:
-        copy.wait()
+    if copies:
+        filled = out_ref.at[:, pl.ds(0, height - 8), :]
+        pltpu.make_async_copy(filled, filled, sems.at[2]).wait()
 
 
 def own_place():
@@ -380,9 +381,11 @@
         before, now = jnp.ones_like(arg), arg
         for degree in range(0, DEGREES, 2):
             pair = jnp.concatenate([before, now], axis=0)
-            terms = split_bf16(pair, 2 if degree < FINE else 1)
-            for term, value in enumerate(terms):
-                basis_ref[term * depth + degree * 8 : term * depth + degree * 8 + 16, :] = value
+            if degree < FINE:
+                high = (pair + ROUNDER) - ROUNDER
+                basis_ref[depth + degree * 8 : depth + degree * 8 + 16, :] = (pair - high).astype(jnp.bfloat16)
+                pair = high
+            basis_ref[degree * 8 : degree * 8 + 16, :] = pair.astype(jnp.bfloat16)
             before = twice * now - before
             now = twice * before - now
             if degree % 8 == 6:
@@ -480,7 +483,7 @@
         scratch_shapes=[
             bins_scratch,
             pltpu.VMEM(traces.shape, traces.dtype),
-            pltpu.SemaphoreType.DMA((2 + devices * max(pieces, 1),)),
+            pltpu.SemaphoreType.DMA((3,)),
         ],
         compiler_params=params(0),
         name="send",

time: 37.4 us -> 37.5 us (level)
    pallas_call x1, Pallas kernels: 9.64 us -> 10.4 us  [on_device(): pl.pallas_call(functools.partial(image_kernel, merged, stations_dev), out...]
    pallas_call x1, Pallas kernels: 2.75 us -> 2.09 us  [on_device(): pl.pallas_call(functools.partial(send_kernel, nodes), out_shape=jax.Shape...]
where the time goes in v16:
time: 37.5 us; the launch traced here: 37.2 us
  Pallas kernels  21.1 us (56%)
  starting transfers between devices  8.38 us (22%)
  waiting for transfers between devices  7.08 us (19%)
  between operations  0.66 us (2%)
    pallas_call x1, Pallas kernels, on_device(): pl.pallas_call(functools.partial(image_kernel, merged, stations_dev), out...  10.4 us
    pallas_call x1, Pallas kernels, on_device(): pl.pallas_call(prepare_kernel, out_shape=jax.ShapeDtypeStruct(packed_shap...  7.88 us
    all_to_all x1, starting transfers between devices, on_device(): lax.all_to_all(blocks, ('win', 'sta', 'freq'), split_axis=0, concat_axis=...  7.31 us
    all_to_all x1, waiting for transfers between devices, on_device(): lax.all_to_all(blocks, ('win', 'sta', 'freq'), split_axis=0, concat_axis=...  3.81 us
    ppermute x1, waiting for transfers between devices, on_device(): got = lax.ppermute(send, 'win', [(0, 1), (1, 0)])  3.26 us
    pallas_call x1, Pallas kernels, on_device(): pl.pallas_call(functools.partial(send_kernel, nodes), out_shape=jax.Shape...  2.09 us
    ppermute x1, starting transfers between devices, on_device(): got = lax.ppermute(send, 'win', [(0, 1), (1, 0)])  1.07 us
  transfers between devices with their start and end apart: 2, of which 2 were waited for; matrix products, arithmetic and copies ran while one was open for 0% of the time, Pallas kernels for 21%

profile of v16, /device:TPU:0, one launch (start us, length us, event | category | flops | bytes accessed | tf_op | source)
XLA Modules:
  0.0 37.2 jit_solution(6036577293682215526)
XLA Ops:
  0.6 2.1 %send.1 = bf16[32,40,128]{2,1,0:T(8,128)(2,1)} custom-call(s32[1,16]{1,0:T(1,128)} %bitcast.5, bf16[16,2560]{1,0:T(8,128)(2,1)} %traces_hbm.1, bf16[16,32768]{1,0:T(8,128)(2,1)} %corr_hbm.1), custom_call_target="tpu_custom_call" | custom-call | tf_op jit(solution)/shard_map/send/pallas_call | solution.py:478
  2.7 7.3 %all-to-all-start = ((bf16[32,40,128]{2,1,0:T(8,128)(2,1)}), bf16[32,40,128]{2,1,0:T(8,128)(2,1)S(1)}, u32[]{:S(2)}, u32[]{:S(2)}) async-start(bf16[32,40,128]{2,1,0:T(8,128)(2,1)} %send.1), calls=%async_computation | async-start | bytes 655360 | tf_op jit(solution)/shard_map/all_to_all | solution.py:491
  10.0 7.9 %prepare.1.packed_hbm = f32[552,1024]{1,0:T(8,128)} custom-call(s32[1,16]{1,0:T(1,128)} %bitcast.6, s32[1,128]{1,0:T(1,128)} %bitcast.7, s32[256,128]{1,0:T(8,128)} %bitcast.4, f32[16,32768]{1,0:T(8,128)} %tables_hbm.1), custom_call_target="tpu_custom_call" | custom-call | tf_op jit(solution)/shard_map/prepare/pallas_call | solution.py:505
  17.9 3.8 %all-to-all-done.block_ref = bf16[32,40,128]{2,1,0:T(8,128)(2,1)S(1)} async-done(((bf16[32,40,128]{2,1,0:T(8,128)(2,1)}), bf16[32,40,128]{2,1,0:T(8,128)(2,1)S(1)}, u32[]{:S(2)}, u32[]{:S(2)}) %all-to-all-start) | async-done | bytes 327712 | tf_op jit(solution)/shard_map/all_to_all | solution.py:491
  21.8 10.4 %image.1 = (f32[16,1024]{1,0:T(8,128)S(1)}, f32[16,1024]{1,0:T(8,128)S(1)}) custom-call(f32[552,1024]{1,0:T(8,128)} %prepare.1.packed_hbm, bf16[32,40,128]{2,1,0:T(8,128)(2,1)S(1)} %all-to-all-done.block_ref), custom_call_target="tpu_custom_call" | custom-call | tf_op jit(solution)/shard_map/image/pallas_call | solution.py:532
  32.2 1.1 %collective-permute-start = (f32[16,1024]{1,0:T(8,128)S(1)}, f32[16,1024]{1,0:T(8,128)S(1)}, u32[]{:S(2)}, u32[]{:S(2)}) collective-permute-start(f32[16,1024]{1,0:T(8,128)S(1)} %get-tuple-element.7), channel_id=1, source_target_pairs={{0,16},{16,0},{1,17},{17,1},{2,18},{18,2},{3,19},{19,3},{4,20},{20... | collective-permute-start | bytes 196616 | tf_op jit(solution)/shard_map/ppermute | solution.py:554
  33.3 3.3 %collective-permute-done.got_ref = f32[16,1024]{1,0:T(8,128)S(1)} collective-permute-done((f32[16,1024]{1,0:T(8,128)S(1)}, f32[16,1024]{1,0:T(8,128)S(1)}, u32[]{:S(2)}, u32[]{:S(2)}) %collective-permute-start) | collective-permute-done | bytes 65568 | tf_op jit(solution)/shard_map/ppermute | solution.py:554
  36.5 0.7 %finish.1 = (f32[16,2048]{1,0:T(8,128)}, f32[1,2048]{1,0:T(1,128)}) custom-call(f32[16,1024]{1,0:T(8,128)S(1)} %get-tuple-element.6.keep_ref, f32[16,1024]{1,0:T(8,128)S(1)} %collective-permute-done.got_ref), custom_call_target="tpu_custom_call" | custom-call | tf_op jit(solution)/shard_map/finish/pallas_call | solution.py:555
Async XLA Ops:
  2.7 19.0 %all-to-all-start = ((bf16[32,40,128]{2,1,0:T(8,128)(2,1)}), bf16[32,40,128]{2,1,0:T(8,128)(2,1)S(1)}, u32[]{:S(2)}, u32[]{:S(2)}) async-start(bf16[32,40,128]{2,1,0:T(8,128)(2,1)} %send.1), calls=%async_computation | async-start | bytes 655360 | tf_op jit(solution)/shard_map/all_to_all | solution.py:491
  32.2 4.3 %collective-permute-start = (f32[16,1024]{1,0:T(8,128)S(1)}, f32[16,1024]{1,0:T(8,128)S(1)}, u32[]{:S(2)}, u32[]{:S(2)}) collective-permute-start(f32[16,1024]{1,0:T(8,128)S(1)} %get-tuple-element.7), channel_id=1, source_target_pairs={{0,16},{16,0},{1,17},{17,1},{2,18},{18,2},{3,19},{19,3},{4,20},{20... | collective-permute-start | bytes 196616 | tf_op jit(solution)/shard_map/ppermute | solution.py:554

commit v17 on v16

--- a/solution.py
+++ b/solution.py
@@ -17,7 +17,6 @@
 FINE = 24
 REACH = 1.5
 TABLE_PIECES = 4
-ROUNDER = 1.5 * 2.0**15
 VMEM_LIMIT = 64 * 1024 * 1024 - 64 * 1024
 
 
@@ -152,7 +151,7 @@
     return found
 
 
-def chebyshev_coefs(bins_ref):
+def product_coefs(bins_ref):
     shape = (DEGREES, DEGREES)
     degree = lax.broadcasted_iota(jnp.int32, shape, 0)
     node = lax.broadcasted_iota(jnp.int32, shape, 1)
@@ -167,7 +166,12 @@
     spot, _ = cos_sin((2.0 * at + 1.0) * (1.0 / period))
     cosine, sine = cos_sin(bins * (spot * (REACH / 256.0)))
     dot = functools.partial(jnp.dot, precision=lax.Precision.HIGHEST, preferred_element_type=jnp.float32)
-    return dot(even, cosine) + dot(odd, sine)
+    coefs = dot(even, cosine) + dot(odd, sine)
+    for first in range(DEGREES - 8, 0, -8):
+        mirror = (degree + node == 2 * first) & (node > first) & (node < first + 8)
+        coefs = coefs - dot(jnp.where(mirror, 1.0, 0.0), coefs)
+    twice = (at >= 8.0) & ((at.astype(jnp.int32) & 7) != 0)
+    return jnp.where(twice, 2.0 * coefs, coefs)
 
 
 def station_plan(table_row, width):
@@ -235,7 +239,7 @@
     for copy in ins:
         copy.wait()
     cos_at, sin_at, coef_at, plan_at = packed_rows(ntab)
-    coef_ref[...] = chebyshev_coefs(bins_ref)
+    coef_ref[...] = product_coefs(bins_ref)
     plan_ref[...] = station_plan(table_ref[...], plan_ref.shape[1])
     outs = start_all(
         [
@@ -375,27 +379,25 @@
     else:
         lax.fori_loop(0, sure, lambda pair, carry: (make_left(pair), carry)[1], 0)
     lax.fori_loop(sure, (used + 1) // 2, lambda pair, carry: (make_left(pair), carry)[1], 0)
-    def basis_steps(group, basis_ref):
-        arg = place_ref[pl.ds(pl.multiple_of(group * 8, 8), 8), :]
+    def make_basis(group, basis_ref, at):
+        arg = place_ref[pl.ds(pl.multiple_of(group * 8, 8), 8), at]
         twice = arg + arg
-        before, now = jnp.ones_like(arg), arg
+        low = [jnp.ones_like(arg), arg]
+        while len(low) < 8:
+            low.append(twice * low[-1] - low[-2])
+        eight = (low[4] + low[4]) * low[4] - 1.0
+        sixteen = (eight + eight) * eight - 1.0
+        steps = [None, eight, sixteen, (sixteen + sixteen - 1.0) * eight]
         for degree in range(0, DEGREES, 2):
-            pair = jnp.concatenate([before, now], axis=0)
-            if degree < FINE:
-                high = (pair + ROUNDER) - ROUNDER
-                basis_ref[depth + degree * 8 : depth + degree * 8 + 16, :] = (pair - high).astype(jnp.bfloat16)
-                pair = high
-            basis_ref[degree * 8 : degree * 8 + 16, :] = pair.astype(jnp.bfloat16)
-            before = twice * now - before
-            now = twice * before - now
-            if degree % 8 == 6:
-                yield
-
-    def run(steps):
-        for _ in steps:
-            pass
-
-    def add_group(group, basis_ref, steps):
+            pair = []
+            for factor in low[degree % 8 : degree % 8 + 2]:
+                step = steps[degree // 8]
+                pair.append(factor if step is None else step if factor is low[0] else factor * step)
+            pair = jnp.concatenate(pair, axis=0)
+            for term, value in enumerate(split_bf16(pair, 2 if degree < FINE else 1)):
+                basis_ref[term * depth + degree * 8 : term * depth + degree * 8 + 16, at] = value
+
+    def add_group(group, basis_ref, next_basis):
         left = left_ref[group]
         tables = [plan_ref[slot, group].astype(jnp.int32) for slot in range(2)]
         phasor_rows = [pl.ds(pl.multiple_of(table * NF, NF), NF) for table in tables]
@@ -408,7 +410,8 @@
                 basis_ref[:LANES, at],
             ]
             got = jnp.dot(left, jnp.concatenate(right, axis=0), preferred_element_type=jnp.float32)
-            next(steps, None)
+            if next_basis is not None:
+                make_basis(group + 1, next_basis, at)
             for win in range(windows):
                 row = win * 2 * NF
                 real_sum, imag_sum = sums_ref[row : row + NF, at], sums_ref[row + NF : row + 2 * NF, at]
@@ -419,23 +422,23 @@
                     real_sum += real * cosine - imag * sine
                     imag_sum += real * sine + imag * cosine
                 sums_ref[row : row + NF, at], sums_ref[row + NF : row + 2 * NF, at] = real_sum, imag_sum
-        run(steps)
-
-    run(basis_steps(0, basis_a))
+
+    for first in range(0, nodes, chunk):
+        make_basis(0, basis_a, slice(first, first + chunk))
     for copy in copies[3:]:
         copy.wait()
 
     def body(pair, carry):
         group = pair * 2
-        add_group(group, basis_a, basis_steps(group + 1, basis_b))
-        add_group(group + 1, basis_b, basis_steps(jnp.minimum(group + 2, places // 8 - 1), basis_a))
+        add_group(group, basis_a, basis_b)
+        add_group(group + 1, basis_b, basis_a)
         return carry
 
     lax.fori_loop(0, used // 2, body, 0)
 
     @pl.when(used % 2 == 1)
     def _():
-        add_group(used - 1, basis_a, iter(()))
+        add_group(used - 1, basis_a, None)
 
     powers = []
     for win in range(windows):
@@ -525,7 +528,7 @@
         name="prepare",
     )(bins, station_table.reshape(1, stations), node_ids.reshape(grid // LANES, LANES), tables)
 
-    places = (stations // 8 + ntab // 2 + 2) // 2 * 16
+    places = (stations // 8 + ntab // 2 + 3) // 2 * 16
     half = jax.ShapeDtypeStruct((NF, nodes), jnp.float32)
     rows = 2 * windows * 2 * NF
     basis = pltpu.VMEM(((DEGREES + FINE) * 8, nodes), jnp.bfloat16)

time: 37.5 us -> 36.8 us (0.981)
  waiting for transfers between devices: 7.08 us -> 6.69 us
    pallas_call x1, Pallas kernels: 10.4 us -> 9.77 us  [on_device(): pl.pallas_call(functools.partial(image_kernel, merged, stations_dev), out...]
    pallas_call x1, Pallas kernels: 7.88 us -> 8.26 us  [on_device(): pl.pallas_call(prepare_kernel, out_shape=jax.ShapeDtypeStruct(packed_shap...]
    all_to_all x1, waiting for transfers between devices: 3.81 us -> 3.43 us  [on_device(): lax.all_to_all(blocks, ('win', 'sta', 'freq'), split_axis=0, concat_axis=...]
  transfers between devices with their start and end apart: 2 -> 2, of which waited for: 2 -> 2; matrix products, arithmetic and copies ran while one was open for 0% -> 0% of each run, Pallas kernels for 21% -> 23%
where the time goes in v17:
time: 36.8 us; the launch traced here: 36.6 us
  Pallas kernels  20.8 us (57%)
  starting transfers between devices  8.38 us (23%)
  waiting for transfers between devices  6.69 us (18%)
  between operations  0.66 us (2%)
    pallas_call x1, Pallas kernels, on_device(): pl.pallas_call(functools.partial(image_kernel, merged, stations_dev), out...  9.77 us
    pallas_call x1, Pallas kernels, on_device(): pl.pallas_call(prepare_kernel, out_shape=jax.ShapeDtypeStruct(packed_shap...  8.26 us
    all_to_all x1, starting transfers between devices, on_device(): lax.all_to_all(blocks, ('win', 'sta', 'freq'), split_axis=0, concat_axis=...  7.31 us
    all_to_all x1, waiting for transfers between devices, on_device(): lax.all_to_all(blocks, ('win', 'sta', 'freq'), split_axis=0, concat_axis=...  3.43 us
    ppermute x1, waiting for transfers between devices, on_device(): got = lax.ppermute(send, 'win', [(0, 1), (1, 0)])  3.26 us
    pallas_call x1, Pallas kernels, on_device(): pl.pallas_call(functools.partial(send_kernel, nodes), out_shape=jax.Shape...  2.09 us
    ppermute x1, starting transfers between devices, on_device(): got = lax.ppermute(send, 'win', [(0, 1), (1, 0)])  1.07 us
  transfers between devices with their start and end apart: 2, of which 2 were waited for; matrix products, arithmetic and copies ran while one was open for 0% of the time, Pallas kernels for 23%

profile of v17, /device:TPU:0, one launch (start us, length us, event | category | flops | bytes accessed | tf_op | source)
XLA Modules:
  0.0 36.6 jit_solution(14308179729869913949)
XLA Ops:
  0.6 2.1 %send.1 = bf16[32,40,128]{2,1,0:T(8,128)(2,1)} custom-call(s32[1,16]{1,0:T(1,128)} %bitcast.5, bf16[16,2560]{1,0:T(8,128)(2,1)} %traces_hbm.1, bf16[16,32768]{1,0:T(8,128)(2,1)} %corr_hbm.1), custom_call_target="tpu_custom_call" | custom-call | tf_op jit(solution)/shard_map/send/pallas_call | solution.py:481
  2.7 7.3 %all-to-all-start = ((bf16[32,40,128]{2,1,0:T(8,128)(2,1)}), bf16[32,40,128]{2,1,0:T(8,128)(2,1)S(1)}, u32[]{:S(2)}, u32[]{:S(2)}) async-start(bf16[32,40,128]{2,1,0:T(8,128)(2,1)} %send.1), calls=%async_computation | async-start | bytes 655360 | tf_op jit(solution)/shard_map/all_to_all | solution.py:494
  10.0 8.3 %prepare.1.packed_hbm = f32[552,1024]{1,0:T(8,128)} custom-call(s32[1,16]{1,0:T(1,128)} %bitcast.6, s32[1,128]{1,0:T(1,128)} %bitcast.7, s32[256,128]{1,0:T(8,128)} %bitcast.4, f32[16,32768]{1,0:T(8,128)} %tables_hbm.1), custom_call_target="tpu_custom_call" | custom-call | tf_op jit(solution)/shard_map/prepare/pallas_call | solution.py:508
  18.3 3.4 %all-to-all-done.block_ref = bf16[32,40,128]{2,1,0:T(8,128)(2,1)S(1)} async-done(((bf16[32,40,128]{2,1,0:T(8,128)(2,1)}), bf16[32,40,128]{2,1,0:T(8,128)(2,1)S(1)}, u32[]{:S(2)}, u32[]{:S(2)}) %all-to-all-start) | async-done | bytes 327712 | tf_op jit(solution)/shard_map/all_to_all | solution.py:494
  21.8 9.8 %image.1 = (f32[16,1024]{1,0:T(8,128)S(1)}, f32[16,1024]{1,0:T(8,128)S(1)}) custom-call(f32[552,1024]{1,0:T(8,128)} %prepare.1.packed_hbm, bf16[32,40,128]{2,1,0:T(8,128)(2,1)S(1)} %all-to-all-done.block_ref), custom_call_target="tpu_custom_call" | custom-call | tf_op jit(solution)/shard_map/image/pallas_call | solution.py:535
  31.5 1.1 %collective-permute-start = (f32[16,1024]{1,0:T(8,128)S(1)}, f32[16,1024]{1,0:T(8,128)S(1)}, u32[]{:S(2)}, u32[]{:S(2)}) collective-permute-start(f32[16,1024]{1,0:T(8,128)S(1)} %get-tuple-element.7), channel_id=1, source_target_pairs={{0,16},{16,0},{1,17},{17,1},{2,18},{18,2},{3,19},{19,3},{4,20},{20... | collective-permute-start | bytes 196616 | tf_op jit(solution)/shard_map/ppermute | solution.py:557
  32.6 3.3 %collective-permute-done.got_ref = f32[16,1024]{1,0:T(8,128)S(1)} collective-permute-done((f32[16,1024]{1,0:T(8,128)S(1)}, f32[16,1024]{1,0:T(8,128)S(1)}, u32[]{:S(2)}, u32[]{:S(2)}) %collective-permute-start) | collective-permute-done | bytes 65568 | tf_op jit(solution)/shard_map/ppermute | solution.py:557
  35.9 0.7 %finish.1 = (f32[16,2048]{1,0:T(8,128)}, f32[1,2048]{1,0:T(1,128)}) custom-call(f32[16,1024]{1,0:T(8,128)S(1)} %get-tuple-element.6.keep_ref, f32[16,1024]{1,0:T(8,128)S(1)} %collective-permute-done.got_ref), custom_call_target="tpu_custom_call" | custom-call | tf_op jit(solution)/shard_map/finish/pallas_call | solution.py:558
Async XLA Ops:
  2.7 19.0 %all-to-all-start = ((bf16[32,40,128]{2,1,0:T(8,128)(2,1)}), bf16[32,40,128]{2,1,0:T(8,128)(2,1)S(1)}, u32[]{:S(2)}, u32[]{:S(2)}) async-start(bf16[32,40,128]{2,1,0:T(8,128)(2,1)} %send.1), calls=%async_computation | async-start | bytes 655360 | tf_op jit(solution)/shard_map/all_to_all | solution.py:494
  31.5 4.3 %collective-permute-start = (f32[16,1024]{1,0:T(8,128)S(1)}, f32[16,1024]{1,0:T(8,128)S(1)}, u32[]{:S(2)}, u32[]{:S(2)}) collective-permute-start(f32[16,1024]{1,0:T(8,128)S(1)} %get-tuple-element.7), channel_id=1, source_target_pairs={{0,16},{16,0},{1,17},{17,1},{2,18},{18,2},{3,19},{19,3},{4,20},{20... | collective-permute-start | bytes 196616 | tf_op jit(solution)/shard_map/ppermute | solution.py:557

commit v18 on v17

--- a/solution.py
+++ b/solution.py
@@ -273,7 +273,7 @@
 def image_kernel(merged, stations_dev, packed_hbm, block_ref, *rest):
     corr_ref, rest = (None, rest) if merged else (rest[0], rest[1:])
     keep_ref, send_ref, plan_ref, place_of_ref, coef_ref, cos_ref, sin_ref, sems = rest[:8]
-    place_ref, weight_ref, left_ref, sums_ref, basis_a, basis_b = rest[8:]
+    place_ref, weight_ref, left_ref, sums_ref = rest[8:]
     places, nodes = place_ref.shape
     windows, groups, cores = (lax.axis_size(a) for a in ("win", "sta", "freq"))
     stations = stations_dev * groups
@@ -340,6 +340,7 @@
     for copy in copies[1:3]:
         copy.wait()
 
+    rows = 2 * lanes
     spot = (lax.broadcasted_iota(jnp.int32, (lanes, LANES), 1) & 7).astype(jnp.float32)
 
     def make_left(pair):
@@ -363,13 +364,13 @@
                 value = turned[which * lanes : (which + 1) * lanes]
                 value = jnp.concatenate([jnp.where(mask, value, 0.0), jnp.where(mask, 0.0, value)], axis=0)
                 high, low = split_bf16(value, 2)
-                if fine == LANES:
-                    parts = [(first, high), (depth + first, high), (2 * FINE * 8 + first + LANES, low)]
-                else:
-                    mixed = [high[:, :fine].astype(jnp.float32), low[:, :fine].astype(jnp.float32)]
-                    parts = [(first, high), (depth + first, jnp.concatenate(mixed, axis=1).astype(jnp.bfloat16))]
-                for at, part in parts:
-                    left_ref[group, :, at : at + LANES] = part
+                left_ref[group, :rows, first : first + LANES] = high
+                left_ref[group, rows:, first : first + LANES] = low
+                if fine < LANES:
+                    lane = lax.broadcasted_iota(jnp.int32, high.shape, 1)
+                    high = jnp.where(lane < fine, high.astype(jnp.float32), 0.0).astype(jnp.bfloat16)
+                left_ref[group, :rows, depth + first : depth + first + LANES] = high
+                left_ref[group, rows:, depth + first : depth + first + LANES] = jnp.zeros_like(low)
 
     used = plan_ref[3, 0].astype(jnp.int32)
     sure = stations // 16
@@ -379,7 +380,7 @@
     else:
         lax.fori_loop(0, sure, lambda pair, carry: (make_left(pair), carry)[1], 0)
     lax.fori_loop(sure, (used + 1) // 2, lambda pair, carry: (make_left(pair), carry)[1], 0)
-    def make_basis(group, basis_ref, at):
+    def basis_of(group, at):
         arg = place_ref[pl.ds(pl.multiple_of(group * 8, 8), 8), at]
         twice = arg + arg
         low = [jnp.ones_like(arg), arg]
@@ -388,6 +389,7 @@
         eight = (low[4] + low[4]) * low[4] - 1.0
         sixteen = (eight + eight) * eight - 1.0
         steps = [None, eight, sixteen, (sixteen + sixteen - 1.0) * eight]
+        terms = [[], []]
         for degree in range(0, DEGREES, 2):
             pair = []
             for factor in low[degree % 8 : degree % 8 + 2]:
@@ -395,23 +397,18 @@
                 pair.append(factor if step is None else step if factor is low[0] else factor * step)
             pair = jnp.concatenate(pair, axis=0)
             for term, value in enumerate(split_bf16(pair, 2 if degree < FINE else 1)):
-                basis_ref[term * depth + degree * 8 : term * depth + degree * 8 + 16, at] = value
-
-    def add_group(group, basis_ref, next_basis):
+                terms[term].append(value)
+        spare = jnp.zeros((depth - FINE * 8, chunk), jnp.bfloat16)
+        return jnp.concatenate(terms[0] + terms[1] + [spare], axis=0)
+
+    def add_group(group):
         left = left_ref[group]
         tables = [plan_ref[slot, group].astype(jnp.int32) for slot in range(2)]
         phasor_rows = [pl.ds(pl.multiple_of(table * NF, NF), NF) for table in tables]
-        fine = FINE * 8
         for first in range(0, nodes, chunk):
             at = slice(first, first + chunk)
-            right = [
-                basis_ref[: depth + fine, at],
-                basis_ref[LANES:fine, at],
-                basis_ref[:LANES, at],
-            ]
-            got = jnp.dot(left, jnp.concatenate(right, axis=0), preferred_element_type=jnp.float32)
-            if next_basis is not None:
-                make_basis(group + 1, next_basis, at)
+            got = jnp.dot(left, basis_of(group, at), preferred_element_type=jnp.float32)
+            got = got[: 2 * lanes] + got[2 * lanes :]
             for win in range(windows):
                 row = win * 2 * NF
                 real_sum, imag_sum = sums_ref[row : row + NF, at], sums_ref[row + NF : row + 2 * NF, at]
@@ -423,22 +420,19 @@
                     imag_sum += real * sine + imag * cosine
                 sums_ref[row : row + NF, at], sums_ref[row + NF : row + 2 * NF, at] = real_sum, imag_sum
 
-    for first in range(0, nodes, chunk):
-        make_basis(0, basis_a, slice(first, first + chunk))
     for copy in copies[3:]:
         copy.wait()
 
     def body(pair, carry):
-        group = pair * 2
-        add_group(group, basis_a, basis_b)
-        add_group(group + 1, basis_b, basis_a)
+        add_group(pair * 2)
+        add_group(pair * 2 + 1)
         return carry
 
     lax.fori_loop(0, used // 2, body, 0)
 
     @pl.when(used % 2 == 1)
     def _():
-        add_group(used - 1, basis_a, None)
+        add_group(used - 1)
 
     powers = []
     for win in range(windows):
@@ -531,7 +525,6 @@
     places = (stations // 8 + ntab // 2 + 3) // 2 * 16
     half = jax.ShapeDtypeStruct((NF, nodes), jnp.float32)
     rows = 2 * windows * 2 * NF
-    basis = pltpu.VMEM(((DEGREES + FINE) * 8, nodes), jnp.bfloat16)
     keep, send = pl.pallas_call(
         functools.partial(image_kernel, merged, stations_dev),
         out_shape=[half, half],
@@ -546,10 +539,8 @@
             pltpu.SemaphoreType.DMA((3 + ntab // 2,)),
             pltpu.VMEM((places, nodes), jnp.float32),
             pltpu.VMEM((places, rows), jnp.float32),
-            pltpu.VMEM((places // 8, rows, (DEGREES + 2 * FINE) * 8), jnp.bfloat16),
+            pltpu.VMEM((places // 8, 2 * rows, 2 * DEGREES * 8), jnp.bfloat16),
             pltpu.VMEM((rows // 2, nodes), jnp.float32),
-            basis,
-            basis,
         ],
         compiler_params=params(23 * 512 * 1024),
         name="image",

time: 36.8 us -> 36.4 us (0.989)
  Pallas kernels: 20.8 us -> 20.3 us
    pallas_call x1, Pallas kernels: 9.77 us -> 9.29 us  [on_device(): pl.pallas_call(functools.partial(image_kernel, merged, stations_dev), out...]
where the time goes in v18:
time: 36.4 us; the launch traced here: 36.1 us
  Pallas kernels  20.3 us (56%)
  starting transfers between devices  8.38 us (23%)
  waiting for transfers between devices  6.7 us (18%)
  between operations  0.66 us (2%)
    pallas_call x1, Pallas kernels, on_device(): pl.pallas_call(functools.partial(image_kernel, merged, stations_dev), out...  9.29 us
    pallas_call x1, Pallas kernels, on_device(): pl.pallas_call(prepare_kernel, out_shape=jax.ShapeDtypeStruct(packed_shap...  8.26 us
    all_to_all x1, starting transfers between devices, on_device(): lax.all_to_all(blocks, ('win', 'sta', 'freq'), split_axis=0, concat_axis=...  7.31 us
    all_to_all x1, waiting for transfers between devices, on_device(): lax.all_to_all(blocks, ('win', 'sta', 'freq'), split_axis=0, concat_axis=...  3.43 us
    ppermute x1, waiting for transfers between devices, on_device(): got = lax.ppermute(send, 'win', [(0, 1), (1, 0)])  3.26 us
    pallas_call x1, Pallas kernels, on_device(): pl.pallas_call(functools.partial(send_kernel, nodes), out_shape=jax.Shape...  2.09 us
    ppermute x1, starting transfers between devices, on_device(): got = lax.ppermute(send, 'win', [(0, 1), (1, 0)])  1.07 us
  transfers between devices with their start and end apart: 2, of which 2 were waited for; matrix products, arithmetic and copies ran while one was open for 0% of the time, Pallas kernels for 23%

profile of v18, /device:TPU:0, one launch (start us, length us, event | category | flops | bytes accessed | tf_op | source)
XLA Modules:
  0.0 36.1 jit_solution(8699954937255214351)
XLA Ops:
  0.6 2.1 %send.1 = bf16[32,40,128]{2,1,0:T(8,128)(2,1)} custom-call(s32[1,16]{1,0:T(1,128)} %bitcast.5, bf16[16,2560]{1,0:T(8,128)(2,1)} %traces_hbm.1, bf16[16,32768]{1,0:T(8,128)(2,1)} %corr_hbm.1), custom_call_target="tpu_custom_call" | custom-call | tf_op jit(solution)/shard_map/send/pallas_call | solution.py:475
  2.7 7.3 %all-to-all-start = ((bf16[32,40,128]{2,1,0:T(8,128)(2,1)}), bf16[32,40,128]{2,1,0:T(8,128)(2,1)S(1)}, u32[]{:S(2)}, u32[]{:S(2)}) async-start(bf16[32,40,128]{2,1,0:T(8,128)(2,1)} %send.1), calls=%async_computation | async-start | bytes 655360 | tf_op jit(solution)/shard_map/all_to_all | solution.py:488
  10.0 8.3 %prepare.1.packed_hbm = f32[552,1024]{1,0:T(8,128)} custom-call(s32[1,16]{1,0:T(1,128)} %bitcast.6, s32[1,128]{1,0:T(1,128)} %bitcast.7, s32[256,128]{1,0:T(8,128)} %bitcast.4, f32[16,32768]{1,0:T(8,128)} %tables_hbm.1), custom_call_target="tpu_custom_call" | custom-call | tf_op jit(solution)/shard_map/prepare/pallas_call | solution.py:502
  18.3 3.4 %all-to-all-done.block_ref = bf16[32,40,128]{2,1,0:T(8,128)(2,1)S(1)} async-done(((bf16[32,40,128]{2,1,0:T(8,128)(2,1)}), bf16[32,40,128]{2,1,0:T(8,128)(2,1)S(1)}, u32[]{:S(2)}, u32[]{:S(2)}) %all-to-all-start) | async-done | bytes 327712 | tf_op jit(solution)/shard_map/all_to_all | solution.py:488
  21.8 9.3 %image.1 = (f32[16,1024]{1,0:T(8,128)S(1)}, f32[16,1024]{1,0:T(8,128)S(1)}) custom-call(f32[552,1024]{1,0:T(8,128)} %prepare.1.packed_hbm, bf16[32,40,128]{2,1,0:T(8,128)(2,1)S(1)} %all-to-all-done.block_ref), custom_call_target="tpu_custom_call" | custom-call | tf_op jit(solution)/shard_map/image/pallas_call | solution.py:528
  31.1 1.1 %collective-permute-start = (f32[16,1024]{1,0:T(8,128)S(1)}, f32[16,1024]{1,0:T(8,128)S(1)}, u32[]{:S(2)}, u32[]{:S(2)}) collective-permute-start(f32[16,1024]{1,0:T(8,128)S(1)} %get-tuple-element.7), channel_id=1, source_target_pairs={{0,16},{16,0},{1,17},{17,1},{2,18},{18,2},{3,19},{19,3},{4,20},{20... | collective-permute-start | bytes 196616 | tf_op jit(solution)/shard_map/ppermute | solution.py:548
  32.1 3.3 %collective-permute-done.got_ref = f32[16,1024]{1,0:T(8,128)S(1)} collective-permute-done((f32[16,1024]{1,0:T(8,128)S(1)}, f32[16,1024]{1,0:T(8,128)S(1)}, u32[]{:S(2)}, u32[]{:S(2)}) %collective-permute-start) | collective-permute-done | bytes 65568 | tf_op jit(solution)/shard_map/ppermute | solution.py:548
  35.4 0.7 %finish.1 = (f32[16,2048]{1,0:T(8,128)}, f32[1,2048]{1,0:T(1,128)}) custom-call(f32[16,1024]{1,0:T(8,128)S(1)} %get-tuple-element.6.keep_ref, f32[16,1024]{1,0:T(8,128)S(1)} %collective-permute-done.got_ref), custom_call_target="tpu_custom_call" | custom-call | tf_op jit(solution)/shard_map/finish/pallas_call | solution.py:549
Async XLA Ops:
  2.7 19.0 %all-to-all-start = ((bf16[32,40,128]{2,1,0:T(8,128)(2,1)}), bf16[32,40,128]{2,1,0:T(8,128)(2,1)S(1)}, u32[]{:S(2)}, u32[]{:S(2)}) async-start(bf16[32,40,128]{2,1,0:T(8,128)(2,1)} %send.1), calls=%async_computation | async-start | bytes 655360 | tf_op jit(solution)/shard_map/all_to_all | solution.py:488
  31.1 4.3 %collective-permute-start = (f32[16,1024]{1,0:T(8,128)S(1)}, f32[16,1024]{1,0:T(8,128)S(1)}, u32[]{:S(2)}, u32[]{:S(2)}) collective-permute-start(f32[16,1024]{1,0:T(8,128)S(1)} %get-tuple-element.7), channel_id=1, source_target_pairs={{0,16},{16,0},{1,17},{17,1},{2,18},{18,2},{3,19},{19,3},{4,20},{20... | collective-permute-start | bytes 196616 | tf_op jit(solution)/shard_map/ppermute | solution.py:548

commit v19 on v18

--- a/solution.py
+++ b/solution.py
@@ -72,7 +72,7 @@
     return copies
 
 
-def send_kernel(nodes, bins_hbm, traces_hbm, corr_hbm, out_ref, bins_ref, traces_ref, sems):
+def send_kernel(nodes, bins_hbm, traces_hbm, corr_hbm, out_hbm, out_ref, bins_ref, traces_ref, sems):
     devices, height, _ = out_ref.shape
     stations_dev, half_length = traces_ref.shape
     pieces = (height - 8) // stations_dev
@@ -104,6 +104,15 @@
     scale = 1.0 / math.sqrt(NT)
     table = jnp.concatenate([(1.0 - versine) * scale, sine * -scale], axis=0)
     both = jnp.concatenate(split_bf16(table, 2), axis=0)
+    parts = [pl.ds(0, height - 8), pl.ds(height - 8, 8)]
+    outs = [
+        pltpu.make_async_copy(out_ref.at[:, part, :], out_hbm.at[:, part, :], sems.at[3 + at])
+        for at, part in enumerate(parts)
+    ]
+    if copies:
+        filled = out_ref.at[:, parts[0], :]
+        pltpu.make_async_copy(filled, filled, sems.at[2]).wait()
+        outs[0].start()
     small[1].wait()
     sums = lax.dot_general(
         both, traces_ref[...], (((1,), (1,)), ((), ())), preferred_element_type=jnp.float32
@@ -114,9 +123,9 @@
     tile = tile.astype(jnp.bfloat16)
     for dev in range(devices):
         out_ref[dev, height - 8 :, :] = tile
-    if copies:
-        filled = out_ref.at[:, pl.ds(0, height - 8), :]
-        pltpu.make_async_copy(filled, filled, sems.at[2]).wait()
+    outs[1].start()
+    for copy in outs if copies else outs[1:]:
+        copy.wait()
 
 
 def own_place():
@@ -340,7 +349,6 @@
     for copy in copies[1:3]:
         copy.wait()
 
-    rows = 2 * lanes
     spot = (lax.broadcasted_iota(jnp.int32, (lanes, LANES), 1) & 7).astype(jnp.float32)
 
     def make_left(pair):
@@ -364,13 +372,13 @@
                 value = turned[which * lanes : (which + 1) * lanes]
                 value = jnp.concatenate([jnp.where(mask, value, 0.0), jnp.where(mask, 0.0, value)], axis=0)
                 high, low = split_bf16(value, 2)
-                left_ref[group, :rows, first : first + LANES] = high
-                left_ref[group, rows:, first : first + LANES] = low
-                if fine < LANES:
-                    lane = lax.broadcasted_iota(jnp.int32, high.shape, 1)
-                    high = jnp.where(lane < fine, high.astype(jnp.float32), 0.0).astype(jnp.bfloat16)
-                left_ref[group, :rows, depth + first : depth + first + LANES] = high
-                left_ref[group, rows:, depth + first : depth + first + LANES] = jnp.zeros_like(low)
+                if fine == LANES:
+                    parts = [(first, high), (depth + first, high), (2 * FINE * 8 + first + LANES, low)]
+                else:
+                    mixed = [high[:, :fine].astype(jnp.float32), low[:, :fine].astype(jnp.float32)]
+                    parts = [(first, high), (depth + first, jnp.concatenate(mixed, axis=1).astype(jnp.bfloat16))]
+                for at, part in parts:
+                    left_ref[group, :, at : at + LANES] = part
 
     used = plan_ref[3, 0].astype(jnp.int32)
     sure = stations // 16
@@ -398,8 +406,8 @@
             pair = jnp.concatenate(pair, axis=0)
             for term, value in enumerate(split_bf16(pair, 2 if degree < FINE else 1)):
                 terms[term].append(value)
-        spare = jnp.zeros((depth - FINE * 8, chunk), jnp.bfloat16)
-        return jnp.concatenate(terms[0] + terms[1] + [spare], axis=0)
+        high, low = terms
+        return jnp.concatenate(high + low + high[8 : FINE // 2] + high[:8], axis=0)
 
     def add_group(group):
         left = left_ref[group]
@@ -408,7 +416,6 @@
         for first in range(0, nodes, chunk):
             at = slice(first, first + chunk)
             got = jnp.dot(left, basis_of(group, at), preferred_element_type=jnp.float32)
-            got = got[: 2 * lanes] + got[2 * lanes :]
             for win in range(windows):
                 row = win * 2 * NF
                 real_sum, imag_sum = sums_ref[row : row + NF, at], sums_ref[row + NF : row + 2 * NF, at]
@@ -476,11 +483,12 @@
         functools.partial(send_kernel, nodes),
         out_shape=jax.ShapeDtypeStruct((devices, height, LANES), jnp.bfloat16),
         in_specs=[hbm] * 3,
-        out_specs=vmem,
+        out_specs=hbm,
         scratch_shapes=[
+            pltpu.VMEM((devices, height, LANES), jnp.bfloat16),
             bins_scratch,
             pltpu.VMEM(traces.shape, traces.dtype),
-            pltpu.SemaphoreType.DMA((3,)),
+            pltpu.SemaphoreType.DMA((5,)),
         ],
         compiler_params=params(0),
         name="send",
@@ -539,7 +547,7 @@
             pltpu.SemaphoreType.DMA((3 + ntab // 2,)),
             pltpu.VMEM((places, nodes), jnp.float32),
             pltpu.VMEM((places, rows), jnp.float32),
-            pltpu.VMEM((places // 8, 2 * rows, 2 * DEGREES * 8), jnp.bfloat16),
+            pltpu.VMEM((places // 8, rows, (DEGREES + 2 * FINE) * 8), jnp.bfloat16),
             pltpu.VMEM((rows // 2, nodes), jnp.float32),
         ],
         compiler_params=params(23 * 512 * 1024),

time: 36.4 us -> 35.9 us (0.986)
  Pallas kernels: 20.3 us -> 19.6 us
    pallas_call x1, Pallas kernels: 9.29 us -> 8.48 us  [on_device(): pl.pallas_call(functools.partial(image_kernel, merged, stations_dev), out...]
where the time goes in v19:
time: 35.9 us; the launch traced here: 35.3 us
  Pallas kernels  19.6 us (55%)
  starting transfers between devices  8.37 us (23%)
  waiting for transfers between devices  6.7 us (19%)
  between operations  0.66 us (2%)
    pallas_call x1, Pallas kernels, on_device(): pl.pallas_call(functools.partial(image_kernel, merged, stations_dev), out...  8.48 us
    pallas_call x1, Pallas kernels, on_device(): pl.pallas_call(prepare_kernel, out_shape=jax.ShapeDtypeStruct(packed_shap...  8.26 us
    all_to_all x1, starting transfers between devices, on_device(): lax.all_to_all(blocks, ('win', 'sta', 'freq'), split_axis=0, concat_axis=...  7.3 us
    all_to_all x1, waiting for transfers between devices, on_device(): lax.all_to_all(blocks, ('win', 'sta', 'freq'), split_axis=0, concat_axis=...  3.43 us
    ppermute x1, waiting for transfers between devices, on_device(): got = lax.ppermute(send, 'win', [(0, 1), (1, 0)])  3.26 us
    pallas_call x1, Pallas kernels, on_device(): pl.pallas_call(functools.partial(send_kernel, nodes), out_shape=jax.Shape...  2.14 us
    ppermute x1, starting transfers between devices, on_device(): got = lax.ppermute(send, 'win', [(0, 1), (1, 0)])  1.07 us
  transfers between devices with their start and end apart: 2, of which 2 were waited for; matrix products, arithmetic and copies ran while one was open for 0% of the time, Pallas kernels for 23%

profile of v19, /device:TPU:0, one launch (start us, length us, event | category | flops | bytes accessed | tf_op | source)
XLA Modules:
  0.0 35.3 jit_solution(14216865783077413772)
XLA Ops:
  0.6 2.1 %send.1 = bf16[32,40,128]{2,1,0:T(8,128)(2,1)} custom-call(s32[1,16]{1,0:T(1,128)} %bitcast.5, bf16[16,2560]{1,0:T(8,128)(2,1)} %traces_hbm.1, bf16[16,32768]{1,0:T(8,128)(2,1)} %corr_hbm.1), custom_call_target="tpu_custom_call" | custom-call | tf_op jit(solution)/shard_map/send/pallas_call | solution.py:482
  2.8 7.3 %all-to-all-start = ((bf16[32,40,128]{2,1,0:T(8,128)(2,1)}), bf16[32,40,128]{2,1,0:T(8,128)(2,1)S(1)}, u32[]{:S(2)}, u32[]{:S(2)}) async-start(bf16[32,40,128]{2,1,0:T(8,128)(2,1)} %send.1), calls=%async_computation | async-start | bytes 655360 | tf_op jit(solution)/shard_map/all_to_all | solution.py:496
  10.1 8.3 %prepare.1.packed_hbm = f32[552,1024]{1,0:T(8,128)} custom-call(s32[1,16]{1,0:T(1,128)} %bitcast.6, s32[1,128]{1,0:T(1,128)} %bitcast.7, s32[256,128]{1,0:T(8,128)} %bitcast.4, f32[16,32768]{1,0:T(8,128)} %tables_hbm.1), custom_call_target="tpu_custom_call" | custom-call | tf_op jit(solution)/shard_map/prepare/pallas_call | solution.py:510
  18.4 3.4 %all-to-all-done.block_ref = bf16[32,40,128]{2,1,0:T(8,128)(2,1)S(1)} async-done(((bf16[32,40,128]{2,1,0:T(8,128)(2,1)}), bf16[32,40,128]{2,1,0:T(8,128)(2,1)S(1)}, u32[]{:S(2)}, u32[]{:S(2)}) %all-to-all-start) | async-done | bytes 327712 | tf_op jit(solution)/shard_map/all_to_all | solution.py:496
  21.8 8.5 %image.1 = (f32[16,1024]{1,0:T(8,128)S(1)}, f32[16,1024]{1,0:T(8,128)S(1)}) custom-call(f32[552,1024]{1,0:T(8,128)} %prepare.1.packed_hbm, bf16[32,40,128]{2,1,0:T(8,128)(2,1)S(1)} %all-to-all-done.block_ref), custom_call_target="tpu_custom_call" | custom-call | tf_op jit(solution)/shard_map/image/pallas_call | solution.py:536
  30.3 1.1 %collective-permute-start = (f32[16,1024]{1,0:T(8,128)S(1)}, f32[16,1024]{1,0:T(8,128)S(1)}, u32[]{:S(2)}, u32[]{:S(2)}) collective-permute-start(f32[16,1024]{1,0:T(8,128)S(1)} %get-tuple-element.7), channel_id=1, source_target_pairs={{0,16},{16,0},{1,17},{17,1},{2,18},{18,2},{3,19},{19,3},{4,20},{20... | collective-permute-start | bytes 196616 | tf_op jit(solution)/shard_map/ppermute | solution.py:556
  31.3 3.3 %collective-permute-done.got_ref = f32[16,1024]{1,0:T(8,128)S(1)} collective-permute-done((f32[16,1024]{1,0:T(8,128)S(1)}, f32[16,1024]{1,0:T(8,128)S(1)}, u32[]{:S(2)}, u32[]{:S(2)}) %collective-permute-start) | collective-permute-done | bytes 65568 | tf_op jit(solution)/shard_map/ppermute | solution.py:556
  34.6 0.7 %finish.1 = (f32[16,2048]{1,0:T(8,128)}, f32[1,2048]{1,0:T(1,128)}) custom-call(f32[16,1024]{1,0:T(8,128)S(1)} %get-tuple-element.6.keep_ref, f32[16,1024]{1,0:T(8,128)S(1)} %collective-permute-done.got_ref), custom_call_target="tpu_custom_call" | custom-call | tf_op jit(solution)/shard_map/finish/pallas_call | solution.py:557
Async XLA Ops:
  2.8 19.0 %all-to-all-start = ((bf16[32,40,128]{2,1,0:T(8,128)(2,1)}), bf16[32,40,128]{2,1,0:T(8,128)(2,1)S(1)}, u32[]{:S(2)}, u32[]{:S(2)}) async-start(bf16[32,40,128]{2,1,0:T(8,128)(2,1)} %send.1), calls=%async_computation | async-start | bytes 655360 | tf_op jit(solution)/shard_map/all_to_all | solution.py:496
  30.3 4.3 %collective-permute-start = (f32[16,1024]{1,0:T(8,128)S(1)}, f32[16,1024]{1,0:T(8,128)S(1)}, u32[]{:S(2)}, u32[]{:S(2)}) collective-permute-start(f32[16,1024]{1,0:T(8,128)S(1)} %get-tuple-element.7), channel_id=1, source_target_pairs={{0,16},{16,0},{1,17},{17,1},{2,18},{18,2},{3,19},{19,3},{4,20},{20... | collective-permute-start | bytes 196616 | tf_op jit(solution)/shard_map/ppermute | solution.py:556

commit v20 on v17

--- a/solution.py
+++ b/solution.py
@@ -411,7 +411,8 @@
             ]
             got = jnp.dot(left, jnp.concatenate(right, axis=0), preferred_element_type=jnp.float32)
             if next_basis is not None:
-                make_basis(group + 1, next_basis, at)
+                for part in range(first, first + chunk, LANES):
+                    make_basis(group + 1, next_basis, slice(part, part + LANES))
             for win in range(windows):
                 row = win * 2 * NF
                 real_sum, imag_sum = sums_ref[row : row + NF, at], sums_ref[row + NF : row + 2 * NF, at]
@@ -423,8 +424,8 @@
                     imag_sum += real * sine + imag * cosine
                 sums_ref[row : row + NF, at], sums_ref[row + NF : row + 2 * NF, at] = real_sum, imag_sum
 
-    for first in range(0, nodes, chunk):
-        make_basis(0, basis_a, slice(first, first + chunk))
+    for first in range(0, nodes, LANES):
+        make_basis(0, basis_a, slice(first, first + LANES))
     for copy in copies[3:]:
         copy.wait()
 

time: 36.8 us -> 38.7 us (1.052)
  Pallas kernels: 20.8 us -> 22.7 us
    pallas_call x1, Pallas kernels: 9.77 us -> 11.7 us  [on_device(): pl.pallas_call(functools.partial(image_kernel, merged, stations_dev), out...]
  transfers between devices with their start and end apart: 2 -> 2, of which waited for: 2 -> 2; matrix products, arithmetic and copies ran while one was open for 0% -> 0% of each run, Pallas kernels for 23% -> 22%
where the time goes in v20:
time: 38.7 us; the launch traced here: 38.4 us
  Pallas kernels  22.7 us (59%)
  starting transfers between devices  8.38 us (22%)
  waiting for transfers between devices  6.69 us (17%)
  between operations  0.66 us (2%)
    pallas_call x1, Pallas kernels, on_device(): pl.pallas_call(functools.partial(image_kernel, merged, stations_dev), out...  11.7 us
    pallas_call x1, Pallas kernels, on_device(): pl.pallas_call(prepare_kernel, out_shape=jax.ShapeDtypeStruct(packed_shap...  8.26 us
    all_to_all x1, starting transfers between devices, on_device(): lax.all_to_all(blocks, ('win', 'sta', 'freq'), split_axis=0, concat_axis=...  7.31 us
    all_to_all x1, waiting for transfers between devices, on_device(): lax.all_to_all(blocks, ('win', 'sta', 'freq'), split_axis=0, concat_axis=...  3.43 us
    ppermute x1, waiting for transfers between devices, on_device(): got = lax.ppermute(send, 'win', [(0, 1), (1, 0)])  3.26 us
    pallas_call x1, Pallas kernels, on_device(): pl.pallas_call(functools.partial(send_kernel, nodes), out_shape=jax.Shape...  2.09 us
    ppermute x1, starting transfers between devices, on_device(): got = lax.ppermute(send, 'win', [(0, 1), (1, 0)])  1.07 us
  transfers between devices with their start and end apart: 2, of which 2 were waited for; matrix products, arithmetic and copies ran while one was open for 0% of the time, Pallas kernels for 22%

profile of v20, /device:TPU:0, one launch (start us, length us, event | category | flops | bytes accessed | tf_op | source)
XLA Modules:
  0.0 38.4 jit_solution(1134248190470259768)
XLA Ops:
  0.6 2.1 %send.1 = bf16[32,40,128]{2,1,0:T(8,128)(2,1)} custom-call(s32[1,16]{1,0:T(1,128)} %bitcast.5, bf16[16,2560]{1,0:T(8,128)(2,1)} %traces_hbm.1, bf16[16,32768]{1,0:T(8,128)(2,1)} %corr_hbm.1), custom_call_target="tpu_custom_call" | custom-call | tf_op jit(solution)/shard_map/send/pallas_call | solution.py:482
  2.7 7.3 %all-to-all-start = ((bf16[32,40,128]{2,1,0:T(8,128)(2,1)}), bf16[32,40,128]{2,1,0:T(8,128)(2,1)S(1)}, u32[]{:S(2)}, u32[]{:S(2)}) async-start(bf16[32,40,128]{2,1,0:T(8,128)(2,1)} %send.1), calls=%async_computation | async-start | bytes 655360 | tf_op jit(solution)/shard_map/all_to_all | solution.py:495
  10.0 8.3 %prepare.1.packed_hbm = f32[552,1024]{1,0:T(8,128)} custom-call(s32[1,16]{1,0:T(1,128)} %bitcast.6, s32[1,128]{1,0:T(1,128)} %bitcast.7, s32[256,128]{1,0:T(8,128)} %bitcast.4, f32[16,32768]{1,0:T(8,128)} %tables_hbm.1), custom_call_target="tpu_custom_call" | custom-call | tf_op jit(solution)/shard_map/prepare/pallas_call | solution.py:509
  18.3 3.4 %all-to-all-done.block_ref = bf16[32,40,128]{2,1,0:T(8,128)(2,1)S(1)} async-done(((bf16[32,40,128]{2,1,0:T(8,128)(2,1)}), bf16[32,40,128]{2,1,0:T(8,128)(2,1)S(1)}, u32[]{:S(2)}, u32[]{:S(2)}) %all-to-all-start) | async-done | bytes 327712 | tf_op jit(solution)/shard_map/all_to_all | solution.py:495
  21.8 11.7 %image.1 = (f32[16,1024]{1,0:T(8,128)S(1)}, f32[16,1024]{1,0:T(8,128)S(1)}) custom-call(f32[552,1024]{1,0:T(8,128)} %prepare.1.packed_hbm, bf16[32,40,128]{2,1,0:T(8,128)(2,1)S(1)} %all-to-all-done.block_ref), custom_call_target="tpu_custom_call" | custom-call | tf_op jit(solution)/shard_map/image/pallas_call | solution.py:536
  33.4 1.1 %collective-permute-start = (f32[16,1024]{1,0:T(8,128)S(1)}, f32[16,1024]{1,0:T(8,128)S(1)}, u32[]{:S(2)}, u32[]{:S(2)}) collective-permute-start(f32[16,1024]{1,0:T(8,128)S(1)} %get-tuple-element.7), channel_id=1, source_target_pairs={{0,16},{16,0},{1,17},{17,1},{2,18},{18,2},{3,19},{19,3},{4,20},{20... | collective-permute-start | bytes 196616 | tf_op jit(solution)/shard_map/ppermute | solution.py:558
  34.5 3.3 %collective-permute-done.got_ref = f32[16,1024]{1,0:T(8,128)S(1)} collective-permute-done((f32[16,1024]{1,0:T(8,128)S(1)}, f32[16,1024]{1,0:T(8,128)S(1)}, u32[]{:S(2)}, u32[]{:S(2)}) %collective-permute-start) | collective-permute-done | bytes 65568 | tf_op jit(solution)/shard_map/ppermute | solution.py:558
  37.7 0.7 %finish.1 = (f32[16,2048]{1,0:T(8,128)}, f32[1,2048]{1,0:T(1,128)}) custom-call(f32[16,1024]{1,0:T(8,128)S(1)} %get-tuple-element.6.keep_ref, f32[16,1024]{1,0:T(8,128)S(1)} %collective-permute-done.got_ref), custom_call_target="tpu_custom_call" | custom-call | tf_op jit(solution)/shard_map/finish/pallas_call | solution.py:559
Async XLA Ops:
  2.7 19.0 %all-to-all-start = ((bf16[32,40,128]{2,1,0:T(8,128)(2,1)}), bf16[32,40,128]{2,1,0:T(8,128)(2,1)S(1)}, u32[]{:S(2)}, u32[]{:S(2)}) async-start(bf16[32,40,128]{2,1,0:T(8,128)(2,1)} %send.1), calls=%async_computation | async-start | bytes 655360 | tf_op jit(solution)/shard_map/all_to_all | solution.py:495
  33.4 4.3 %collective-permute-start = (f32[16,1024]{1,0:T(8,128)S(1)}, f32[16,1024]{1,0:T(8,128)S(1)}, u32[]{:S(2)}, u32[]{:S(2)}) collective-permute-start(f32[16,1024]{1,0:T(8,128)S(1)} %get-tuple-element.7), channel_id=1, source_target_pairs={{0,16},{16,0},{1,17},{17,1},{2,18},{18,2},{3,19},{19,3},{4,20},{20... | collective-permute-start | bytes 196616 | tf_op jit(solution)/shard_map/ppermute | solution.py:558

commit v21 on v17

--- a/solution.py
+++ b/solution.py
@@ -334,7 +334,7 @@
     weight_ref[...] = found
     place_ref[...] = jnp.dot(sorter, corr, preferred_element_type=jnp.float32) * (1.0 / REACH)
     sums_ref[...] = jnp.zeros_like(sums_ref)
-    chunk = min(256, nodes)
+    chunk, broad = min(256, nodes), min(512, nodes)
     depth = DEGREES * 8
     lanes = windows * 2 * NF
     for copy in copies[1:3]:
@@ -410,8 +410,8 @@
                 basis_ref[:LANES, at],
             ]
             got = jnp.dot(left, jnp.concatenate(right, axis=0), preferred_element_type=jnp.float32)
-            if next_basis is not None:
-                make_basis(group + 1, next_basis, at)
+            if next_basis is not None and first % broad == 0:
+                make_basis(group + 1, next_basis, slice(first, first + broad))
             for win in range(windows):
                 row = win * 2 * NF
                 real_sum, imag_sum = sums_ref[row : row + NF, at], sums_ref[row + NF : row + 2 * NF, at]
@@ -423,8 +423,8 @@
                     imag_sum += real * sine + imag * cosine
                 sums_ref[row : row + NF, at], sums_ref[row + NF : row + 2 * NF, at] = real_sum, imag_sum
 
-    for first in range(0, nodes, chunk):
-        make_basis(0, basis_a, slice(first, first + chunk))
+    for first in range(0, nodes, broad):
+        make_basis(0, basis_a, slice(first, first + broad))
     for copy in copies[3:]:
         copy.wait()
 

time: 36.8 us -> 36.6 us (level); the launches traced: 36.6 us -> 36 us
  Pallas kernels: 20.8 us -> 20.2 us
    pallas_call x1, Pallas kernels: 9.77 us -> 9.17 us  [on_device(): pl.pallas_call(functools.partial(image_kernel, merged, stations_dev), out...]
where the time goes in v21:
time: 36.6 us; the launch traced here: 36 us
  Pallas kernels  20.2 us (55%)
  starting transfers between devices  8.38 us (23%)
  waiting for transfers between devices  6.69 us (18%)
  between operations  0.66 us (2%)
    pallas_call x1, Pallas kernels, on_device(): pl.pallas_call(functools.partial(image_kernel, merged, stations_dev), out...  9.17 us
    pallas_call x1, Pallas kernels, on_device(): pl.pallas_call(prepare_kernel, out_shape=jax.ShapeDtypeStruct(packed_shap...  8.26 us
    all_to_all x1, starting transfers between devices, on_device(): lax.all_to_all(blocks, ('win', 'sta', 'freq'), split_axis=0, concat_axis=...  7.31 us
    all_to_all x1, waiting for transfers between devices, on_device(): lax.all_to_all(blocks, ('win', 'sta', 'freq'), split_axis=0, concat_axis=...  3.43 us
    ppermute x1, waiting for transfers between devices, on_device(): got = lax.ppermute(send, 'win', [(0, 1), (1, 0)])  3.26 us
    pallas_call x1, Pallas kernels, on_device(): pl.pallas_call(functools.partial(send_kernel, nodes), out_shape=jax.Shape...  2.09 us
    ppermute x1, starting transfers between devices, on_device(): got = lax.ppermute(send, 'win', [(0, 1), (1, 0)])  1.07 us
  transfers between devices with their start and end apart: 2, of which 2 were waited for; matrix products, arithmetic and copies ran while one was open for 0% of the time, Pallas kernels for 23%

profile of v21, /device:TPU:0, one launch (start us, length us, event | category | flops | bytes accessed | tf_op | source)
XLA Modules:
  0.0 36.0 jit_solution(2456774686505733339)
XLA Ops:
  0.6 2.1 %send.1 = bf16[32,40,128]{2,1,0:T(8,128)(2,1)} custom-call(s32[1,16]{1,0:T(1,128)} %bitcast.5, bf16[16,2560]{1,0:T(8,128)(2,1)} %traces_hbm.1, bf16[16,32768]{1,0:T(8,128)(2,1)} %corr_hbm.1), custom_call_target="tpu_custom_call" | custom-call | tf_op jit(solution)/shard_map/send/pallas_call | solution.py:481
  2.7 7.3 %all-to-all-start = ((bf16[32,40,128]{2,1,0:T(8,128)(2,1)}), bf16[32,40,128]{2,1,0:T(8,128)(2,1)S(1)}, u32[]{:S(2)}, u32[]{:S(2)}) async-start(bf16[32,40,128]{2,1,0:T(8,128)(2,1)} %send.1), calls=%async_computation | async-start | bytes 655360 | tf_op jit(solution)/shard_map/all_to_all | solution.py:494
  10.0 8.3 %prepare.1.packed_hbm = f32[552,1024]{1,0:T(8,128)} custom-call(s32[1,16]{1,0:T(1,128)} %bitcast.6, s32[1,128]{1,0:T(1,128)} %bitcast.7, s32[256,128]{1,0:T(8,128)} %bitcast.4, f32[16,32768]{1,0:T(8,128)} %tables_hbm.1), custom_call_target="tpu_custom_call" | custom-call | tf_op jit(solution)/shard_map/prepare/pallas_call | solution.py:508
  18.3 3.4 %all-to-all-done.block_ref = bf16[32,40,128]{2,1,0:T(8,128)(2,1)S(1)} async-done(((bf16[32,40,128]{2,1,0:T(8,128)(2,1)}), bf16[32,40,128]{2,1,0:T(8,128)(2,1)S(1)}, u32[]{:S(2)}, u32[]{:S(2)}) %all-to-all-start) | async-done | bytes 327712 | tf_op jit(solution)/shard_map/all_to_all | solution.py:494
  21.8 9.2 %image.1 = (f32[16,1024]{1,0:T(8,128)S(1)}, f32[16,1024]{1,0:T(8,128)S(1)}) custom-call(f32[552,1024]{1,0:T(8,128)} %prepare.1.packed_hbm, bf16[32,40,128]{2,1,0:T(8,128)(2,1)S(1)} %all-to-all-done.block_ref), custom_call_target="tpu_custom_call" | custom-call | tf_op jit(solution)/shard_map/image/pallas_call | solution.py:535
  30.9 1.1 %collective-permute-start = (f32[16,1024]{1,0:T(8,128)S(1)}, f32[16,1024]{1,0:T(8,128)S(1)}, u32[]{:S(2)}, u32[]{:S(2)}) collective-permute-start(f32[16,1024]{1,0:T(8,128)S(1)} %get-tuple-element.7), channel_id=1, source_target_pairs={{0,16},{16,0},{1,17},{17,1},{2,18},{18,2},{3,19},{19,3},{4,20},{20... | collective-permute-start | bytes 196616 | tf_op jit(solution)/shard_map/ppermute | solution.py:557
  32.0 3.3 %collective-permute-done.got_ref = f32[16,1024]{1,0:T(8,128)S(1)} collective-permute-done((f32[16,1024]{1,0:T(8,128)S(1)}, f32[16,1024]{1,0:T(8,128)S(1)}, u32[]{:S(2)}, u32[]{:S(2)}) %collective-permute-start) | collective-permute-done | bytes 65568 | tf_op jit(solution)/shard_map/ppermute | solution.py:557
  35.3 0.7 %finish.1 = (f32[16,2048]{1,0:T(8,128)}, f32[1,2048]{1,0:T(1,128)}) custom-call(f32[16,1024]{1,0:T(8,128)S(1)} %get-tuple-element.6.keep_ref, f32[16,1024]{1,0:T(8,128)S(1)} %collective-permute-done.got_ref), custom_call_target="tpu_custom_call" | custom-call | tf_op jit(solution)/shard_map/finish/pallas_call | solution.py:558
Async XLA Ops:
  2.7 19.0 %all-to-all-start = ((bf16[32,40,128]{2,1,0:T(8,128)(2,1)}), bf16[32,40,128]{2,1,0:T(8,128)(2,1)S(1)}, u32[]{:S(2)}, u32[]{:S(2)}) async-start(bf16[32,40,128]{2,1,0:T(8,128)(2,1)} %send.1), calls=%async_computation | async-start | bytes 655360 | tf_op jit(solution)/shard_map/all_to_all | solution.py:494
  30.9 4.3 %collective-permute-start = (f32[16,1024]{1,0:T(8,128)S(1)}, f32[16,1024]{1,0:T(8,128)S(1)}, u32[]{:S(2)}, u32[]{:S(2)}) collective-permute-start(f32[16,1024]{1,0:T(8,128)S(1)} %get-tuple-element.7), channel_id=1, source_target_pairs={{0,16},{16,0},{1,17},{17,1},{2,18},{18,2},{3,19},{19,3},{4,20},{20... | collective-permute-start | bytes 196616 | tf_op jit(solution)/shard_map/ppermute | solution.py:557

commit v22 on v16

--- a/solution.py
+++ b/solution.py
@@ -17,7 +17,6 @@
 FINE = 24
 REACH = 1.5
 TABLE_PIECES = 4
-ROUNDER = 1.5 * 2.0**15
 VMEM_LIMIT = 64 * 1024 * 1024 - 64 * 1024
 
 
@@ -381,11 +380,9 @@
         before, now = jnp.ones_like(arg), arg
         for degree in range(0, DEGREES, 2):
             pair = jnp.concatenate([before, now], axis=0)
-            if degree < FINE:
-                high = (pair + ROUNDER) - ROUNDER
-                basis_ref[depth + degree * 8 : depth + degree * 8 + 16, :] = (pair - high).astype(jnp.bfloat16)
-                pair = high
-            basis_ref[degree * 8 : degree * 8 + 16, :] = pair.astype(jnp.bfloat16)
+            terms = split_bf16(pair, 2 if degree < FINE else 1)
+            for term, value in enumerate(terms):
+                basis_ref[term * depth + degree * 8 : term * depth + degree * 8 + 16, :] = value
             before = twice * now - before
             now = twice * before - now
             if degree % 8 == 6:

time: 37.5 us -> 36.7 us (0.979)
  Pallas kernels: 21.1 us -> 20.3 us
    pallas_call x1, Pallas kernels: 10.4 us -> 9.64 us  [on_device(): pl.pallas_call(functools.partial(image_kernel, merged, stations_dev), out...]
  transfers between devices with their start and end apart: 2 -> 2, of which waited for: 2 -> 2; matrix products, arithmetic and copies ran while one was open for 0% -> 0% of each run, Pallas kernels for 21% -> 22%
where the time goes in v22:
time: 36.7 us; the launch traced here: 36.4 us
  Pallas kernels  20.3 us (55%)
  starting transfers between devices  8.38 us (23%)
  waiting for transfers between devices  7.07 us (19%)
  between operations  0.66 us (2%)
    pallas_call x1, Pallas kernels, on_device(): pl.pallas_call(functools.partial(image_kernel, merged, stations_dev), out...  9.64 us
    pallas_call x1, Pallas kernels, on_device(): pl.pallas_call(prepare_kernel, out_shape=jax.ShapeDtypeStruct(packed_shap...  7.88 us
    all_to_all x1, starting transfers between devices, on_device(): lax.all_to_all(blocks, ('win', 'sta', 'freq'), split_axis=0, concat_axis=...  7.31 us
    all_to_all x1, waiting for transfers between devices, on_device(): lax.all_to_all(blocks, ('win', 'sta', 'freq'), split_axis=0, concat_axis=...  3.81 us
    ppermute x1, waiting for transfers between devices, on_device(): got = lax.ppermute(send, 'win', [(0, 1), (1, 0)])  3.26 us
    pallas_call x1, Pallas kernels, on_device(): pl.pallas_call(functools.partial(send_kernel, nodes), out_shape=jax.Shape...  2.09 us
    ppermute x1, starting transfers between devices, on_device(): got = lax.ppermute(send, 'win', [(0, 1), (1, 0)])  1.07 us
  transfers between devices with their start and end apart: 2, of which 2 were waited for; matrix products, arithmetic and copies ran while one was open for 0% of the time, Pallas kernels for 22%

profile of v22, /device:TPU:0, one launch (start us, length us, event | category | flops | bytes accessed | tf_op | source)
XLA Modules:
  0.0 36.4 jit_solution(14394119234304093480)
XLA Ops:
  0.6 2.1 %send.1 = bf16[32,40,128]{2,1,0:T(8,128)(2,1)} custom-call(s32[1,16]{1,0:T(1,128)} %bitcast.5, bf16[16,2560]{1,0:T(8,128)(2,1)} %traces_hbm.1, bf16[16,32768]{1,0:T(8,128)(2,1)} %corr_hbm.1), custom_call_target="tpu_custom_call" | custom-call | tf_op jit(solution)/shard_map/send/pallas_call | solution.py:475
  2.7 7.3 %all-to-all-start = ((bf16[32,40,128]{2,1,0:T(8,128)(2,1)}), bf16[32,40,128]{2,1,0:T(8,128)(2,1)S(1)}, u32[]{:S(2)}, u32[]{:S(2)}) async-start(bf16[32,40,128]{2,1,0:T(8,128)(2,1)} %send.1), calls=%async_computation | async-start | bytes 655360 | tf_op jit(solution)/shard_map/all_to_all | solution.py:488
  10.0 7.9 %prepare.1.packed_hbm = f32[552,1024]{1,0:T(8,128)} custom-call(s32[1,16]{1,0:T(1,128)} %bitcast.6, s32[1,128]{1,0:T(1,128)} %bitcast.7, s32[256,128]{1,0:T(8,128)} %bitcast.4, f32[16,32768]{1,0:T(8,128)} %tables_hbm.1), custom_call_target="tpu_custom_call" | custom-call | tf_op jit(solution)/shard_map/prepare/pallas_call | solution.py:502
  17.9 3.8 %all-to-all-done.block_ref = bf16[32,40,128]{2,1,0:T(8,128)(2,1)S(1)} async-done(((bf16[32,40,128]{2,1,0:T(8,128)(2,1)}), bf16[32,40,128]{2,1,0:T(8,128)(2,1)S(1)}, u32[]{:S(2)}, u32[]{:S(2)}) %all-to-all-start) | async-done | bytes 327712 | tf_op jit(solution)/shard_map/all_to_all | solution.py:488
  21.8 9.6 %image.1 = (f32[16,1024]{1,0:T(8,128)S(1)}, f32[16,1024]{1,0:T(8,128)S(1)}) custom-call(f32[552,1024]{1,0:T(8,128)} %prepare.1.packed_hbm, bf16[32,40,128]{2,1,0:T(8,128)(2,1)S(1)} %all-to-all-done.block_ref), custom_call_target="tpu_custom_call" | custom-call | tf_op jit(solution)/shard_map/image/pallas_call | solution.py:529
  31.4 1.1 %collective-permute-start = (f32[16,1024]{1,0:T(8,128)S(1)}, f32[16,1024]{1,0:T(8,128)S(1)}, u32[]{:S(2)}, u32[]{:S(2)}) collective-permute-start(f32[16,1024]{1,0:T(8,128)S(1)} %get-tuple-element.7), channel_id=1, source_target_pairs={{0,16},{16,0},{1,17},{17,1},{2,18},{18,2},{3,19},{19,3},{4,20},{20... | collective-permute-start | bytes 196616 | tf_op jit(solution)/shard_map/ppermute | solution.py:551
  32.5 3.3 %collective-permute-done.got_ref = f32[16,1024]{1,0:T(8,128)S(1)} collective-permute-done((f32[16,1024]{1,0:T(8,128)S(1)}, f32[16,1024]{1,0:T(8,128)S(1)}, u32[]{:S(2)}, u32[]{:S(2)}) %collective-permute-start) | collective-permute-done | bytes 65568 | tf_op jit(solution)/shard_map/ppermute | solution.py:551
  35.7 0.7 %finish.1 = (f32[16,2048]{1,0:T(8,128)}, f32[1,2048]{1,0:T(1,128)}) custom-call(f32[16,1024]{1,0:T(8,128)S(1)} %get-tuple-element.6.keep_ref, f32[16,1024]{1,0:T(8,128)S(1)} %collective-permute-done.got_ref), custom_call_target="tpu_custom_call" | custom-call | tf_op jit(solution)/shard_map/finish/pallas_call | solution.py:552
Async XLA Ops:
  2.7 19.0 %all-to-all-start = ((bf16[32,40,128]{2,1,0:T(8,128)(2,1)}), bf16[32,40,128]{2,1,0:T(8,128)(2,1)S(1)}, u32[]{:S(2)}, u32[]{:S(2)}) async-start(bf16[32,40,128]{2,1,0:T(8,128)(2,1)} %send.1), calls=%async_computation | async-start | bytes 655360 | tf_op jit(solution)/shard_map/all_to_all | solution.py:488
  31.4 4.3 %collective-permute-start = (f32[16,1024]{1,0:T(8,128)S(1)}, f32[16,1024]{1,0:T(8,128)S(1)}, u32[]{:S(2)}, u32[]{:S(2)}) collective-permute-start(f32[16,1024]{1,0:T(8,128)S(1)} %get-tuple-element.7), channel_id=1, source_target_pairs={{0,16},{16,0},{1,17},{17,1},{2,18},{18,2},{3,19},{19,3},{4,20},{20... | collective-permute-start | bytes 196616 | tf_op jit(solution)/shard_map/ppermute | solution.py:551

commit v23 on v22

--- a/solution.py
+++ b/solution.py
@@ -405,7 +405,7 @@
                 basis_ref[:LANES, at],
             ]
             got = jnp.dot(left, jnp.concatenate(right, axis=0), preferred_element_type=jnp.float32)
-            next(steps, None)
+            run(steps)
             for win in range(windows):
                 row = win * 2 * NF
                 real_sum, imag_sum = sums_ref[row : row + NF, at], sums_ref[row + NF : row + 2 * NF, at]
@@ -416,7 +416,6 @@
                     real_sum += real * cosine - imag * sine
                     imag_sum += real * sine + imag * cosine
                 sums_ref[row : row + NF, at], sums_ref[row + NF : row + 2 * NF, at] = real_sum, imag_sum
-        run(steps)
 
     run(basis_steps(0, basis_a))
     for copy in copies[3:]:

time: 36.7 us -> 36.7 us (level)
  no operation moved by 1% of the time
where the time goes in v23:
time: 36.7 us; the launch traced here: 36.4 us
  Pallas kernels  20.3 us (55%)
  starting transfers between devices  8.38 us (23%)
  waiting for transfers between devices  7.07 us (19%)
  between operations  0.66 us (2%)
    pallas_call x1, Pallas kernels, on_device(): pl.pallas_call(functools.partial(image_kernel, merged, stations_dev), out...  9.64 us
    pallas_call x1, Pallas kernels, on_device(): pl.pallas_call(prepare_kernel, out_shape=jax.ShapeDtypeStruct(packed_shap...  7.88 us
    all_to_all x1, starting transfers between devices, on_device(): lax.all_to_all(blocks, ('win', 'sta', 'freq'), split_axis=0, concat_axis=...  7.31 us
    all_to_all x1, waiting for transfers between devices, on_device(): lax.all_to_all(blocks, ('win', 'sta', 'freq'), split_axis=0, concat_axis=...  3.81 us
    ppermute x1, waiting for transfers between devices, on_device(): got = lax.ppermute(send, 'win', [(0, 1), (1, 0)])  3.26 us
    pallas_call x1, Pallas kernels, on_device(): pl.pallas_call(functools.partial(send_kernel, nodes), out_shape=jax.Shape...  2.09 us
    ppermute x1, starting transfers between devices, on_device(): got = lax.ppermute(send, 'win', [(0, 1), (1, 0)])  1.07 us
  transfers between devices with their start and end apart: 2, of which 2 were waited for; matrix products, arithmetic and copies ran while one was open for 0% of the time, Pallas kernels for 22%

profile of v23, /device:TPU:0, one launch (start us, length us, event | category | flops | bytes accessed | tf_op | source)
XLA Modules:
  0.0 36.4 jit_solution(14394119234304093480)
XLA Ops:
  0.6 2.1 %send.1 = bf16[32,40,128]{2,1,0:T(8,128)(2,1)} custom-call(s32[1,16]{1,0:T(1,128)} %bitcast.5, bf16[16,2560]{1,0:T(8,128)(2,1)} %traces_hbm.1, bf16[16,32768]{1,0:T(8,128)(2,1)} %corr_hbm.1), custom_call_target="tpu_custom_call" | custom-call | tf_op jit(solution)/shard_map/send/pallas_call | solution.py:474
  2.7 7.3 %all-to-all-start = ((bf16[32,40,128]{2,1,0:T(8,128)(2,1)}), bf16[32,40,128]{2,1,0:T(8,128)(2,1)S(1)}, u32[]{:S(2)}, u32[]{:S(2)}) async-start(bf16[32,40,128]{2,1,0:T(8,128)(2,1)} %send.1), calls=%async_computation | async-start | bytes 655360 | tf_op jit(solution)/shard_map/all_to_all | solution.py:487
  10.0 7.9 %prepare.1.packed_hbm = f32[552,1024]{1,0:T(8,128)} custom-call(s32[1,16]{1,0:T(1,128)} %bitcast.6, s32[1,128]{1,0:T(1,128)} %bitcast.7, s32[256,128]{1,0:T(8,128)} %bitcast.4, f32[16,32768]{1,0:T(8,128)} %tables_hbm.1), custom_call_target="tpu_custom_call" | custom-call | tf_op jit(solution)/shard_map/prepare/pallas_call | solution.py:501
  17.9 3.8 %all-to-all-done.block_ref = bf16[32,40,128]{2,1,0:T(8,128)(2,1)S(1)} async-done(((bf16[32,40,128]{2,1,0:T(8,128)(2,1)}), bf16[32,40,128]{2,1,0:T(8,128)(2,1)S(1)}, u32[]{:S(2)}, u32[]{:S(2)}) %all-to-all-start) | async-done | bytes 327712 | tf_op jit(solution)/shard_map/all_to_all | solution.py:487
  21.8 9.6 %image.1 = (f32[16,1024]{1,0:T(8,128)S(1)}, f32[16,1024]{1,0:T(8,128)S(1)}) custom-call(f32[552,1024]{1,0:T(8,128)} %prepare.1.packed_hbm, bf16[32,40,128]{2,1,0:T(8,128)(2,1)S(1)} %all-to-all-done.block_ref), custom_call_target="tpu_custom_call" | custom-call | tf_op jit(solution)/shard_map/image/pallas_call | solution.py:528
  31.4 1.1 %collective-permute-start = (f32[16,1024]{1,0:T(8,128)S(1)}, f32[16,1024]{1,0:T(8,128)S(1)}, u32[]{:S(2)}, u32[]{:S(2)}) collective-permute-start(f32[16,1024]{1,0:T(8,128)S(1)} %get-tuple-element.7), channel_id=1, source_target_pairs={{0,16},{16,0},{1,17},{17,1},{2,18},{18,2},{3,19},{19,3},{4,20},{20... | collective-permute-start | bytes 196616 | tf_op jit(solution)/shard_map/ppermute | solution.py:550
  32.5 3.3 %collective-permute-done.got_ref = f32[16,1024]{1,0:T(8,128)S(1)} collective-permute-done((f32[16,1024]{1,0:T(8,128)S(1)}, f32[16,1024]{1,0:T(8,128)S(1)}, u32[]{:S(2)}, u32[]{:S(2)}) %collective-permute-start) | collective-permute-done | bytes 65568 | tf_op jit(solution)/shard_map/ppermute | solution.py:550
  35.7 0.7 %finish.1 = (f32[16,2048]{1,0:T(8,128)}, f32[1,2048]{1,0:T(1,128)}) custom-call(f32[16,1024]{1,0:T(8,128)S(1)} %get-tuple-element.6.keep_ref, f32[16,1024]{1,0:T(8,128)S(1)} %collective-permute-done.got_ref), custom_call_target="tpu_custom_call" | custom-call | tf_op jit(solution)/shard_map/finish/pallas_call | solution.py:551
Async XLA Ops:
  2.7 19.0 %all-to-all-start = ((bf16[32,40,128]{2,1,0:T(8,128)(2,1)}), bf16[32,40,128]{2,1,0:T(8,128)(2,1)S(1)}, u32[]{:S(2)}, u32[]{:S(2)}) async-start(bf16[32,40,128]{2,1,0:T(8,128)(2,1)} %send.1), calls=%async_computation | async-start | bytes 655360 | tf_op jit(solution)/shard_map/all_to_all | solution.py:487
  31.4 4.3 %collective-permute-start = (f32[16,1024]{1,0:T(8,128)S(1)}, f32[16,1024]{1,0:T(8,128)S(1)}, u32[]{:S(2)}, u32[]{:S(2)}) collective-permute-start(f32[16,1024]{1,0:T(8,128)S(1)} %get-tuple-element.7), channel_id=1, source_target_pairs={{0,16},{16,0},{1,17},{17,1},{2,18},{18,2},{3,19},{19,3},{4,20},{20... | collective-permute-start | bytes 196616 | tf_op jit(solution)/shard_map/ppermute | solution.py:550
